TPU v7x, 32 devices: a whole 2x2x4 slice. The times are simulated.
32 devices in a mesh: dp: 8 (over z, y), mp: 4 (over x, core).
Axes of the slice: x: 2, y: 2, z: 4, core: 2. Of those that a mesh axis runs over, the one named last changes fastest.
Arguments:
- token_ids: int32 [2048], P('dp'), may hold values from 0 to 31999
- target_ids: int32 [2048], P('dp'), may hold values from 0 to 31999
- exit_mask: int32 [2, 2048], P(None, 'dp'), may hold values from 0 to 1, as said below
- table: float32 [32000, 2048], P(('dp', 'mp'))
- table_first: float32 [32000, 2048], P(('dp', 'mp'))
- table_second: float32 [32000, 2048], P(('dp', 'mp')), as said below
- qkv_weight: float32 [2048, 3, 2048], P('dp', None, 'mp'), may hold values from -0.125 to 0.125
- qkv_first: float32 [2048, 3, 2048], P('dp', None, 'mp')
- qkv_second: float32 [2048, 3, 2048], P('dp', None, 'mp'), as said below
- out_weight: float32 [2048, 2048], P('mp', 'dp'), may hold values from -0.25 to 0.25
- out_first: float32 [2048, 2048], P('mp', 'dp')
- out_second: float32 [2048, 2048], P('mp', 'dp'), as said below
- gate_up_weight: float32 [2048, 2, 5632], P('dp', None, 'mp'), may hold values from -0.125 to 0.125
- gate_up_first: float32 [2048, 2, 5632], P('dp', None, 'mp')
- gate_up_second: float32 [2048, 2, 5632], P('dp', None, 'mp'), as said below
- down_weight: float32 [5632, 2048], P('mp', 'dp'), may hold values from -0.078125 to 0.078125
- down_first: float32 [5632, 2048], P('mp', 'dp')
- down_second: float32 [5632, 2048], P('mp', 'dp'), as said below
- gains: float32 [3, 2048], P(None, 'dp')
- gains_first: float32 [3, 2048], P(None, 'dp')
- gains_second: float32 [3, 2048], P(None, 'dp'), as said below
Outputs:
- loss_sums: float32 [2], replicated
- exit_counts: float32 [2], replicated
- grad_norm: float32 [], replicated
- table_new: float32 [32000, 2048], P(('dp', 'mp'))
- table_first_new: float32 [32000, 2048], P(('dp', 'mp'))
- table_second_new: float32 [32000, 2048], P(('dp', 'mp'))
- qkv_new: float32 [2048, 3, 2048], P('dp', None, 'mp')
- qkv_first_new: float32 [2048, 3, 2048], P('dp', None, 'mp')
- qkv_second_new: float32 [2048, 3, 2048], P('dp', None, 'mp')
- out_new: float32 [2048, 2048], P('mp', 'dp')
- out_first_new: float32 [2048, 2048], P('mp', 'dp')
- out_second_new: float32 [2048, 2048], P('mp', 'dp')
- gate_up_new: float32 [2048, 2, 5632], P('dp', None, 'mp')
- gate_up_first_new: float32 [2048, 2, 5632], P('dp', None, 'mp')
- gate_up_second_new: float32 [2048, 2, 5632], P('dp', None, 'mp')
- down_new: float32 [5632, 2048], P('mp', 'dp')
- down_first_new: float32 [5632, 2048], P('mp', 'dp')
- down_second_new: float32 [5632, 2048], P('mp', 'dp')
- gains_new: float32 [3, 2048], P(None, 'dp')
- gains_first_new: float32 [3, 2048], P(None, 'dp')
- gains_second_new: float32 [3, 2048], P(None, 'dp')
Inputs may be any that keep to these rules, and one draw needn't show every extreme that they name: `exit_mask`: in each exit, the 256 positions of one block of tokens hold at most 64 ones, and some block holds exactly 64. `table_second`: Positive. `qkv_second`: Positive. `out_second`: Positive. `gate_up_second`: Positive. `down_second`: Positive. `gains_second`: Positive.
All inputs are finite; a program needn't handle non-finite values.
Results may differ from a plain program's by a relative error of at most 0.023.
Values may be sent and summed in bfloat16 or wider, within the bound.
A program may use at most 256 MiB of HBM per device.

v0:
```python
import math

import jax
import jax.numpy as jnp
from jax import lax
from jax.sharding import PartitionSpec as P

HEAD_DIM = 128
R_DEV = 64
STEP = 10


EPS_NORM = 1e-05
BETA_ONE = 0.9
BETA_TWO = 0.95
ADAM_EPS = 1e-08
DECAY = 0.1
RATE_MATRIX = 0.02
RATE_GAIN = 1.0
CLIP = 0.02
EXIT_SCALE = (1.0 / 3.0, 2.0 / 3.0)
NEG = -1e30
exact_mode = lax.Precision.HIGHEST


def joined(value, axis, join):
    pieces = jax.tree.map(lambda part: lax.all_gather(part, axis), value)
    head = jax.tree.map(lambda part: part[0], pieces)
    tail = jax.tree.map(lambda part: part[1:], pieces)
    total, _ = lax.scan(lambda total, section: (join(total, section), None), head, tail)
    return total


def norm_fwd(values, gain):
    row_scale = lax.rsqrt(jnp.mean(values * values, axis=-1, keepdims=True) + EPS_NORM)
    unit_rows = values * row_scale
    return (unit_rows * gain, unit_rows, row_scale)


def norm_back(unit_rows, row_scale, gain, gradient):
    weighted = gradient * gain
    back_rows = row_scale * (
        weighted - unit_rows * jnp.mean(weighted * unit_rows, axis=-1, keepdims=True)
    )
    return (back_rows, jnp.sum(gradient * unit_rows, axis=0))


def rotary(places, width):
    half_width = width // 2
    frequency = jnp.exp(
        jnp.arange(half_width, dtype=jnp.float32) * (-math.log(10000.0) / half_width)
    )
    angles = places.astype(jnp.float32)[:, None] * frequency[None, :]
    return (jnp.cos(angles), jnp.sin(angles))


def rotate_pairs(values, cosine, sine_table):
    half_width = values.shape[-1] // 2
    front_half = values[..., :half_width]
    back_half = values[..., half_width:]
    cosine = cosine[:, None, :]
    sine_table = sine_table[:, None, :]
    return jnp.concatenate(
        [
            front_half * cosine - back_half * sine_table,
            back_half * cosine + front_half * sine_table,
        ],
        axis=-1,
    )


def model_sum(values):
    return lax.psum(values, "mp")


def block_scores(query_rows, key_block, query_place, key_place, seq_len, score_scale):
    scores = (
        jnp.einsum("qhd,khd->hqk", query_rows, key_block, preferred_element_type=jnp.float32)
        * score_scale
    )
    allowed = (
        (key_place[None, :] <= query_place[:, None])
        & (key_place[None, :] // seq_len == query_place[:, None] // seq_len)
    )[None]
    return (jnp.where(allowed, scores, NEG), allowed)


def key_range(query_place, seq_len, block_rows):
    first_block = query_place[0] // seq_len * seq_len // block_rows
    end_block = query_place[-1] // block_rows + 1
    return (first_block, end_block)


def attend(query_rows, keys_all, values_all, query_place, seq_len, score_scale):
    key_count = keys_all.shape[0]
    block_rows = min(512, key_count)
    heads_here = query_rows.shape[1]
    row_count = query_rows.shape[0]
    first_block, end_block = key_range(query_place, seq_len, block_rows)

    def stats_step(block_idx, carry):
        row_top, row_mass = carry
        row_start = block_idx * block_rows
        key_block = lax.dynamic_slice_in_dim(keys_all, row_start, block_rows, 0)
        key_place = row_start + jnp.arange(block_rows, dtype=jnp.int32)
        scores, allowed = block_scores(
            query_rows, key_block, query_place, key_place, seq_len, score_scale
        )
        new_top = jnp.maximum(row_top, jnp.max(scores, axis=-1))
        weights = jnp.where(allowed, jnp.exp(scores - new_top[..., None]), 0.0)
        return (new_top, row_mass * jnp.exp(row_top - new_top) + jnp.sum(weights, axis=-1))

    start_carry = (
        jnp.full((heads_here, row_count), NEG, jnp.float32),
        jnp.zeros((heads_here, row_count), jnp.float32),
    )
    row_top, row_mass = lax.fori_loop(first_block, end_block, stats_step, start_carry)
    row_lse = row_top + jnp.log(row_mass)

    def output_step(block_idx, total_sum):
        row_start = block_idx * block_rows
        key_block = lax.dynamic_slice_in_dim(keys_all, row_start, block_rows, 0)
        value_block = lax.dynamic_slice_in_dim(values_all, row_start, block_rows, 0)
        key_place = row_start + jnp.arange(block_rows, dtype=jnp.int32)
        scores, allowed = block_scores(
            query_rows, key_block, query_place, key_place, seq_len, score_scale
        )
        probability = jnp.where(allowed, jnp.exp(scores - row_lse[..., None]), 0.0).astype(
            jnp.bfloat16
        )
        return total_sum + jnp.einsum(
            "hqk,khd->qhd", probability, value_block, preferred_element_type=jnp.float32
        )

    attn_raw = lax.fori_loop(
        first_block, end_block, output_step, jnp.zeros(query_rows.shape, jnp.float32)
    )
    return (attn_raw, row_lse)


def pair_grads(
    query_rows,
    grad_out,
    row_lse,
    delta,
    query_place,
    key_block,
    value_block,
    key_place,
    seq_len,
    score_scale,
):
    scores, allowed = block_scores(
        query_rows, key_block, query_place, key_place, seq_len, score_scale
    )
    probability = jnp.where(allowed, jnp.exp(scores - row_lse[..., None]), 0.0)
    grad_values = jnp.einsum(
        "hqk,qhd->khd",
        probability.astype(jnp.bfloat16),
        grad_out,
        preferred_element_type=jnp.float32,
    )
    grad_prob = jnp.einsum(
        "qhd,khd->hqk", grad_out, value_block, preferred_element_type=jnp.float32
    )
    grad_score = (probability * (grad_prob - delta[..., None])).astype(jnp.bfloat16)
    grad_query = (
        jnp.einsum("hqk,khd->qhd", grad_score, key_block, preferred_element_type=jnp.float32)
        * score_scale
    )
    grad_keys = (
        jnp.einsum("hqk,qhd->khd", grad_score, query_rows, preferred_element_type=jnp.float32)
        * score_scale
    )
    return (grad_query, grad_keys, grad_values)


def key_loop(
    query_rows, grad_out, row_lse, delta, query_place, keys_all, values_all, seq_len, score_scale
):
    key_count = keys_all.shape[0]
    block_rows = min(512, key_count)
    first_block, end_block = key_range(query_place, seq_len, block_rows)

    def key_step(block_idx, carry):
        total_sum, pieces = carry
        row_start = block_idx * block_rows
        key_block = lax.dynamic_slice_in_dim(keys_all, row_start, block_rows, 0)
        value_block = lax.dynamic_slice_in_dim(values_all, row_start, block_rows, 0)
        key_place = row_start + jnp.arange(block_rows, dtype=jnp.int32)
        grad_query, grad_keys, grad_values = pair_grads(
            query_rows,
            grad_out,
            row_lse,
            delta,
            query_place,
            key_block,
            value_block,
            key_place,
            seq_len,
            score_scale,
        )
        pieces = lax.dynamic_update_slice_in_dim(
            pieces, jnp.stack([grad_keys, grad_values], axis=1), row_start, 0
        )
        return (total_sum + grad_query, pieces)

    start_pieces = jnp.zeros((key_count, 2) + keys_all.shape[1:], jnp.float32)
    grad_query, pieces = lax.fori_loop(
        first_block, end_block, key_step, (jnp.zeros(query_rows.shape, jnp.float32), start_pieces)
    )
    return (grad_query, pieces.reshape(key_count, 2, -1))


def combine_stats(earlier, later):
    top_a, mass_a, hit_a = earlier
    top_b, mass_b, hit_b = later
    row_top = jnp.maximum(top_a, top_b)
    return (
        row_top,
        mass_a * jnp.exp(top_a - row_top) + mass_b * jnp.exp(top_b - row_top),
        hit_a + hit_b,
    )


def adam_update(weight, moment_one, moment_two, gradient, rate, decay):
    moment_one = BETA_ONE * moment_one + (1.0 - BETA_ONE) * gradient
    moment_two = BETA_TWO * moment_two + (1.0 - BETA_TWO) * gradient * gradient
    ratio = (
        moment_one
        / (1.0 - BETA_ONE**STEP)
        / (jnp.sqrt(moment_two / (1.0 - BETA_TWO**STEP)) + ADAM_EPS)
    )
    return (weight - rate * (ratio + decay * weight), moment_one, moment_two)


def body(
    token_ids,
    target_ids,
    exit_mask,
    table,
    table_first,
    table_second,
    qkv_weight,
    qkv_first,
    qkv_second,
    out_weight,
    out_first,
    out_second,
    gate_up_weight,
    gate_up_first,
    gate_up_second,
    down_weight,
    down_first,
    down_second,
    gains,
    gains_first,
    gains_second,
):
    data_size = lax.axis_size("dp")
    model_size = lax.axis_size("mp")
    data_index = lax.axis_index("dp")
    model_index = lax.axis_index("mp")
    rows_here = token_ids.shape[0]
    seq_len = rows_here * data_size
    heads_here = qkv_weight.shape[2] // HEAD_DIM
    vocab_here = table.shape[0]
    vocab_base = (data_index * model_size + model_index) * vocab_here
    vocab_ids = vocab_base + jnp.arange(vocab_here, dtype=jnp.int32)
    score_scale = 1.0 / math.sqrt(HEAD_DIM)
    qkv_full, out_full, gate_up_full, down_full, gain_low = (
        lax.all_gather(qkv_weight.astype(jnp.bfloat16), "dp", axis=0, tiled=True),
        lax.all_gather(out_weight.astype(jnp.bfloat16), "dp", axis=1, tiled=True),
        lax.all_gather(gate_up_weight.astype(jnp.bfloat16), "dp", axis=0, tiled=True),
        lax.all_gather(down_weight.astype(jnp.bfloat16), "dp", axis=1, tiled=True),
        lax.all_gather(gains.astype(jnp.bfloat16), "dp", axis=1, tiled=True),
    )
    gain_rows = gain_low.astype(jnp.float32)
    table_low = table.astype(jnp.bfloat16)
    slot_ids = jnp.arange(R_DEV, dtype=jnp.int32)
    slot_ranks = jnp.cumsum(exit_mask, axis=1) - 1
    pick_int = (
        (slot_ranks[:, None, :] == slot_ids[None, :, None]) & (exit_mask[:, None, :] == 1)
    ).astype(jnp.int32)
    picked_targets = jnp.sum(pick_int * target_ids[None, None, :], axis=2).reshape(-1)
    live_slots = (
        (slot_ids[None, :] < jnp.sum(exit_mask, axis=1)[:, None]).astype(jnp.int32).reshape(-1)
    )
    all_ids, all_targets, all_live = (
        lax.all_gather(token_ids, "dp", axis=0, tiled=True),
        lax.all_gather(picked_targets, "dp", axis=0, tiled=True),
        lax.all_gather(live_slots, "dp", axis=0, tiled=True),
    )
    ids_part = all_ids
    id_hits = (ids_part[:, None] == vocab_ids[None, :]).astype(jnp.bfloat16)
    resid_zero = model_sum(
        lax.psum_scatter(
            jnp.dot(id_hits, table_low, preferred_element_type=jnp.float32).astype(jnp.bfloat16),
            "dp",
            scatter_dimension=0,
            tiled=True,
        ).astype(jnp.float32)
    )
    attn_in, attn_unit, attn_scale = norm_fwd(resid_zero, gain_rows[0])
    attn_low = attn_in.astype(jnp.bfloat16)
    projected = jnp.einsum("td,dcf->tcf", attn_low, qkv_full, preferred_element_type=jnp.float32)
    shaped = projected.reshape(rows_here, 3, heads_here, HEAD_DIM)
    query_place = data_index * rows_here + jnp.arange(rows_here, dtype=jnp.int32)
    cosine, sine_table = rotary(query_place, HEAD_DIM)
    query_low = rotate_pairs(shaped[:, 0], cosine, sine_table).astype(jnp.bfloat16)
    key_low = rotate_pairs(shaped[:, 1], cosine, sine_table).astype(jnp.bfloat16)
    value_low = shaped[:, 2].astype(jnp.bfloat16)
    keys_all, values_all = (
        lax.all_gather(key_low, "dp", axis=0, tiled=True),
        lax.all_gather(value_low, "dp", axis=0, tiled=True),
    )
    attn_raw, row_lse = attend(query_low, keys_all, values_all, query_place, seq_len, score_scale)
    attn_low_rows = attn_raw.astype(jnp.bfloat16).reshape(rows_here, -1)
    resid_one = resid_zero + model_sum(
        jnp.dot(attn_low_rows, out_full, preferred_element_type=jnp.float32)
    )
    mlp_in, mlp_unit, mlp_scale = norm_fwd(resid_one, gain_rows[1])
    mlp_low = mlp_in.astype(jnp.bfloat16)
    gate_up = jnp.einsum("td,dcf->tcf", mlp_low, gate_up_full, preferred_element_type=jnp.float32)
    gate_part = gate_up[:, 0]
    up_part = gate_up[:, 1]
    gate_sigma = jax.nn.sigmoid(gate_part)
    hidden_low = (gate_part * gate_sigma * up_part).astype(jnp.bfloat16)
    resid_two = resid_one + model_sum(
        jnp.dot(hidden_low, down_full, preferred_element_type=jnp.float32)
    )
    exit_one, unit_one, scale_one = norm_fwd(resid_one, gain_rows[2])
    exit_two, unit_two, scale_two = norm_fwd(resid_two, gain_rows[2])
    exit_low = jnp.stack([exit_one, exit_two]).astype(jnp.bfloat16)
    chosen = jnp.einsum(
        "ert,etd->erd", pick_int.astype(jnp.bfloat16), exit_low, preferred_element_type=jnp.float32
    )
    rows_all = lax.all_gather(
        chosen.astype(jnp.bfloat16).reshape(2 * R_DEV, -1), "dp", axis=0, tiled=True
    )
    logits = lax.dot_general(
        rows_all, table_low, (((1,), (1,)), ((), ())), preferred_element_type=jnp.float32
    )
    target_hits = all_targets[:, None] == vocab_ids[None, :]
    local_top = jnp.max(logits, axis=1)
    local_mass = jnp.sum(jnp.exp(logits - local_top[:, None]), axis=1)
    local_hit = jnp.sum(jnp.where(target_hits, logits, 0.0), axis=1)
    row_top, row_mass, row_hit = joined(
        (local_top, local_mass, local_hit), ("dp", "mp"), combine_stats
    )
    row_lse_head = row_top + jnp.log(row_mass)
    entropy = row_lse_head - row_hit
    exit_of_row = jnp.arange(rows_all.shape[0], dtype=jnp.int32) // R_DEV % 2
    live_float = all_live.astype(jnp.float32)
    count_one = jnp.sum(jnp.where(exit_of_row == 0, live_float, 0.0))
    count_two = jnp.sum(jnp.where(exit_of_row == 1, live_float, 0.0))
    loss_one = jnp.sum(jnp.where(exit_of_row == 0, entropy * live_float, 0.0))
    loss_two = jnp.sum(jnp.where(exit_of_row == 1, entropy * live_float, 0.0))
    row_weight = live_float * jnp.where(
        exit_of_row == 0, EXIT_SCALE[0] / count_one, EXIT_SCALE[1] / count_two
    )
    grad_logits = (
        row_weight[:, None]
        * (jnp.exp(logits - row_lse_head[:, None]) - target_hits.astype(jnp.float32))
    ).astype(jnp.bfloat16)
    table_head = lax.dot_general(
        grad_logits, rows_all, (((0,), (0,)), ((), ())), preferred_element_type=jnp.float32
    )
    row_terms = jnp.dot(grad_logits, table_low, preferred_element_type=jnp.float32)
    row_grads = model_sum(
        lax.psum_scatter(row_terms, "dp", scatter_dimension=0, tiled=True)
    ).reshape(2, R_DEV, -1)
    exit_grads = jnp.einsum(
        "ert,erd->etd", pick_int.astype(jnp.float32), row_grads, precision=exact_mode
    )
    dresid_two, final_two = norm_back(unit_two, scale_two, gain_rows[2], exit_grads[1])
    dexit_one, final_one = norm_back(unit_one, scale_one, gain_rows[2], exit_grads[0])
    dtwo_low = dresid_two.astype(jnp.bfloat16)
    down_local = lax.dot_general(
        hidden_low, dtwo_low, (((0,), (0,)), ((), ())), preferred_element_type=jnp.float32
    )
    dhidden = lax.dot_general(
        dtwo_low, down_full, (((1,), (1,)), ((), ())), preferred_element_type=jnp.float32
    )
    dgate = dhidden * up_part * gate_sigma * (1.0 + gate_part * (1.0 - gate_sigma))
    dup_part = dhidden * gate_part * gate_sigma
    dgate_up = jnp.stack([dgate, dup_part], axis=1).astype(jnp.bfloat16)
    gate_up_local = jnp.einsum("td,tcf->dcf", mlp_low, dgate_up, preferred_element_type=jnp.float32)
    dmlp_in = model_sum(
        jnp.einsum("tcf,dcf->td", dgate_up, gate_up_full, preferred_element_type=jnp.float32)
    )
    dmlp_rows, mlp_gain_grad = norm_back(mlp_unit, mlp_scale, gain_rows[1], dmlp_in)
    dresid_one = dresid_two + dexit_one + dmlp_rows
    done_low = dresid_one.astype(jnp.bfloat16)
    out_local = lax.dot_general(
        attn_low_rows, done_low, (((0,), (0,)), ((), ())), preferred_element_type=jnp.float32
    )
    dattn = lax.dot_general(
        done_low, out_full, (((1,), (1,)), ((), ())), preferred_element_type=jnp.float32
    )
    dattn_low = dattn.astype(jnp.bfloat16).reshape(rows_here, heads_here, HEAD_DIM)
    delta = jnp.sum(dattn_low.astype(jnp.float32) * attn_raw, axis=-1).T
    grad_query, key_terms = key_loop(
        query_low,
        dattn_low,
        row_lse,
        delta,
        query_place,
        keys_all,
        values_all,
        seq_len,
        score_scale,
    )
    own_grads = lax.psum_scatter(key_terms, "dp", scatter_dimension=0, tiled=True)
    own_grads = own_grads.reshape(rows_here, 2, heads_here, HEAD_DIM)
    dquery_back = rotate_pairs(grad_query, cosine, -sine_table)
    dkey_back = rotate_pairs(own_grads[:, 0], cosine, -sine_table)
    dprojected = (
        jnp.stack([dquery_back, dkey_back, own_grads[:, 1]], axis=1)
        .reshape(rows_here, 3, -1)
        .astype(jnp.bfloat16)
    )
    qkv_local = jnp.einsum("td,tcf->dcf", attn_low, dprojected, preferred_element_type=jnp.float32)
    dattn_in = model_sum(
        jnp.einsum("tcf,dcf->td", dprojected, qkv_full, preferred_element_type=jnp.float32)
    )
    dattn_rows, attn_gain_grad = norm_back(attn_unit, attn_scale, gain_rows[0], dattn_in)
    dzero_low = (dresid_one + dattn_rows).astype(jnp.bfloat16)
    ids_part = all_ids
    id_hits = (ids_part[:, None] == vocab_ids[None, :]).astype(jnp.bfloat16)
    table_grad = table_head + lax.dot_general(
        id_hits,
        lax.all_gather(dzero_low, "dp", axis=0, tiled=True),
        (((0,), (0,)), ((), ())),
        preferred_element_type=jnp.float32,
    )
    gain_local = jnp.stack([attn_gain_grad, mlp_gain_grad, final_one + final_two])
    qkv_grad, out_grad, gate_up_grad, down_grad, gain_grad = (
        lax.psum_scatter(qkv_local, "dp", scatter_dimension=0, tiled=True),
        lax.psum_scatter(out_local, "dp", scatter_dimension=1, tiled=True),
        lax.psum_scatter(gate_up_local, "dp", scatter_dimension=0, tiled=True),
        lax.psum_scatter(down_local, "dp", scatter_dimension=1, tiled=True),
        lax.psum_scatter(gain_local, "dp", scatter_dimension=1, tiled=True),
    )
    squares = (
        jnp.sum(table_grad * table_grad)
        + jnp.sum(qkv_grad * qkv_grad)
        + jnp.sum(out_grad * out_grad)
        + jnp.sum(gate_up_grad * gate_up_grad)
        + jnp.sum(down_grad * down_grad)
        + jnp.where(model_index == 0, jnp.sum(gain_grad * gain_grad), 0.0)
    )
    grad_norm = jnp.sqrt(lax.psum(squares, ("dp", "mp")))
    factor = jnp.minimum(1.0, CLIP / (grad_norm + 1e-06))
    table_new = adam_update(
        table, table_first, table_second, table_grad * factor, RATE_MATRIX, DECAY
    )
    qkv_new = adam_update(qkv_weight, qkv_first, qkv_second, qkv_grad * factor, RATE_MATRIX, DECAY)
    out_new = adam_update(out_weight, out_first, out_second, out_grad * factor, RATE_MATRIX, DECAY)
    gate_up_new = adam_update(
        gate_up_weight, gate_up_first, gate_up_second, gate_up_grad * factor, RATE_MATRIX, DECAY
    )
    down_new = adam_update(
        down_weight, down_first, down_second, down_grad * factor, RATE_MATRIX, DECAY
    )
    gains_new = adam_update(gains, gains_first, gains_second, gain_grad * factor, RATE_GAIN, 0.0)
    return (
        jnp.stack([loss_one, loss_two]),
        jnp.stack([count_one, count_two]),
        grad_norm,
        table_new[0],
        table_new[1],
        table_new[2],
        qkv_new[0],
        qkv_new[1],
        qkv_new[2],
        out_new[0],
        out_new[1],
        out_new[2],
        gate_up_new[0],
        gate_up_new[1],
        gate_up_new[2],
        down_new[0],
        down_new[1],
        down_new[2],
        gains_new[0],
        gains_new[1],
        gains_new[2],
    )


def solution(mesh):
    return jax.shard_map(
        body,
        mesh=mesh,
        in_specs=(
            P("dp"),
            P("dp"),
            P(None, "dp"),
            P(("dp", "mp"), None),
            P(("dp", "mp"), None),
            P(("dp", "mp"), None),
            P("dp", None, "mp"),
            P("dp", None, "mp"),
            P("dp", None, "mp"),
            P("mp", "dp"),
            P("mp", "dp"),
            P("mp", "dp"),
            P("dp", None, "mp"),
            P("dp", None, "mp"),
            P("dp", None, "mp"),
            P("mp", "dp"),
            P("mp", "dp"),
            P("mp", "dp"),
            P(None, "dp"),
            P(None, "dp"),
            P(None, "dp"),
        ),
        out_specs=(
            P(),
            P(),
            P(),
            P(("dp", "mp"), None),
            P(("dp", "mp"), None),
            P(("dp", "mp"), None),
            P("dp", None, "mp"),
            P("dp", None, "mp"),
            P("dp", None, "mp"),
            P("mp", "dp"),
            P("mp", "dp"),
            P("mp", "dp"),
            P("dp", None, "mp"),
            P("dp", None, "mp"),
            P("dp", None, "mp"),
            P("mp", "dp"),
            P("mp", "dp"),
            P("mp", "dp"),
            P(None, "dp"),
            P(None, "dp"),
            P(None, "dp"),
        ),
        check_vma=False,
    )
```

profile of v0, /device:TPU:0, one launch (start us, length us, event | category | flops | bytes accessed | tf_op | source)
XLA Modules:
  0.0 2766.3 jit_solution(18387143981146895800)
XLA Ops:
  7.3 22.5 all-gather.4
  47.4 27.6 all_gather.55
  75.9 115.8 %reduce-scatter.11.cloned.1.call-done = bf16[256,2048]{1,0:T(8,128)(2,1)} async-done(((bf16[2048,2048]{1,0:T(8,128)(2,1)}), bf16[256,2048]{1,0:T(8,128)(2,1)}) %reduce-scatter.11.cloned.1.call-update) | async-done | bytes 1048592 | tf_op jit(solution)/shard_map/reduce_scatter | solution.py:297
  191.8 42.3 %all-reduce.16 = f32[256,2048]{1,0:T(8,128)S(1)} all-reduce(bf16[256,2048]{1,0:T(8,128)(2,1)} %reduce-scatter.11.cloned.1.call-done), channel_id=1, replica_groups=mesh['dp'=8,'mp'=4] {'mp'}, use_global_device_ids=true, to_apply=%region_3.4 | all-reduce | flops 524288 | bytes 3145728 | tf_op jit(solution)/shard_map/psum | solution.py:73
  234.3 58.5 %all-gather.16.cloned.1.call-done = bf16[2048,3,512]{2,0,1:T(8,128)(2,1)} async-done(((bf16[256,3,512]{2,0,1:T(8,128)(2,1)}), bf16[2048,3,512]{2,0,1:T(8,128)(2,1)}) %all-gather.16.cloned.1.call-update) | async-done | bytes 6291472 | tf_op jit(solution)/shard_map/all_gather | solution.py:272
  312.8 40.6 %all-gather.18.cloned.1.call-done = bf16[2048,4,128]{0,2,1:T(8,128)(2,1)} async-done(((bf16[256,4,128]{0,2,1:T(8,128)(2,1)}), bf16[2048,4,128]{0,2,1:T(8,128)(2,1)}) %all-gather.18.cloned.1.call-update) | async-done | bytes 2097168 | tf_op jit(solution)/shard_map/all_gather | solution.py:314
  359.7 44.0 %all-gather.30.cloned.1.call-done = bf16[2048,1,4,128]{3,0,2,1:T(8,128)(2,1)} async-done(((bf16[256,1,4,128]{3,0,2,1:T(8,128)(2,1)}), bf16[2048,1,4,128]{3,0,2,1:T(8,128)(2,1)}) %all-gather.30.cloned.1.call-update) | async-done | bytes 2097168 | tf_op jit(solution)/shard_map/all_gather | solution.py:315
  406.3 49.7 %all-gather.20.cloned.1.call-done = bf16[512,2048]{1,0:T(8,128)(2,1)} async-done(((bf16[512,256]{1,0:T(8,128)(2,1)}), bf16[512,2048]{1,0:T(8,128)(2,1)}) %all-gather.20.cloned.1.call-update) | async-done | bytes 2097168 | tf_op jit(solution)/shard_map/all_gather | solution.py:273
  464.1 45.2 %all-reduce.7.cloned.1.call-done = f32[256,2048]{1,0:T(8,128)} async-done(((f32[256,2048]{1,0:T(8,128)}), f32[256,2048]{1,0:T(8,128)}) %all-reduce.7.cloned.1.call-update) | async-done | bytes 2097168 | tf_op jit(solution)/shard_map/psum | solution.py:73
  511.9 164.0 %all-gather.22.cloned.1.call-done = bf16[2048,2,1408]{2,0,1:T(8,128)(2,1)} async-done(((bf16[256,2,1408]{2,0,1:T(8,128)(2,1)}), bf16[2048,2,1408]{2,0,1:T(8,128)(2,1)}) %all-gather.22.cloned.1.call-update) | async-done | bytes 11534352 | tf_op jit(solution)/shard_map/all_gather | solution.py:274
  685.1 85.2 %all-gather.24.cloned.1.call-done = bf16[1408,2048]{1,0:T(8,128)(2,1)} async-done(((bf16[1408,256]{1,0:T(8,128)(2,1)}), bf16[1408,2048]{1,0:T(8,128)(2,1)}) %all-gather.24.cloned.1.call-update) | async-done | bytes 5767184 | tf_op jit(solution)/shard_map/all_gather | solution.py:275
  778.0 48.0 %all-reduce.9.cloned.1.call-done = f32[256,2048]{1,0:T(8,128)} async-done(((f32[256,2048]{1,0:T(8,128)}), f32[256,2048]{1,0:T(8,128)}) %all-reduce.9.cloned.1.call-update) | async-done | bytes 2097168 | tf_op jit(solution)/shard_map/psum | solution.py:73
  830.1 20.5 all-gather.6
  850.8 16.3 all-gather.5
  867.1 36.4 %all-gather.26.cloned.1.call-done = bf16[1024,2048]{1,0:T(8,128)(2,1)} async-done(((bf16[128,2048]{1,0:T(8,128)(2,1)}), bf16[1024,2048]{1,0:T(8,128)(2,1)}) %all-gather.26.cloned.1.call-update) | async-done | bytes 4194320 | tf_op jit(solution)/shard_map/all_gather | solution.py:338
  911.7 39.1 %all-gather.1 = f32[32768]{0:T(1024)S(1)} all-gather(f32[1024]{0:T(1024)S(1)} %get-tuple-element.991), channel_id=3, replica_groups=mesh['dp'=8,'mp'=4] {'dp','mp'}, dimensions={0}, use_global_device_ids=true | all-gather | bytes 135168 | tf_op jit(solution)/shard_map/all_gather | solution.py:27
  952.2 37.0 %all-gather.2 = f32[32768]{0:T(1024)S(1)} all-gather(f32[1024]{0:T(1024)S(1)} %get-tuple-element.852), channel_id=4, replica_groups=mesh['dp'=8,'mp'=4] {'dp','mp'}, dimensions={0}, use_global_device_ids=true | all-gather | bytes 135168 | tf_op jit(solution)/shard_map/all_gather | solution.py:27
  989.9 38.3 %all-gather.3 = f32[32768]{0:T(1024)S(1)} all-gather(f32[1024]{0:T(1024)S(1)} %get-tuple-element.851), channel_id=5, replica_groups=mesh['dp'=8,'mp'=4] {'dp','mp'}, dimensions={0}, use_global_device_ids=true | all-gather | bytes 135168 | tf_op jit(solution)/shard_map/all_gather | solution.py:27
  1032.1 26.5 while.63
  1073.8 145.3 %reduce-scatter.13.cloned.1.call-done = f32[128,2048]{1,0:T(8,128)} async-done(((f32[1024,2048]{1,0:T(8,128)}), f32[128,2048]{1,0:T(8,128)}) %reduce-scatter.13.cloned.1.call-update) | async-done | bytes 1048592 | tf_op jit(solution)/shard_map/reduce_scatter | solution.py:371
  1219.4 37.0 %all-reduce.11.cloned.1.call-done = f32[2,64,2048]{2,1,0:T(8,128)} async-done(((f32[2,64,2048]{2,1,0:T(8,128)}), f32[2,64,2048]{2,1,0:T(8,128)}) %all-reduce.11.cloned.1.call-update) | async-done | bytes 1048592 | tf_op jit(solution)/shard_map/psum | solution.py:73
  1275.8 51.4 %all-reduce.13.cloned.1.call-done = f32[256,2048]{1,0:T(8,128)} async-done(((f32[256,2048]{1,0:T(8,128)}), f32[256,2048]{1,0:T(8,128)}) %all-reduce.13.cloned.1.call-update) | async-done | bytes 2097168 | tf_op jit(solution)/shard_map/psum | solution.py:73
  1350.5 182.5 %reduce-scatter.15.cloned.1.call-done = f32[256,2,512]{0,2,1:T(8,128)} async-done(((f32[2048,2,512]{0,2,1:T(8,128)}), f32[256,2,512]{0,2,1:T(8,128)}) %reduce-scatter.15.cloned.1.call-update) | async-done | bytes 1048592 | tf_op jit(solution)/shard_map/reduce_scatter | solution.py:414
  1547.6 45.5 %all-reduce.15.cloned.1.call-done = f32[256,2048]{1,0:T(8,128)} async-done(((f32[256,2048]{1,0:T(8,128)}), f32[256,2048]{1,0:T(8,128)}) %all-reduce.15.cloned.1.call-update) | async-done | bytes 2097168 | tf_op jit(solution)/shard_map/psum | solution.py:73
  1628.9 56.9 %reduce-scatter.19.cloned.1.call-done = f32[512,256]{1,0:T(8,128)} async-done(((f32[512,2048]{1,0:T(8,128)}), f32[512,256]{1,0:T(8,128)}) %reduce-scatter.19.cloned.1.call-update) | async-done | bytes 524304 | tf_op jit(solution)/shard_map/reduce_scatter | solution.py:440
  1687.5 65.6 %reduce-scatter.25.cloned.1.call-done = f32[256,3]{1,0:T(8,128)} async-done(((f32[2048,3]{1,0:T(8,128)}), f32[256,3]{1,0:T(8,128)}) %reduce-scatter.25.cloned.1.call-update) | async-done | bytes 3088
  1755.4 193.4 %reduce-scatter.23.cloned.1.call-done = f32[1408,256]{1,0:T(8,128)} async-done(((f32[1408,2048]{1,0:T(8,128)}), f32[1408,256]{1,0:T(8,128)}) %reduce-scatter.23.cloned.1.call-update) | async-done | bytes 1441808 | tf_op jit(solution)/shard_map/reduce_scatter | solution.py:442
  1951.1 124.4 %all-gather.28.cloned.1.call-done = bf16[2048,2048]{1,0:T(8,128)(2,1)} async-done(((bf16[256,2048]{1,0:T(8,128)(2,1)}), bf16[2048,2048]{1,0:T(8,128)(2,1)}) %all-gather.28.cloned.1.call-update) | async-done | bytes 8388624 | tf_op jit(solution)/shard_map/all_gather | solution.py:433
  2096.2 188.8 %reduce-scatter.17.cloned.1.call-done = f32[256,3,512]{2,0,1:T(8,128)} async-done(((f32[2048,3,512]{2,0,1:T(8,128)}), f32[256,3,512]{2,0,1:T(8,128)}) %reduce-scatter.17.cloned.1.call-update) | async-done | bytes 1572880 | tf_op jit(solution)/shard_map/reduce_scatter | solution.py:439
  2289.4 371.7 %reduce-scatter.21.cloned.1.call-done = f32[256,2,1408]{2,0,1:T(8,128)} async-done(((f32[2048,2,1408]{2,0,1:T(8,128)}), f32[256,2,1408]{2,0,1:T(8,128)}) %reduce-scatter.21.cloned.1.call-update) | async-done | bytes 2883600 | tf_op jit(solution)/shard_map/reduce_scatter | solution.py:441
  2667.3 39.5 %psum.55 = f32[]{:T(128)} all-reduce(f32[]{:T(128)S(6)} %add.508), channel_id=1, replica_groups=mesh['dp'=8,'mp'=4] {'dp','mp'}, use_global_device_ids=true, to_apply=%region_53.54 | all-reduce | flops 1 | bytes 8 | tf_op jit(solution)/shard_map/psum | solution.py:453
  2724.4 23.1 multiply_subtract_fusion
  (455 shorter events, 296.8 us)
Async XLA Ops:
  7.2 184.6 %reduce-scatter.11.cloned.1.call-start = ((), (), s32[]{:S(2)}) async-start(), calls=%async_computation.8 | async-start | bytes 9437184 | tf_op jit(solution)/shard_map/reduce_scatter | solution.py:297
  7.3 1053.3 %copy-start.44 = (s32[1000]{0:T(1024)}, s32[1000]{0:T(1024)S(1)}, u32[]{:S(2)}) copy-start(s32[1000]{0:T(1024)S(1)} %iota_add_fusion.9) | copy-start | bytes 12004
  44.9 247.9 %all-gather.16.cloned.1.call-start = ((), (), s32[]{:S(2)}) async-start(), calls=%async_computation.9 | async-start | bytes 7077888 | tf_op jit(solution)/shard_map/all_gather | solution.py:272
  47.3 306.1 %all-gather.18.cloned.1.call-start = ((), (), s32[]{:S(2)}) async-start(), calls=%async_computation.10 | async-start | bytes 2359296 | tf_op jit(solution)/shard_map/all_gather | solution.py:314
  303.9 99.8 %all-gather.30.cloned.1.call-start = ((), (), s32[]{:S(2)}) async-start(), calls=%async_computation.27 | async-start | bytes 2359296 | tf_op jit(solution)/shard_map/all_gather | solution.py:315
  305.9 150.1 %all-gather.20.cloned.1.call-start = ((), (), s32[]{:S(2)}) async-start(), calls=%async_computation.11 | async-start | bytes 2359296 | tf_op jit(solution)/shard_map/all_gather | solution.py:273
  306.7 202.6 %all-reduce.7.cloned.1.call-start = ((), (), s32[]{:S(2)}) async-start(), calls=%async_computation.12 | async-start | bytes 4194304 | tf_op jit(solution)/shard_map/psum | solution.py:73
  459.6 216.2 %all-gather.22.cloned.1.call-start = ((), (), s32[]{:S(2)}) async-start(), calls=%async_computation.13 | async-start | bytes 12976128 | tf_op jit(solution)/shard_map/all_gather | solution.py:274
  462.9 307.4 %all-gather.24.cloned.1.call-start = ((), (), s32[]{:S(2)}) async-start(), calls=%async_computation.14 | async-start | bytes 6488064 | tf_op jit(solution)/shard_map/all_gather | solution.py:275
  463.9 362.1 %all-reduce.9.cloned.1.call-start = ((), (), s32[]{:S(2)}) async-start(), calls=%async_computation.15 | async-start | bytes 4194304 | tf_op jit(solution)/shard_map/psum | solution.py:73
  511.9 818.3 %copy-start = (f32[256,2048]{1,0:T(8,128)}, f32[256,2048]{1,0:T(8,128)S(1)}, u32[]{:S(2)}) copy-start(f32[256,2048]{1,0:T(8,128)S(1)} %get-tuple-element.949) | copy-start | bytes 6291460
  511.9 818.3 %copy-start.38 = (f32[256]{0:T(256)}, f32[256]{0:T(256)S(1)}, u32[]{:S(2)}) copy-start(f32[256]{0:T(256)S(1)} %add_rsqrt_fusion.1) | copy-start | bytes 3076
  776.3 127.2 %all-gather.26.cloned.1.call-start = ((), (), s32[]{:S(2)}) async-start(), calls=%async_computation.16 | async-start | bytes 4718592 | tf_op jit(solution)/shard_map/all_gather | solution.py:338
  829.8 389.3 %reduce-scatter.13.cloned.1.call-start = ((), (), s32[]{:S(2)}) async-start(), calls=%async_computation.17 | async-start | bytes 9437184 | tf_op jit(solution)/shard_map/reduce_scatter | solution.py:371
  867.1 193.5 %copy-start.46 = (s32[8,1,128]{2,1,0:T(1,128)}, s32[8,1,128]{2,1,0:T(1,128)S(1)}, u32[]{:S(2)}) copy-start(s32[8,1,128]{2,1,0:T(1,128)S(1)} %all-gather.5) | copy-start | bytes 12292
  1073.8 182.6 %all-reduce.11.cloned.1.call-start = ((), (), s32[]{:S(2)}) async-start(), calls=%async_computation.18 | async-start | bytes 2097152 | tf_op jit(solution)/shard_map/psum | solution.py:73
  1219.1 108.1 %all-reduce.13.cloned.1.call-start = ((), (), s32[]{:S(2)}) async-start(), calls=%async_computation.19 | async-start | bytes 4194304 | tf_op jit(solution)/shard_map/psum | solution.py:73
  1275.3 257.6 %reduce-scatter.15.cloned.1.call-start = ((), (), s32[]{:S(2)}) async-start(), calls=%async_computation.20 | async-start | bytes 9437184 | tf_op jit(solution)/shard_map/reduce_scatter | solution.py:414
  1350.4 184.8 %copy-start.37 = (f32[256,64]{0,1:T(8,128)S(1)}, f32[256,64]{0,1:T(8,128)}, u32[]{:S(2)}) copy-start(f32[256,64]{0,1:T(8,128)} %get-tuple-element.986) | copy-start | bytes 196612
  1350.4 242.7 %all-reduce.15.cloned.1.call-start = ((), (), s32[]{:S(2)}) async-start(), calls=%async_computation.21 | async-start | bytes 4194304 | tf_op jit(solution)/shard_map/psum | solution.py:73
  1542.6 143.2 %reduce-scatter.19.cloned.1.call-start = ((), (), s32[]{:S(2)}) async-start(), calls=%async_computation.24 | async-start | bytes 4718592 | tf_op jit(solution)/shard_map/reduce_scatter | solution.py:440
  1546.9 206.3 %reduce-scatter.25.cloned.1.call-start = ((), (), s32[]{:S(2)}) async-start(), calls=%async_computation.28 | async-start | bytes 1179648
  1596.7 352.1 %reduce-scatter.23.cloned.1.call-start = ((), (), s32[]{:S(2)}) async-start(), calls=%async_computation.26 | async-start | bytes 12976128 | tf_op jit(solution)/shard_map/reduce_scatter | solution.py:442
  1604.4 471.2 %all-gather.28.cloned.1.call-start = ((), (), s32[]{:S(2)}) async-start(), calls=%async_computation.22 | async-start | bytes 9437184 | tf_op jit(solution)/shard_map/all_gather | solution.py:433
  1608.3 676.7 %reduce-scatter.17.cloned.1.call-start = ((), (), s32[]{:S(2)}) async-start(), calls=%async_computation.23 | async-start | bytes 14155776 | tf_op jit(solution)/shard_map/reduce_scatter | solution.py:439
  1615.0 1046.0 %reduce-scatter.21.cloned.1.call-start = ((), (), s32[]{:S(2)}) async-start(), calls=%async_computation.25 | async-start | bytes 25952256 | tf_op jit(solution)/shard_map/reduce_scatter | solution.py:441
  1626.9 448.6 %copy-start.45 = (s32[1000]{0:T(1024)S(1)}, s32[1000]{0:T(1024)}, u32[]{:S(2)}) copy-start(s32[1000]{0:T(1024)} %copy-done.44) | copy-start | bytes 12004
  1627.0 448.6 %copy-start.53 = (s32[8,1,256]{2,1,0:T(1,128)S(1)}, s32[8,1,256]{2,1,0:T(1,128)}, u32[]{:S(2)}) copy-start(s32[8,1,256]{2,1,0:T(1,128)} %copy-done.52) | copy-start | bytes 24580
  1951.1 136.5 %copy-start.47 = (s32[8,1,128]{2,1,0:T(1,128)S(1)}, s32[8,1,128]{2,1,0:T(1,128)}, u32[]{:S(2)}) copy-start(s32[8,1,128]{2,1,0:T(1,128)} %copy-done.46) | copy-start | bytes 12292
  1951.1 136.5 %copy-start.57 = (f32[1024]{0:T(1024)S(1)}, f32[1024]{0:T(1024)}, u32[]{:S(2)}) copy-start(f32[1024]{0:T(1024)} %copy-done.56) | copy-start | bytes 12292
  1951.1 136.5 %copy-start.59 = (f32[1024]{0:T(1024)S(1)}, f32[1024]{0:T(1024)}, u32[]{:S(2)}) copy-start(f32[1024]{0:T(1024)} %copy-done.58) | copy-start | bytes 12292
  2096.2 611.4 %copy-start.13 = (f32[256,2,1408]{2,1,0:T(2,128)S(1)}, f32[256,2,1408]{2,1,0:T(2,128)}, u32[]{:S(2)}) copy-start(f32[256,2,1408]{2,1,0:T(2,128)} %param.41) | copy-start | bytes 8650756
  (56 other events, 563.5 us)
Sparse Core Ops, SparseCore 0:
  45.0 146.6 reduce-scatter.10
  194.8 98.0 all-gather.15
  304.0 49.2 all-gather.17
  356.2 47.4 all-gather.29
  406.4 49.5 all-gather.19
  459.7 49.5 all-reduce.6
  512.1 163.7 all-gather.21
  678.5 91.7 all-gather.23
  776.4 49.5 all-reduce.8
  829.9 73.5 all-gather.25
  1073.9 145.1 reduce-scatter.12
  1221.3 35.0 all-reduce.10
  1275.5 51.7 all-reduce.12
  1350.5 182.3 reduce-scatter.14
  1542.7 50.3 all-reduce.14
  1597.2 88.5 reduce-scatter.18
  1690.0 63.1 reduce-scatter.24
  1756.6 192.0 reduce-scatter.22
  1951.5 124.0 all-gather.27
  2079.0 205.9 reduce-scatter.16
  2288.9 372.1 reduce-scatter.20
where the time goes:
time: 2780 us; the launch traced here: 2770 us
  waiting for transfers between devices  2150 us (77%)
  blocking collectives  283 us (10%)
  matrix products  136 us (5%)
  other arithmetic  84 us (3%)
  local copies, waits for them, and re-layouts  81.7 us (3%)
  between operations  28 us (1%)
    reduce_scatter x1, waiting for transfers between devices, body(): lax.psum_scatter(gate_up_local, 'dp', scatter_dimension=0, tiled=True)  372 us
    psum x5, waiting for transfers between devices, model_sum(): return lax.psum(values, 'mp')  227 us
    reduce_scatter x1, waiting for transfers between devices, body(): lax.psum_scatter(down_local, 'dp', scatter_dimension=1, tiled=True)  193 us
    reduce_scatter x1, waiting for transfers between devices, body(): lax.psum_scatter(qkv_local, 'dp', scatter_dimension=0, tiled=True)  189 us
    reduce_scatter x1, waiting for transfers between devices, body(): lax.psum_scatter(key_terms, 'dp', scatter_dimension=0, tiled=True)  182 us
    all_gather x1, waiting for transfers between devices, body(): lax.all_gather(gate_up_weight.astype(jnp.bfloat16), 'dp', axis=0, tiled=T...  164 us
    reduce_scatter x1, waiting for transfers between devices, body(): lax.psum_scatter(row_terms, 'dp', scatter_dimension=0, tiled=True)  145 us
    all_gather x1, waiting for transfers between devices, body(): lax.all_gather(dzero_low, 'dp', axis=0, tiled=True)  124 us
  transfers between devices with their start and end apart: 21, of which 21 were waited for; matrix products, arithmetic and copies ran while one was open for 3% of the time, Pallas kernels for 0%

commit v1 on v0

v1 whole, which is shorter than its diff:
```python
import functools
import math

import jax
import jax.numpy as jnp
from jax import lax
from jax.experimental import pallas as pl
from jax.experimental.pallas import tpu as pltpu
from jax.sharding import PartitionSpec as P

HEAD_DIM = 128
R_DEV = 64
STEP = 10


EPS_NORM = 1e-05
BETA_ONE = 0.9
BETA_TWO = 0.95
ADAM_EPS = 1e-08
DECAY = 0.1
RATE_MATRIX = 0.02
RATE_GAIN = 1.0
CLIP = 0.02
EXIT_SCALE = (1.0 / 3.0, 2.0 / 3.0)
NEG = -1e30
BOTH = ("dp", "mp")
MESH = pl.DeviceIdType.MESH
VMEM_LIMIT = 60 * 1024 * 1024
ANY = pl.BlockSpec(memory_space=pl.ANY)


def kernel_mesh():
    return lax.axis_size("dp") == 8 and lax.axis_size("mp") == 4


def place():
    data_index, model_index = lax.axis_index("dp"), lax.axis_index("mp")
    return (data_index // 2, data_index % 2, model_index // 2, model_index % 2)


def z_peers(z):
    return (z, z + 1 - 2 * (z % 2), (z + 2) % 4, 3 - z)


def device(z, y, x, c):
    return (z * 2 + y, x * 2 + c)


def chunk(ref, rows, z, y, x, c):
    start = ((z * 2 + y) * 4 + x * 2 + c) * rows
    return ref.at[pl.ds(pl.multiple_of(start, rows), rows)]


def greet(peers):
    barrier = pltpu.get_barrier_semaphore()
    for peer in peers:
        pl.semaphore_signal(barrier, inc=1, device_id=peer, device_id_type=MESH)
    pl.semaphore_wait(barrier, len(peers))


def comm_params(ident):
    return pltpu.CompilerParams(
        collective_id=ident, has_side_effects=True, vmem_limit_bytes=VMEM_LIMIT
    )


def gather_kernel(rows, x_ref, o_ref, send_sem, recv_sem, own_sem):
    z, y, x, c = place()
    zs = z_peers(z)
    x_side, y_side, c_side = device(z, y, 1 - x, c), device(z, 1 - y, x, c), device(z, y, x, 1 - c)
    greet([device(zs[d], y, x, c) for d in (1, 2, 3)] + [x_side, y_side, c_side])
    origins = ((y, x), (y, 1 - x), (1 - y, x), (1 - y, 1 - x))
    sent = []

    def send(source, target, d, group, core):
        copy = pltpu.make_async_remote_copy(
            src_ref=source[0],
            dst_ref=source[1],
            send_sem=send_sem.at[len(sent)],
            recv_sem=recv_sem.at[(d * 4 + group) * 2 + core],
            device_id=target,
            device_id_type=MESH,
        )
        copy.start()
        sent.append(copy)

    def spot(d, group, core=0):
        oy, ox = origins[group]
        return chunk(o_ref, rows, zs[d], oy, ox, c if core == 0 else 1 - c)

    def arrived(d, group, core):
        here = spot(d, group, core)
        pltpu.make_async_copy(here, here, recv_sem.at[(d * 4 + group) * 2 + core]).wait()

    mine = (x_ref, spot(0, 0))
    own = pltpu.make_async_copy(x_ref, spot(0, 0), own_sem)
    own.start()
    for d in (3, 2, 1):
        send(mine, device(zs[d], y, x, c), d, 0, 0)
    send(mine, x_side, 0, 1, 0)
    send(mine, y_side, 0, 2, 0)
    send(mine, c_side, 0, 0, 1)
    for d in (1, 2, 3):
        arrived(d, 0, 0)
        here = (spot(d, 0), spot(d, 0))
        send(here, x_side, d, 1, 0)
        send(here, y_side, d, 2, 0)
        send(here, c_side, d, 0, 1)
    for d in (0, 1, 2, 3):
        for group, side in ((1, y_side), (2, x_side)):
            arrived(d, group, 0)
            here = (spot(d, group), spot(d, group))
            if (d % 2 == 0) == (group == 1):
                send(here, side, d, 3, 0)
            send(here, c_side, d, group, 1)
    for d in (0, 1, 2, 3):
        arrived(d, 3, 0)
        send((spot(d, 3), spot(d, 3)), c_side, d, 3, 1)
    for d in (0, 1, 2, 3):
        for group in range(4):
            arrived(d, group, 1)
    own.wait()
    for copy in sent:
        copy.wait_send()


def gather_all(value, ident):
    if not kernel_mesh():
        return lax.all_gather(value, BOTH, axis=0, tiled=True)
    rows, width = value.shape
    return pl.pallas_call(
        functools.partial(gather_kernel, rows),
        out_shape=jax.ShapeDtypeStruct((32 * rows, width), value.dtype),
        in_specs=[ANY],
        out_specs=ANY,
        scratch_shapes=[
            pltpu.SemaphoreType.DMA((31,)),
            pltpu.SemaphoreType.DMA((32,)),
            pltpu.SemaphoreType.DMA,
        ],
        compiler_params=comm_params(ident),
    )(value)


def scatter_kernel(
    rows, p_ref, o_ref, core_buf, diag_buf, side_buf, z_buf, held, send_sem, recv_sem
):
    z, y, x, c = place()
    zs = z_peers(z)
    x_side, y_side, c_side = device(z, y, 1 - x, c), device(z, 1 - y, x, c), device(z, y, x, 1 - c)
    greet([device(zs[d], y, x, c) for d in (1, 2, 3)] + [x_side, y_side, c_side])
    origins = ((y, x), (y, 1 - x), (1 - y, x), (1 - y, 1 - x))
    step = 16
    sent = []

    def send(source, target, slot_ref, slot):
        copy = pltpu.make_async_remote_copy(
            src_ref=source,
            dst_ref=slot_ref,
            send_sem=send_sem.at[len(sent)],
            recv_sem=recv_sem.at[slot],
            device_id=target,
            device_id_type=MESH,
        )
        copy.start()
        sent.append(copy)

    def arrived(slot_ref, slot):
        pltpu.make_async_copy(slot_ref, slot_ref, recv_sem.at[slot]).wait()

    def part(d, group, core=0):
        oy, ox = origins[group]
        return chunk(p_ref, rows, zs[d], oy, ox, c if core == 0 else 1 - c)

    def add(target, sources):
        @pl.loop(0, rows // step)
        def _(index):
            at = pl.ds(index * step, step)
            total = sources[0][at].astype(jnp.float32)
            for source in sources[1:]:
                total = total + source[at].astype(jnp.float32)
            target[at] = total.astype(target.dtype)

    order = [(d, 3) for d in range(4)]
    order += [(d, group) for d in range(4) for group in (1, 2)]
    order += [(d, 0) for d in (3, 2, 1, 0)]
    for d, group in order:
        send(part(d, group, 1), c_side, core_buf.at[d * 4 + group], d * 4 + group)
    for d, group in order:
        slot = d * 4 + group
        arrived(core_buf.at[slot], slot)
        terms = [part(d, group), core_buf.at[slot]]
        if group == 3:
            add(held.at[slot], terms)
            send(held.at[slot], y_side if d % 2 == 0 else x_side, diag_buf.at[d], 16 + d)
        elif group in (1, 2):
            if (d % 2 == 0) == (group == 1):
                arrived(diag_buf.at[d], 16 + d)
                terms.append(diag_buf.at[d])
            add(held.at[slot], terms)
            side = d * 2 + group - 1
            target = x_side if group == 1 else y_side
            send(held.at[slot], target, side_buf.at[side], 20 + side)
        else:
            for side in (d * 2, d * 2 + 1):
                arrived(side_buf.at[side], 20 + side)
                terms.append(side_buf.at[side])
            if d == 0:
                for peer in (1, 2, 3):
                    arrived(z_buf.at[peer - 1], 27 + peer)
                    terms.append(z_buf.at[peer - 1])
                add(o_ref, terms)
            else:
                add(held.at[slot], terms)
                send(held.at[slot], device(zs[d], y, x, c), z_buf.at[d - 1], 27 + d)
    for copy in sent:
        copy.wait_send()


def scatter_sum(value, ident):
    if not kernel_mesh():
        return lax.psum_scatter(value, BOTH, scatter_dimension=0, tiled=True).astype(jnp.float32)
    rows, width = value.shape[0] // 32, value.shape[1]
    low = value.dtype
    return pl.pallas_call(
        functools.partial(scatter_kernel, rows),
        out_shape=jax.ShapeDtypeStruct((rows, width), jnp.float32),
        in_specs=[pl.BlockSpec(memory_space=pltpu.VMEM)],
        out_specs=pl.BlockSpec(memory_space=pltpu.VMEM),
        scratch_shapes=[
            pltpu.VMEM((16, rows, width), low),
            pltpu.VMEM((4, rows, width), low),
            pltpu.VMEM((8, rows, width), low),
            pltpu.VMEM((3, rows, width), low),
            pltpu.VMEM((16, rows, width), low),
            pltpu.SemaphoreType.DMA((31,)),
            pltpu.SemaphoreType.DMA((31,)),
        ],
        compiler_params=comm_params(ident),
    )(value)


def exchange_kernel(count, whole, *refs):
    ins, outs = refs[: len(whole)], refs[len(whole) : 2 * len(whole)]
    send_sem, recv_sem, own_sem = refs[2 * len(whole) :]
    me, model_index = lax.axis_index("dp"), lax.axis_index("mp")
    peers = [lax.rem(me + shift, count) for shift in range(1, count)]
    greet([(peer, model_index) for peer in peers])
    owns, sent = [], []
    for array, keep in enumerate(whole):
        own = pltpu.make_async_copy(
            ins[array] if keep else ins[array].at[me], outs[array].at[me], own_sem.at[array]
        )
        own.start()
        owns.append(own)
        for shift in range(count - 1):
            copy = pltpu.make_async_remote_copy(
                src_ref=ins[array] if keep else ins[array].at[peers[shift]],
                dst_ref=outs[array].at[me],
                send_sem=send_sem.at[array, shift],
                recv_sem=recv_sem.at[array, shift],
                device_id=(peers[shift], model_index),
                device_id_type=MESH,
            )
            copy.start()
            sent.append(copy)
    for own in owns:
        own.wait()
    for array in range(len(whole)):
        for shift in range(count - 1):
            source = lax.rem(me + count - 1 - shift, count)
            here = outs[array].at[source]
            pltpu.make_async_copy(here, here, recv_sem.at[array, shift]).wait()
    for copy in sent:
        copy.wait_send()


def exchange(values, whole, ident):
    count = lax.axis_size("dp")
    if not kernel_mesh():
        return [
            lax.all_gather(value, "dp")
            if keep
            else lax.all_to_all(value, "dp", split_axis=0, concat_axis=0, tiled=True)
            for value, keep in zip(values, whole)
        ]
    shapes = [
        jax.ShapeDtypeStruct(((count,) if keep else ()) + value.shape, value.dtype)
        for value, keep in zip(values, whole)
    ]
    return pl.pallas_call(
        functools.partial(exchange_kernel, count, tuple(whole)),
        out_shape=shapes,
        in_specs=[ANY] * len(values),
        out_specs=[ANY] * len(values),
        scratch_shapes=[
            pltpu.SemaphoreType.DMA((len(values), count - 1)),
            pltpu.SemaphoreType.DMA((len(values), count - 1)),
            pltpu.SemaphoreType.DMA((len(values),)),
        ],
        compiler_params=comm_params(ident),
    )(*values)


def norm_fwd(values, gain):
    row_scale = lax.rsqrt(jnp.mean(values * values, axis=-1, keepdims=True) + EPS_NORM)
    unit_rows = values * row_scale
    return (unit_rows * gain, unit_rows, row_scale)


def norm_back(unit_rows, row_scale, gain, gradient):
    weighted = gradient * gain
    back_rows = row_scale * (
        weighted - unit_rows * jnp.mean(weighted * unit_rows, axis=-1, keepdims=True)
    )
    return (back_rows, jnp.sum(gradient * unit_rows, axis=0))


def rotary(places, width):
    half_width = width // 2
    frequency = jnp.exp(
        jnp.arange(half_width, dtype=jnp.float32) * (-math.log(10000.0) / half_width)
    )
    angles = places.astype(jnp.float32)[:, None] * frequency[None, :]
    return (jnp.cos(angles), jnp.sin(angles))


def rotate_pairs(values, cosine, sine_table):
    half_width = values.shape[-1] // 2
    front_half = values[..., :half_width]
    back_half = values[..., half_width:]
    return jnp.concatenate(
        [
            front_half * cosine - back_half * sine_table,
            back_half * cosine + front_half * sine_table,
        ],
        axis=-1,
    )


def dot(left, right, left_dim=1, right_dim=0):
    return lax.dot_general(
        left, right, (((left_dim,), (right_dim,)), ((), ())), preferred_element_type=jnp.float32
    )


def adam_update(weight, moment_one, moment_two, gradient, rate, decay):
    moment_one = BETA_ONE * moment_one + (1.0 - BETA_ONE) * gradient
    moment_two = BETA_TWO * moment_two + (1.0 - BETA_TWO) * gradient * gradient
    ratio = (
        moment_one
        / (1.0 - BETA_ONE**STEP)
        / (jnp.sqrt(moment_two / (1.0 - BETA_TWO**STEP)) + ADAM_EPS)
    )
    return (weight - rate * (ratio + decay * weight), moment_one, moment_two)


def body(
    token_ids,
    target_ids,
    exit_mask,
    table,
    table_first,
    table_second,
    qkv_weight,
    qkv_first,
    qkv_second,
    out_weight,
    out_first,
    out_second,
    gate_up_weight,
    gate_up_first,
    gate_up_second,
    down_weight,
    down_first,
    down_second,
    gains,
    gains_first,
    gains_second,
):
    low = jnp.bfloat16
    data_size, model_size = lax.axis_size("dp"), lax.axis_size("mp")
    data_index, model_index = lax.axis_index("dp"), lax.axis_index("mp")
    devices = data_size * model_size
    block_rows = token_ids.shape[0]
    tokens = block_rows * data_size
    width = table.shape[1]
    width_here = qkv_weight.shape[0]
    heads_here = qkv_weight.shape[2] // HEAD_DIM
    hidden_here = down_weight.shape[0] // data_size
    vocab_here = table.shape[0]
    device_index = data_index * model_size + model_index
    vocab_ids = device_index * vocab_here + jnp.arange(vocab_here, dtype=jnp.int32)
    score_scale = 1.0 / math.sqrt(HEAD_DIM)

    sharers = data_size // heads_here
    shares = sharers // 2
    share_slots = data_size // shares * R_DEV
    exit_here = data_index % sharers % 2
    share_here = data_index % sharers // 2
    slots_here = R_DEV // model_size
    rows_here = block_rows // model_size

    ints, gain_low = exchange(
        [
            jnp.concatenate([token_ids[None], target_ids[None], exit_mask]),
            jnp.pad(gains.astype(low), ((0, 13), (0, 0))),
        ],
        (True, True),
        0,
    )
    gain_rows = jnp.moveaxis(gain_low[:, :3], 0, 1).reshape(3, width).astype(jnp.float32)
    all_ids = ints[:, 0].reshape(tokens)
    mask_blocks = jnp.moveaxis(ints[:, 2:], 0, 1)
    slot_ids = jnp.arange(R_DEV, dtype=jnp.int32)
    slot_ranks = jnp.cumsum(mask_blocks, axis=2) - 1
    pick_int = (
        (slot_ranks[:, :, None, :] == slot_ids[:, None]) & (mask_blocks[:, :, None, :] == 1)
    ).astype(jnp.int32)
    pick_low = pick_int.astype(low)
    token_places = jnp.arange(tokens, dtype=jnp.int32)
    slot_targets = jnp.sum(pick_int * ints[:, 1][None, :, None, :], axis=3).reshape(2, -1)
    slot_places = jnp.sum(
        pick_int * token_places.reshape(1, data_size, 1, block_rows), axis=3
    ).reshape(2, -1)
    live = (slot_ids < jnp.sum(mask_blocks, axis=2)[:, :, None]).astype(jnp.float32).reshape(2, -1)
    counts = jnp.sum(live, axis=1)

    head_major = jnp.moveaxis(
        qkv_weight.astype(low).reshape(width_here, 3, heads_here, HEAD_DIM), 2, 0
    ).reshape(heads_here, width_here, 3 * HEAD_DIM)
    qkv_head, out_head, gate_up_cols, down_rows = exchange(
        [
            jnp.repeat(head_major, sharers, axis=0),
            jnp.repeat(
                out_weight.astype(low).reshape(heads_here, HEAD_DIM, width_here), sharers, axis=0
            ),
            jnp.moveaxis(
                gate_up_weight.astype(low).reshape(width_here, 2, data_size, hidden_here), 2, 0
            ).reshape(data_size, width_here, 2 * hidden_here),
            down_weight.astype(low).reshape(data_size, hidden_here, width_here),
        ],
        (False,) * 4,
        1,
    )
    qkv_head = qkv_head.reshape(width, 3 * HEAD_DIM)
    out_head = jnp.moveaxis(out_head, 0, 1).reshape(HEAD_DIM, width)
    gate_up_cols = gate_up_cols.reshape(width, 2 * hidden_here)
    down_rows = jnp.moveaxis(down_rows, 0, 1).reshape(hidden_here, width)

    table_low = table.astype(low)
    id_hits = (all_ids[:, None] == vocab_ids[None, :]).astype(low)
    resid_here = scatter_sum(dot(id_hits, table_low).astype(low), 2)
    resid_low = gather_all(resid_here.astype(low), 3)
    attn_low = norm_fwd(resid_low.astype(jnp.float32), gain_rows[0])[0].astype(low)

    projected = dot(attn_low, qkv_head)
    cosine, sine_table = rotary(token_places, HEAD_DIM)
    query_low = rotate_pairs(projected[:, :HEAD_DIM], cosine, sine_table).astype(low)
    key_low = rotate_pairs(projected[:, HEAD_DIM : 2 * HEAD_DIM], cosine, sine_table).astype(low)
    value_low = projected[:, 2 * HEAD_DIM :].astype(low)
    pick_share = lax.dynamic_slice_in_dim(
        lax.dynamic_index_in_dim(pick_low, exit_here, 0, keepdims=False),
        share_here * (data_size // shares),
        data_size // shares,
        0,
    )
    query_share = lax.dynamic_slice_in_dim(
        query_low.reshape(data_size, block_rows, HEAD_DIM),
        share_here * (data_size // shares),
        data_size // shares,
        0,
    )
    query_slots = (
        jnp.einsum("brt,btd->brd", pick_share, query_share, preferred_element_type=jnp.float32)
        .astype(low)
        .reshape(share_slots, HEAD_DIM)
    )

    def share_of(per_slot):
        return lax.dynamic_slice(per_slot, (exit_here, share_here * share_slots), (1, share_slots))[
            0
        ]

    places_share, live_share = share_of(slot_places), share_of(live)
    scores = dot(query_slots, key_low, 1, 1) * score_scale
    allowed = token_places[None, :] <= places_share[:, None]
    scores = jnp.where(allowed, scores, NEG)
    weights = jnp.exp(scores - jnp.max(scores, axis=-1, keepdims=True))
    probs = weights / jnp.sum(weights, axis=-1, keepdims=True)
    probs_low = probs.astype(low)
    attn_out = (dot(probs_low, value_low) * live_share[:, None]).astype(low)

    def spread(per_share):
        if shares > 1:
            full = jnp.zeros((data_size * R_DEV, width), per_share.dtype)
            per_share = lax.dynamic_update_slice_in_dim(
                full, per_share, share_here * share_slots, 0
            )
        exits = jnp.arange(2, dtype=jnp.int32)[None, :, None, None]
        rows = per_share.reshape(devices, 1, slots_here, width)
        return jnp.where(exits == exit_here, rows, 0).reshape(-1, width)

    out_slots = scatter_sum(spread(dot(attn_out, out_head).astype(low)), 4)
    block_low = lax.dynamic_slice_in_dim(resid_low, data_index * block_rows, block_rows, 0)
    pick_here = lax.dynamic_slice(
        pick_low,
        (0, data_index, model_index * slots_here, 0),
        (2, 1, slots_here, block_rows),
    ).reshape(2 * slots_here, block_rows)
    resid_one = dot(pick_here, block_low) + out_slots
    exit_one, unit_one, scale_one = norm_fwd(resid_one[:slots_here], gain_rows[2])
    mlp_in, mlp_unit, mlp_scale = norm_fwd(resid_one[slots_here:], gain_rows[1])
    first_rows = gather_all(jnp.concatenate([exit_one, mlp_in]).astype(low), 5).reshape(
        devices, 2, slots_here, width
    )
    exit_rows_one = first_rows[:, 0].reshape(-1, width)
    mlp_low = first_rows[:, 1].reshape(-1, width)

    gate_up = dot(mlp_low, gate_up_cols)
    gate_part, up_part = gate_up[:, :hidden_here], gate_up[:, hidden_here:]
    gate_sigma = jax.nn.sigmoid(gate_part)
    hidden_low = (gate_part * gate_sigma * up_part).astype(low)
    resid_two = resid_one[slots_here:] + scatter_sum(dot(hidden_low, down_rows).astype(low), 6)
    exit_two, unit_two, scale_two = norm_fwd(resid_two, gain_rows[2])
    exit_rows_two = gather_all(exit_two.astype(low), 7)

    exit_rows = (exit_rows_one, exit_rows_two)
    logits = [dot(rows, table_low, 1, 1) for rows in exit_rows]
    hits = [slot_targets[e][:, None] == vocab_ids[None, :] for e in range(2)]
    tops = [jnp.max(values, axis=1) for values in logits]
    masses = [jnp.sum(jnp.exp(values - top[:, None]), axis=1) for values, top in zip(logits, tops)]
    found = [jnp.sum(jnp.where(hit, values, 0.0), axis=1) for hit, values in zip(hits, logits)]
    stats = jnp.concatenate(tops + masses + found).reshape(-1, 128)
    stats = gather_all(stats, 8).reshape(devices, 3, 2, -1)
    row_top = jnp.max(stats[:, 0], axis=0)
    row_mass = jnp.sum(stats[:, 1] * jnp.exp(stats[:, 0] - row_top), axis=0)
    row_lse = row_top + jnp.log(row_mass)
    entropy = row_lse - jnp.sum(stats[:, 2], axis=0)
    loss_sums = jnp.sum(entropy * live, axis=1)
    row_weight = live * (jnp.array(EXIT_SCALE, jnp.float32) / counts)[:, None]
    grad_logits = [
        (
            row_weight[e][:, None]
            * (jnp.exp(logits[e] - row_lse[e][:, None]) - hits[e].astype(jnp.float32))
        ).astype(low)
        for e in range(2)
    ]
    table_head = dot(grad_logits[0], exit_rows_one, 0, 0) + dot(grad_logits[1], exit_rows_two, 0, 0)
    row_terms = jnp.stack(
        [
            dot(grad, table_low).astype(low).reshape(devices, slots_here, width)
            for grad in grad_logits
        ],
        axis=1,
    )
    row_grads = scatter_sum(row_terms.reshape(-1, width), 9)

    dexit_one, final_one = norm_back(unit_one, scale_one, gain_rows[2], row_grads[:slots_here])
    dresid_two, final_two = norm_back(unit_two, scale_two, gain_rows[2], row_grads[slots_here:])
    dtwo_low = gather_all(dresid_two.astype(low), 10)
    down_local = dot(hidden_low, dtwo_low, 0, 0)
    dhidden = dot(dtwo_low, down_rows, 1, 1)
    dgate = dhidden * up_part * gate_sigma * (1.0 + gate_part * (1.0 - gate_sigma))
    dup_part = dhidden * gate_part * gate_sigma
    dgate_up = jnp.concatenate([dgate, dup_part], axis=1).astype(low)
    gate_up_local = dot(mlp_low, dgate_up, 0, 0)
    dmlp_in = scatter_sum(dot(dgate_up, gate_up_cols, 1, 1).astype(low), 11)
    dmlp_rows, mlp_gain_grad = norm_back(mlp_unit, mlp_scale, gain_rows[1], dmlp_in)
    done_here = jnp.concatenate([dexit_one, dresid_two + dmlp_rows]).astype(low)
    done_low = gather_all(done_here, 12).reshape(devices, 2, slots_here, width)

    done_share = lax.dynamic_slice(
        lax.dynamic_index_in_dim(done_low, exit_here, 1, keepdims=False).reshape(-1, width),
        (share_here * share_slots, 0),
        (share_slots, width),
    )
    out_local = dot(attn_out, done_share, 0, 0)
    dattn_low = dot(done_share, out_head, 1, 1).astype(low)
    dprobs = dot(dattn_low, value_low, 1, 1)
    delta = jnp.sum(probs * dprobs, axis=-1, keepdims=True)
    dscores = (probs * (dprobs - delta)).astype(low)
    cosine_share, sine_share = rotary(places_share, HEAD_DIM)
    dquery = rotate_pairs(dot(dscores, key_low) * score_scale, cosine_share, -sine_share).astype(
        low
    )
    dquery_share = jnp.einsum(
        "brt,brd->btd",
        pick_share,
        dquery.reshape(-1, R_DEV, HEAD_DIM),
        preferred_element_type=jnp.float32,
    ).astype(low)
    if shares > 1:
        dquery_share = lax.dynamic_update_slice_in_dim(
            jnp.zeros((data_size, block_rows, HEAD_DIM), low),
            dquery_share,
            share_here * (data_size // shares),
            0,
        )
    dkey = rotate_pairs(dot(dscores, query_slots, 0, 0) * score_scale, cosine, -sine_table)
    dvalue = dot(probs_low, dattn_low, 0, 0)
    dprojected = jnp.concatenate(
        [dquery_share.reshape(tokens, HEAD_DIM), dkey.astype(low), dvalue.astype(low)], axis=1
    )
    qkv_local = dot(attn_low, dprojected, 0, 0)
    dattn_in = scatter_sum(dot(dprojected, qkv_head, 1, 1).astype(low), 13)

    _, attn_unit, attn_scale = norm_fwd(resid_here, gain_rows[0])
    dattn_rows, attn_gain_grad = norm_back(attn_unit, attn_scale, gain_rows[0], dattn_in)
    done_block = lax.dynamic_slice_in_dim(done_low, data_index * model_size, model_size, 0)
    pick_block = lax.dynamic_slice(
        pick_low,
        (0, data_index, 0, model_index * rows_here),
        (2, 1, R_DEV, rows_here),
    ).reshape(2, model_size, slots_here, rows_here)
    dresid_here = jnp.einsum(
        "emst,mesd->td", pick_block, done_block, preferred_element_type=jnp.float32
    )
    dzero_low = gather_all((dresid_here + dattn_rows).astype(low), 14)
    table_grad = table_head + dot(id_hits, dzero_low, 0, 0)

    gain_local = jnp.stack([attn_gain_grad, mlp_gain_grad, final_one + final_two])
    gain_sums = jnp.sum(
        gather_all(gain_local.reshape(-1, 128), 15).reshape(devices, 3, width), axis=0
    )
    qkv_parts, out_parts, gate_up_parts, down_parts = exchange(
        [
            qkv_local.astype(low).reshape(data_size, width_here, 3 * HEAD_DIM),
            jnp.moveaxis(out_local.astype(low).reshape(HEAD_DIM, data_size, width_here), 1, 0),
            gate_up_local.astype(low).reshape(data_size, width_here, 2 * hidden_here),
            jnp.moveaxis(down_local.astype(low).reshape(hidden_here, data_size, width_here), 1, 0),
        ],
        (False,) * 4,
        16,
    )
    qkv_grad = jnp.sum(
        qkv_parts.reshape(heads_here, sharers, width_here, 3, HEAD_DIM).astype(jnp.float32), axis=1
    )
    qkv_grad = jnp.moveaxis(qkv_grad, 0, 2).reshape(qkv_weight.shape)
    out_grad = jnp.sum(
        out_parts.reshape(heads_here, sharers, HEAD_DIM, width_here).astype(jnp.float32), axis=1
    ).reshape(out_weight.shape)
    gate_up_grad = jnp.moveaxis(
        gate_up_parts.reshape(data_size, width_here, 2, hidden_here), 0, 2
    ).reshape(gate_up_weight.shape)
    gate_up_grad = gate_up_grad.astype(jnp.float32)
    down_grad = down_parts.reshape(down_weight.shape).astype(jnp.float32)
    gain_grad = lax.dynamic_slice_in_dim(gain_sums, data_index * width_here, width_here, 1)

    squares = (
        jnp.sum(table_grad * table_grad)
        + jnp.sum(qkv_grad * qkv_grad)
        + jnp.sum(out_grad * out_grad)
        + jnp.sum(gate_up_grad * gate_up_grad)
        + jnp.sum(down_grad * down_grad)
    )
    square_parts = gather_all(jnp.full((8, 128), squares), 17).reshape(devices, 8 * 128)
    grad_norm = jnp.sqrt(jnp.sum(square_parts[:, 0]) + jnp.sum(gain_sums * gain_sums))
    factor = jnp.minimum(1.0, CLIP / (grad_norm + 1e-06))
    table_new = adam_update(
        table, table_first, table_second, table_grad * factor, RATE_MATRIX, DECAY
    )
    qkv_new = adam_update(qkv_weight, qkv_first, qkv_second, qkv_grad * factor, RATE_MATRIX, DECAY)
    out_new = adam_update(out_weight, out_first, out_second, out_grad * factor, RATE_MATRIX, DECAY)
    gate_up_new = adam_update(
        gate_up_weight, gate_up_first, gate_up_second, gate_up_grad * factor, RATE_MATRIX, DECAY
    )
    down_new = adam_update(
        down_weight, down_first, down_second, down_grad * factor, RATE_MATRIX, DECAY
    )
    gains_new = adam_update(gains, gains_first, gains_second, gain_grad * factor, RATE_GAIN, 0.0)
    return (
        loss_sums,
        counts,
        grad_norm,
        *table_new,
        *qkv_new,
        *out_new,
        *gate_up_new,
        *down_new,
        *gains_new,
    )


def solution(mesh):
    rows, sides, cols, gain = P(BOTH, None), P("dp", None, "mp"), P("mp", "dp"), P(None, "dp")
    state = (rows,) * 3 + (sides,) * 3 + (cols,) * 3 + (sides,) * 3 + (cols,) * 3 + (gain,) * 3
    return jax.shard_map(
        body,
        mesh=mesh,
        in_specs=(P("dp"), P("dp"), P(None, "dp")) + state,
        out_specs=(P(), P(), P()) + state,
        check_vma=False,
    )
```

time: 2780 us -> 1030 us (0.37)
  waiting for transfers between devices: 2150 us -> 0 us
  Pallas kernels: 0 us -> 712 us
  blocking collectives: 283 us -> 0 us
  matrix products: 136 us -> 106 us
    reduce_scatter x7 -> x0, waiting for transfers between devices: 1250 us -> none  [the longest x1 372 us: body(): lax.psum_scatter(gate_up_local, 'dp', scatter_dimension=0, tiled=True)]
    pallas_call x0 -> x18, Pallas kernels: none -> 712 us  [the longest x6 267 us: scatter_sum(): pl.pallas_call(functools.partial(scatter_kernel, rows), out_shape=jax.Sha...]
    all_gather x8 -> x0, waiting for transfers between devices: 603 us -> none  [the longest x1 164 us: body(): lax.all_gather(gate_up_weight.astype(jnp.bfloat16), 'dp', axis=0, tiled=T...]
    psum x5 -> x0, waiting for transfers between devices: 227 us -> none  [model_sum(): return lax.psum(values, 'mp')]
    all_gather x7 -> x0, blocking collectives: 201 us -> none  [the longest x3 114 us: joined(): pieces = jax.tree.map(lambda part: lax.all_gather(part, axis), value)]
    psum x2 -> x0, blocking collectives: 81.8 us -> none  [the longest x1 42.3 us: model_sum(): return lax.psum(values, 'mp')]
    unnamed x22 -> x0, waiting for transfers between devices: 66 us -> none
    dot_general x26 -> x30, matrix products: 136 us -> 106 us  [the longest x27 102 us: dot(): lax.dot_general(left, right, (((left_dim,), (right_dim,)), ((), ())), pre...]
  transfers between devices with their start and end apart: 21 -> 0, of which waited for: 21 -> 0; matrix products, arithmetic and copies ran while one was open for 3% -> 0% of each run, Pallas kernels for 0% -> 0%
where the time goes in v1:
time: 1030 us; the launch traced here: 1020 us
  Pallas kernels  712 us (69%)
  other arithmetic  109 us (11%)
  matrix products  106 us (10%)
  local copies, waits for them, and re-layouts  87.5 us (8%)
    pallas_call x6, Pallas kernels, scatter_sum(): pl.pallas_call(functools.partial(scatter_kernel, rows), out_shape=jax.Sha...  267 us
    pallas_call x9, Pallas kernels, gather_all(): pl.pallas_call(functools.partial(gather_kernel, rows), out_shape=jax.Shap...  247 us
    pallas_call x3, Pallas kernels, exchange(): pl.pallas_call(functools.partial(exchange_kernel, count, tuple(whole)), o...  198 us
    dot_general x27, matrix products, dot(): lax.dot_general(left, right, (((left_dim,), (right_dim,)), ((), ())), pre...  102 us
    unnamed x224, local copies, waits for them, and re-layouts  52.3 us
    sub x6, other arithmetic, adam_update(): return (weight - rate * (ratio + decay * weight), moment_one, moment_two)  43.8 us

profile of v1, /device:TPU:0, one launch (start us, length us, event | category | flops | bytes accessed | tf_op | source)
XLA Modules:
  0.0 1022.8 jit_solution(7107991959528203626)
XLA Ops:
  3.3 9.6 shard_map.373
  29.3 93.9 %shard_map.376 = (bf16[8,256,384]{2,1,0:T(8,128)(2,1)}, bf16[8,128,256]{2,1,0:T(8,128)(2,1)}, bf16[8,256,352]{2,1,0:T(8,128)(2,1)}, bf16[8,176,256]{2,1,0:T(8,128)(2,1)}) custom-call(bf16[8,256,384]{2,1,0:T(8,128)(2,1)} %bitcast.208, bf16[8,128,256]{2,1,0:T(8,128)(2,1)} %bitcast.222, bf16[8,256,352]{2,1,0:T(8,128)(2,1)} %copy.204.refs_2_, ...), custom_call_target="tpu_custom_call" | custom-call | tf_op jit(solution)/shard_map/pallas_call | solution.py:291
  123.2 5.9 convert_element_type.206
  129.1 13.3 %fusion.8.p_ref = bf16[2048,2048]{1,0:T(8,128)(2,1)} fusion(bf16[1000,2048]{1,0:T(8,128)(2,1)} %convert_element_type.206, s32[1000]{0:T(1024)S(1)} %iota_add_fusion, s32[2048]{0:T(1024)S(1)} %bitcast.276), kind=kOutput, calls=%fused_computation.15 | convolution fusion | flops 8394850304 | bytes 12496800 | tf_op jit(solution)/shard_map/dot_general | solution.py:342
  142.5 73.2 %shard_map.374 = f32[64,2048]{1,0:T(8,128)} custom-call(bf16[2048,2048]{1,0:T(8,128)(2,1)} %fusion.8.p_ref), custom_call_target="tpu_custom_call" | custom-call | tf_op jit(solution)/shard_map/pallas_call | solution.py:225
  218.2 52.8 %shard_map.375 = bf16[2048,2048]{1,0:T(8,128)(2,1)} custom-call(bf16[64,2048]{1,0:T(8,128)(2,1)} %get-tuple-element.203.x_ref), custom_call_target="tpu_custom_call" | custom-call | tf_op jit(solution)/shard_map/pallas_call | solution.py:131
  277.6 5.3 fusion.21
  306.3 39.0 %shard_map.377 = f32[32,2048]{1,0:T(8,128)} custom-call(bf16[1024,2048]{1,0:T(8,128)(2,1)} %bitcast_select_fusion.p_ref), custom_call_target="tpu_custom_call" | custom-call | tf_op jit(solution)/shard_map/pallas_call | solution.py:225
  349.1 29.7 %shard_map.378 = bf16[1024,2048]{1,0:T(8,128)(2,1)} custom-call(bf16[32,2048]{1,0:T(8,128)(2,1)} %pad_maximum_fusion.10.x_ref), custom_call_target="tpu_custom_call" | custom-call | tf_op jit(solution)/shard_map/pallas_call | solution.py:131
  391.2 23.3 %shard_map.379 = f32[16,2048]{1,0:T(8,128)} custom-call(bf16[512,2048]{1,0:T(8,128)(2,1)} %convolution_convert_fusion.3.p_ref), custom_call_target="tpu_custom_call" | custom-call | tf_op jit(solution)/shard_map/pallas_call | solution.py:225
  417.6 18.5 %shard_map.380 = bf16[512,2048]{1,0:T(8,128)(2,1)} custom-call(bf16[16,2048]{1,0:T(8,128)(2,1)} %multiply_convert_fusion.5.x_ref), custom_call_target="tpu_custom_call" | custom-call | tf_op jit(solution)/shard_map/pallas_call | solution.py:131
  436.1 5.8 fusion.131
  447.2 13.6 %shard_map.381 = f32[768,128]{1,0:T(8,128)} custom-call(f32[24,128]{1,0:T(8,128)} %concatenate.71.x_ref), custom_call_target="tpu_custom_call" | custom-call | tf_op jit(solution)/shard_map/pallas_call | solution.py:131
  473.3 39.1 %shard_map.382 = f32[32,2048]{1,0:T(8,128)} custom-call(bf16[1024,2048]{1,0:T(8,128)(2,1)} %bitcast.199), custom_call_target="tpu_custom_call" | custom-call | tf_op jit(solution)/shard_map/pallas_call | solution.py:225
  516.0 19.3 %shard_map.383 = bf16[512,2048]{1,0:T(8,128)(2,1)} custom-call(bf16[16,2048]{1,0:T(8,128)(2,1)} %fusion.107.x_ref), custom_call_target="tpu_custom_call" | custom-call | tf_op jit(solution)/shard_map/pallas_call | solution.py:131
  540.7 23.1 %shard_map.384 = f32[16,2048]{1,0:T(8,128)} custom-call(bf16[512,2048]{1,0:T(8,128)(2,1)} %convolution_convert_fusion.5.p_ref), custom_call_target="tpu_custom_call" | custom-call | tf_op jit(solution)/shard_map/pallas_call | solution.py:225
  567.1 28.5 %shard_map.385 = bf16[1024,2048]{1,0:T(8,128)(2,1)} custom-call(bf16[32,2048]{1,0:T(8,128)(2,1)} %pad_maximum_fusion.11.x_ref), custom_call_target="tpu_custom_call" | custom-call | tf_op jit(solution)/shard_map/pallas_call | solution.py:131
  610.7 9.6 convolution_convert_fusion.p_ref
  620.2 68.8 %shard_map.386 = f32[64,2048]{1,0:T(8,128)} custom-call(bf16[2048,2048]{1,0:T(8,128)(2,1)} %convolution_convert_fusion.p_ref), custom_call_target="tpu_custom_call" | custom-call | tf_op jit(solution)/shard_map/pallas_call | solution.py:225
  692.6 51.7 %shard_map.387 = bf16[2048,2048]{1,0:T(8,128)(2,1)} custom-call(bf16[64,2048]{1,0:T(8,128)(2,1)} %fusion.24.x_ref), custom_call_target="tpu_custom_call" | custom-call | tf_op jit(solution)/shard_map/pallas_call | solution.py:131
  744.4 12.0 %fusion.3 = f32[1000,2048]{1,0:T(8,128)S(1)} fusion(bf16[2048,2048]{1,0:T(8,128)(2,1)} %shard_map.387, s32[1000]{0:T(1024)S(1)} %iota_add_fusion, s32[2048]{0:T(1024)S(1)} %bitcast.277), kind=kOutput, calls=%fused_computation.6 | convolution fusion | flops 8390656000 | bytes 16592800 | tf_op jit(solution)/shard_map/dot_general | solution.py:342
  756.5 5.9 fusion.111
  762.4 8.3 multiply_reduce_fusion
  770.8 6.3 convolution_convert_fusion.6
  786.6 94.6 %shard_map.388 = (bf16[8,256,384]{2,1,0:T(8,128)(2,1)}, bf16[8,128,256]{2,1,0:T(8,128)(2,1)}, bf16[8,256,352]{2,1,0:T(8,128)(2,1)}, bf16[8,176,256]{2,1,0:T(8,128)(2,1)}) custom-call(bf16[8,256,384]{2,1,0:T(8,128)(2,1)} %bitcast.231, bf16[8,128,256]{2,1,0:T(8,128)(2,1)} %bitcast.221, bf16[8,256,352]{2,1,0:T(8,128)(2,1)} %bitcast.209, ...), custom_call_target="tpu_custom_call" | custom-call | tf_op jit(solution)/shard_map/pallas_call | solution.py:291
  894.7 17.9 %shard_map.389 = f32[256,128]{1,0:T(8,128)} custom-call(f32[8,128]{1,0:T(8,128)} %broadcast_in_dim.94.x_ref), custom_call_target="tpu_custom_call" | custom-call | tf_op jit(solution)/shard_map/pallas_call | solution.py:131
  914.8 15.3 %shard_map.390 = f32[1536,128]{1,0:T(8,128)} custom-call(f32[48,128]{1,0:T(8,128)} %reshape.404.x_ref), custom_call_target="tpu_custom_call" | custom-call | tf_op jit(solution)/shard_map/pallas_call | solution.py:131
  933.7 22.4 %multiply_subtract_fusion = (f32[1000,2048]{1,0:T(8,128)}, f32[1000,2048]{1,0:T(8,128)}, f32[1000,2048]{1,0:T(8,128)}) fusion(f32[1000,2048]{1,0:T(8,128)} %param.25, f32[1000,2048]{1,0:T(8,128)} %get-tuple-element.228, f32[]{:T(128)S(6)} %min.3, f32[1000,2048]{1,0:T(8,128)} %param.26, f32[1000,2048]{1,0:T(8,128)} %param.27), kind=kLoop, calls=%fused_computation.11 | loop fusion | flops 32768000 | bytes 57344004 | tf_op jit(solution)/shard_map/sub | solution.py:355
  985.6 5.7 copy.229
  991.4 8.4 multiply_subtract_fusion.1
  999.7 5.5 copy.235
  1005.3 5.7 copy.236
  (375 shorter events, 182.4 us)
Async XLA Ops:
  129.1 13.4 %copy-start.91 = (s32[8,1,256]{2,1,0:T(1,128)}, s32[8,1,256]{2,1,0:T(1,128)S(1)}, u32[]{:S(2)}) copy-start(s32[8,1,256]{2,1,0:T(1,128)S(1)} %get-tuple-element.212) | copy-start | bytes 24580
  283.0 16.9 %copy-start.26 = (f32[2048,384]{0,1:T(8,128)}, f32[2048,384]{0,1:T(8,128)S(1)}, u32[]{:S(2)}) copy-start(f32[2048,384]{0,1:T(8,128)S(1)} %fusion.21) | copy-start | bytes 9437188
  442.1 20.9 %copy-start.37 = (bf16[2,8,64,256]{3,2,1,0:T(8,128)(2,1)S(1)}, bf16[2,8,64,256]{3,2,1,0:T(8,128)(2,1)}, u32[]{:S(2)}) copy-start(bf16[2,8,64,256]{3,2,1,0:T(8,128)(2,1)} %convert_convert_fusion) | copy-start | bytes 1572868
  442.1 21.0 %copy-start.81 = (f32[2,512]{1,0:T(2,128)S(1)}, f32[2,512]{1,0:T(2,128)}, u32[]{:S(2)}) copy-start(f32[2,512]{1,0:T(2,128)} %get-tuple-element.184) | copy-start | bytes 12292
  442.1 21.0 %copy-start.9 = (f32[512,1000]{0,1:T(8,128)S(1)}, f32[512,1000]{0,1:T(8,128)}, u32[]{:S(2)}) copy-start(f32[512,1000]{0,1:T(8,128)} %get-tuple-element.224) | copy-start | bytes 6144004
  473.3 39.2 %copy-start.20 = (f32[32,2048]{1,0:T(8,128)S(1)}, f32[32,2048]{1,0:T(8,128)}, u32[]{:S(2)}) copy-start(f32[32,2048]{1,0:T(8,128)} %copy-done.19) | copy-start | bytes 786436
  473.3 39.2 %copy-start.32 = (f32[16,2048]{1,0:T(8,128)S(1)}, f32[16,2048]{1,0:T(8,128)}, u32[]{:S(2)}) copy-start(f32[16,2048]{1,0:T(8,128)} %copy-done.31) | copy-start | bytes 393220
  473.3 39.2 %copy-start.94 = (f32[16]{0:T(128)S(1)}, f32[16]{0:T(128)}, u32[]{:S(2)}) copy-start(f32[16]{0:T(128)} %copy-done.93) | copy-start | bytes 196
  473.3 39.2 %copy-start.96 = (f32[16]{0:T(128)S(1)}, f32[16]{0:T(128)}, u32[]{:S(2)}) copy-start(f32[16]{0:T(128)} %copy-done.95) | copy-start | bytes 196
  512.5 22.8 %copy-start.36 = (bf16[8,22,8,256]{3,2,0,1:T(8,128)(2,1)S(1)}, bf16[8,22,8,256]{3,2,0,1:T(8,128)(2,1)}, u32[]{:S(2)}) copy-start(bf16[8,22,8,256]{3,2,0,1:T(8,128)(2,1)} %copy-done.35) | copy-start | bytes 2162692
  512.5 22.8 %copy-start.53 = (f32[512,352]{0,1:T(8,128)S(1)}, f32[512,352]{0,1:T(8,128)}, u32[]{:S(2)}) copy-start(f32[512,352]{0,1:T(8,128)} %copy-done.52) | copy-start | bytes 2162692
  538.0 25.8 %copy-start.64 = (bf16[512,176]{0,1:T(8,128)(2,1)}, bf16[512,176]{0,1:T(8,128)(2,1)S(1)}, u32[]{:S(2)}) copy-start(bf16[512,176]{0,1:T(8,128)(2,1)S(1)} %get-tuple-element.196) | copy-start | bytes 540676
  538.0 25.8 %copy-start.66 = (bf16[512,176]{0,1:T(8,128)(2,1)}, bf16[512,176]{0,1:T(8,128)(2,1)S(1)}, u32[]{:S(2)}) copy-start(bf16[512,176]{0,1:T(8,128)(2,1)S(1)} %get-tuple-element.197) | copy-start | bytes 540676
  540.7 23.1 %copy-start.84 = (f32[16]{0:T(128)S(1)}, f32[16]{0:T(128)}, u32[]{:S(2)}) copy-start(f32[16]{0:T(128)} %copy-done.83) | copy-start | bytes 196
  540.7 24.7 %copy-start.33 = (f32[32,2048]{1,0:T(8,128)S(1)}, f32[32,2048]{1,0:T(8,128)}, u32[]{:S(2)}) copy-start(f32[32,2048]{1,0:T(8,128)} %shard_map.382) | copy-start | bytes 786436
  567.1 30.5 %copy-start.30 = (bf16[128,8,256]{0,2,1:T(8,128)(2,1)S(1)}, bf16[128,8,256]{0,2,1:T(8,128)(2,1)}, u32[]{:S(2)}) copy-start(bf16[128,8,256]{0,2,1:T(8,128)(2,1)} %copy-done.29) | copy-start | bytes 1572868
  620.2 68.8 %copy-start.101 = (f32[64]{0:T(128)S(1)}, f32[64]{0:T(128)}, u32[]{:S(2)}) copy-start(f32[64]{0:T(128)} %get-tuple-element.202) | copy-start | bytes 772
  620.2 68.8 %copy-start.15 = (f32[64,2048]{1,0:T(8,128)S(1)}, f32[64,2048]{1,0:T(8,128)}, u32[]{:S(2)}) copy-start(f32[64,2048]{1,0:T(8,128)} %shard_map.374) | copy-start | bytes 1572868
  620.2 68.8 %copy-start.70 = (f32[1,8,256]{2,0,1:T(1,128)S(1)}, f32[1,8,256]{2,0,1:T(1,128)}, u32[]{:S(2)}) copy-start(f32[1,8,256]{2,0,1:T(1,128)} %copy-done.69) | copy-start | bytes 24580
  692.6 51.8 %copy-start.92 = (s32[8,1,256]{2,1,0:T(1,128)S(1)}, s32[8,1,256]{2,1,0:T(1,128)}, u32[]{:S(2)}) copy-start(s32[8,1,256]{2,1,0:T(1,128)} %copy-done.91) | copy-start | bytes 24580
  744.4 12.1 %copy-start.18 = (f32[512,1000]{0,1:T(8,128)S(1)}, f32[512,1000]{0,1:T(8,128)}, u32[]{:S(2)}) copy-start(f32[512,1000]{0,1:T(8,128)} %get-tuple-element.222) | copy-start | bytes 6144004
  744.4 12.1 %copy-start.42 = (bf16[32,1,16,2048]{3,2,1,0:T(8,128)(2,1)S(1)}, bf16[32,1,16,2048]{3,2,1,0:T(8,128)(2,1)}, u32[]{:S(2)}) copy-start(bf16[32,1,16,2048]{3,2,1,0:T(8,128)(2,1)} %copy-done.41) | copy-start | bytes 6291460
  744.4 12.1 %copy-start.72 = (f32[1,512]{1,0:T(1,128)S(1)}, f32[1,512]{1,0:T(1,128)}, u32[]{:S(2)}) copy-start(f32[1,512]{1,0:T(1,128)} %copy-done.71) | copy-start | bytes 6148
  756.5 14.3 %slice-start = ((s8[8388608]{0:T(1024)(128)(4,1)}), s8[4194304]{0:T(1024)(128)(4,1)S(1)}, s32[]{:S(2)}) async-start(s8[8388608]{0:T(1024)(128)(4,1)} %bitcast.194), calls=%async_computation | async-start | bytes 8388608
  762.4 8.3 slice-start.1
  762.4 8.3 copy-start.55
  762.4 8.3 copy-start.57
  762.4 8.3 copy-start.60
  762.4 8.3 copy-start.61
  885.9 28.2 %copy-start.73 = (f32[2048]{0:T(1024)S(1)}, f32[2048]{0:T(1024)}, u32[]{:S(2)}) copy-start(f32[2048]{0:T(1024)} %get-tuple-element.156) | copy-start | bytes 24580
  885.9 28.2 %copy-start.74 = (f32[2048]{0:T(1024)S(1)}, f32[2048]{0:T(1024)}, u32[]{:S(2)}) copy-start(f32[2048]{0:T(1024)} %get-tuple-element.159) | copy-start | bytes 24580
  885.9 28.2 %copy-start.75 = (f32[2048]{0:T(1024)S(1)}, f32[2048]{0:T(1024)}, u32[]{:S(2)}) copy-start(f32[2048]{0:T(1024)} %get-tuple-element.154) | copy-start | bytes 24580
  (73 other events, 219.8 us)

commit v2 on v1

v2 whole, which is shorter than its diff:
```python
import functools
import math

import jax
import jax.numpy as jnp
from jax import lax
from jax.experimental import pallas as pl
from jax.experimental.layout import Layout, with_layout_constraint
from jax.experimental.pallas import tpu as pltpu
from jax.sharding import PartitionSpec as P

HEAD_DIM = 128
R_DEV = 64
STEP = 10


EPS_NORM = 1e-05
BETA_ONE = 0.9
BETA_TWO = 0.95
ADAM_EPS = 1e-08
DECAY = 0.1
RATE_MATRIX = 0.02
RATE_GAIN = 1.0
CLIP = 0.02
EXIT_SCALE = (1.0 / 3.0, 2.0 / 3.0)
NEG = -1e30
BOTH = ("dp", "mp")
MESH = pl.DeviceIdType.MESH
VMEM_LIMIT = 60 * 1024 * 1024
ANY = pl.BlockSpec(memory_space=pl.ANY)
GROUP = 16


def kernel_mesh():
    return lax.axis_size("dp") == 8 and lax.axis_size("mp") == 4


def comm_params(ident):
    return pltpu.CompilerParams(
        collective_id=ident, has_side_effects=True, vmem_limit_bytes=VMEM_LIMIT
    )


class Links:
    def __init__(self, send_sem, recv_sem, cargo):
        data_index, model_index = lax.axis_index("dp"), lax.axis_index("mp")
        z, y, x, c = data_index // 2, data_index % 2, model_index // 2, model_index % 2
        self.c = c
        self.zs = (z, z + 1 - 2 * (z % 2), (z + 2) % 4, 3 - z)
        self.corners = ((y, x), (y, 1 - x), (1 - y, x), (1 - y, 1 - x))
        self.z_side = [(zd * 2 + y, model_index) for zd in self.zs]
        self.x_side = (data_index, (1 - x) * 2 + c)
        self.y_side = (z * 2 + 1 - y, model_index)
        self.c_side = (data_index, x * 2 + 1 - c)
        self.send_sem, self.recv_sem, self.sent, self.slots = send_sem, recv_sem, [], {}
        peers = self.z_side[1:] + [self.x_side, self.y_side, self.c_side]
        if cargo:
            peers += [(zd * 2 + 1 - y, model_index) for zd in self.zs[1:]]
        barrier = pltpu.get_barrier_semaphore()
        for peer in peers:
            pl.semaphore_signal(barrier, inc=1, device_id=peer, device_id_type=MESH)
        pl.semaphore_wait(barrier, len(peers))

    def first_row(self, rows, d, group, core=0):
        y, x = self.corners[group]
        c = 1 - self.c if core else self.c
        return ((self.zs[d] * 2 + y) * 4 + x * 2 + c) * rows

    def recv(self, name):
        return self.recv_sem.at[self.slots.setdefault(name, len(self.slots))]

    def send(self, source, target, device, name):
        copy = pltpu.make_async_remote_copy(
            src_ref=source,
            dst_ref=target,
            send_sem=self.send_sem.at[len(self.sent)],
            recv_sem=self.recv(name),
            device_id=device,
            device_id_type=MESH,
        )
        copy.start()
        self.sent.append(copy)

    def arrived(self, ref, name):
        pltpu.make_async_copy(ref, ref, self.recv(name)).wait()
        return ref

    def finish(self):
        for copy in self.sent:
            copy.wait_send()


class Cargo:
    def __init__(self, source, target, send_sem, recv_sem, own_sem):
        self.me, self.model_index = lax.axis_index("dp"), lax.axis_index("mp")
        self.source, self.target = source, target
        self.send_sem, self.recv_sem, self.own_sem, self.sent = send_sem, recv_sem, own_sem, []

    def block(self, ref, index):
        if len(ref.shape) == 3:
            return ref.at[index]
        size = ref.shape[1] // 8
        return ref.at[:, pl.ds(pl.multiple_of(index * size, size), size)]

    def start(self):
        self.own = pltpu.make_async_copy(
            self.block(self.source, self.me), self.block(self.target, self.me), self.own_sem
        )
        self.own.start()
        for shift in (4, 3, 5, 2, 6, 1, 7):
            peer = lax.rem(self.me + shift, 8)
            copy = pltpu.make_async_remote_copy(
                src_ref=self.block(self.source, peer),
                dst_ref=self.block(self.target, self.me),
                send_sem=self.send_sem.at[shift - 1],
                recv_sem=self.recv_sem.at[shift - 1],
                device_id=(peer, self.model_index),
                device_id_type=MESH,
            )
            copy.start()
            self.sent.append(copy)

    def finish(self):
        self.own.wait()
        for shift in range(1, 8):
            here = self.block(self.target, lax.rem(self.me + 8 - shift, 8))
            pltpu.make_async_copy(here, here, self.recv_sem.at[shift - 1]).wait()
        for copy in self.sent:
            copy.wait_send()


def swapped(shape):
    if len(shape) == 3:
        return (shape[1], shape[0] * shape[2])
    return (8, shape[0], shape[1] // 8)


class Gather:
    def __init__(self, link, out, steps, own_sem):
        self.link, self.out, self.steps, self.own_sem = link, out, steps, own_sem
        self.owns = []

    def spot(self, g, d, group, core=0):
        rows = self.steps * GROUP
        start = self.link.first_row(rows, d, group, core) + g * GROUP
        return self.out.at[pl.ds(pl.multiple_of(start, GROUP), GROUP)]

    def send(self, g, source, device, here, there):
        self.link.send(source, self.spot(g, *here), device, ("gather", g, *there))

    def arrived(self, g, d, group, core):
        return self.link.arrived(self.spot(g, d, group, core), ("gather", g, d, group, core))

    def begin(self, g, source):
        link = self.link
        own = pltpu.make_async_copy(source, self.spot(g, 0, 0), self.own_sem.at[g])
        own.start()
        self.owns.append(own)
        for d in (1, 2, 3):
            self.send(g, source, link.z_side[d], (0, 0), (d, 0, 0))
        self.send(g, source, link.x_side, (0, 0), (0, 1, 0))
        self.send(g, source, link.y_side, (0, 0), (0, 2, 0))
        self.send(g, source, link.c_side, (0, 0), (0, 0, 1))

    def from_z(self, g, d):
        here = self.arrived(g, d, 0, 0)
        self.send(g, here, self.link.x_side, (d, 0), (d, 1, 0))
        self.send(g, here, self.link.y_side, (d, 0), (d, 2, 0))
        self.send(g, here, self.link.c_side, (d, 0), (d, 0, 1))

    def from_sides(self, g, d):
        for group, side in ((1, self.link.y_side), (2, self.link.x_side)):
            here = self.arrived(g, d, group, 0)
            if (d % 2 == 0) == (group == 1):
                self.send(g, here, side, (d, group), (d, 3, 0))
            self.send(g, here, self.link.c_side, (d, group), (d, group, 1))

    def first(self, g):
        self.from_z(g, 1)
        self.from_sides(g, 0)
        self.from_z(g, 2)
        self.from_z(g, 3)

    def second(self, g):
        for d in (1, 2, 3):
            self.from_sides(g, d)

    def third(self, g):
        for d in range(4):
            here = self.arrived(g, d, 3, 0)
            self.send(g, here, self.link.c_side, (d, 3), (d, 3, 1))

    def finish(self):
        for g in range(self.steps):
            for d in range(4):
                for group in range(4):
                    self.arrived(g, d, group, 1)
        for own in self.owns:
            own.wait()


CORNER = [(d, 3) for d in range(4)]
SIDES = [(1, 1), (3, 1), (0, 2), (2, 2), (0, 1), (2, 1), (1, 2), (3, 2)]
COLUMN = [(d, 0) for d in (3, 2, 1)]


class Scatter:
    def __init__(self, link, partial, rows, order, buffers, own_sem):
        self.link, self.partial, self.rows = link, partial, rows
        self.mine, self.core, self.corner, self.side, self.column = buffers
        self.owns = {}
        for p in order:
            for d, group in CORNER + SIDES + COLUMN + [(0, 0)]:
                k = d * 4 + group
                here = self.mine.at[k, pl.ds(p * GROUP, GROUP)]
                own = pltpu.make_async_copy(self.spot(p, d, group), here, own_sem.at[p * 16 + k])
                own.start()
                self.owns[p, k] = own
                self.send(p, self.spot(p, d, group, 1), self.core, k, link.c_side, "core")

    def spot(self, p, d, group, core=0):
        start = self.link.first_row(self.rows, d, group, core) + p * GROUP
        return self.partial.at[pl.ds(pl.multiple_of(start, GROUP), GROUP)]

    def send(self, p, source, buffer, k, device, name):
        self.link.send(source, buffer.at[k, pl.ds(p * GROUP, GROUP)], device, (name, p, k))

    def term(self, p, buffer, k, name):
        return self.link.arrived(buffer.at[k, pl.ds(p * GROUP, GROUP)], (name, p, k))[...].astype(
            jnp.float32
        )

    def start_terms(self, p, k):
        self.owns[p, k].wait()
        own = self.mine[k, pl.ds(p * GROUP, GROUP)].astype(jnp.float32)
        return own + self.term(p, self.core, k, "core")

    def pass_on(self, p, k, total, buffer, there, device, name):
        here = self.mine.at[k, pl.ds(p * GROUP, GROUP)]
        here[...] = total.astype(here.dtype)
        self.send(p, here, buffer, there, device, name)

    def to_corner(self, p):
        for d, _ in CORNER:
            side = self.link.y_side if d % 2 == 0 else self.link.x_side
            k = d * 4 + 3
            self.pass_on(p, k, self.start_terms(p, k), self.corner, d, side, "corner")

    def to_sides(self, p):
        for d, group in SIDES:
            k = d * 4 + group
            total = self.start_terms(p, k)
            if (d % 2 == 0) == (group == 1):
                total = total + self.term(p, self.corner, d, "corner")
            side = self.link.x_side if group == 1 else self.link.y_side
            self.pass_on(p, k, total, self.side, d * 2 + group - 1, side, "side")

    def column_terms(self, p, d):
        total = self.start_terms(p, d * 4)
        for k in (d * 2, d * 2 + 1):
            total = total + self.term(p, self.side, k, "side")
        return total

    def to_column(self, p):
        for d, _ in COLUMN:
            total = self.column_terms(p, d)
            self.pass_on(p, d * 4, total, self.column, d - 1, self.link.z_side[d], "column")

    def total(self, p):
        total = self.column_terms(p, 0)
        for d in (1, 2, 3):
            total = total + self.term(p, self.column, d - 1, "column")
        return total


def relay_kernel(plan, row_step, *refs):
    refs = list(refs)

    def take(count):
        taken = refs[:count]
        del refs[:count]
        return taken

    (partial,) = take(1)
    ready = take(plan["ready"])
    extras = take(plan["extras"])
    cargo_in = take(plan["cargo"])
    (gathered,) = take(1)
    kept = take(plan["kept"])
    sums = take(plan["sums"])
    cargo_out = take(plan["cargo"])
    buffers = take(5)
    held, send_sem, recv_sem, load_sem, own_sem = take(5)
    order, steps = plan["order"], plan["steps"]
    link = Links(send_sem, recv_sem, plan["cargo"])
    cargo = Cargo(*cargo_in, *cargo_out, *refs) if cargo_in else None
    gather = Gather(link, gathered, steps, own_sem)
    if ready:
        gather.begin(0, ready[0])
    scatter = Scatter(link, partial, plan["rows"], order, buffers, load_sem)
    if cargo:
        cargo.start()
    ticks = len(order) + 7
    agenda = [[] for _ in range(ticks)]
    if ready:
        for tick, step in enumerate((gather.first, gather.second, gather.third)):
            agenda[tick + 2].append((step, 0))

    def last(p):
        rows, keeps, adds = row_step(p, scatter.total(p), extras)
        for ref, value in zip(kept, keeps):
            ref[pl.ds(p * GROUP, GROUP)] = value
        for ref, value in zip(sums, adds):
            ref[...] = value if p == order[0] else ref[...] + value
        if rows is not None:
            g = plan["slot"](p)
            held[g] = rows
            gather.begin(g, held.at[g])

    for q, p in enumerate(order):
        for tick, step in enumerate(
            (scatter.to_corner, scatter.to_sides, scatter.to_column, last)
        ):
            agenda[q + tick].append((step, p))
        if plan["slot"](p) is not None:
            for tick, step in enumerate((gather.first, gather.second, gather.third)):
                agenda[q + 4 + tick].append((step, plan["slot"](p)))
    for tick in agenda:
        for step, index in tick:
            step(index)
    gather.finish()
    link.finish()
    if cargo:
        cargo.finish()


def relay(
    partial, row_step, ident, extras=(), kept=0, sums=0, order=None, slot=None, ready=None, cargo=None
):
    rows, width = partial.shape[0] // (lax.axis_size("dp") * lax.axis_size("mp")), partial.shape[1]
    groups = rows // GROUP
    order = list(range(groups)) if order is None else order
    slot = slot or (lambda p: p)
    steps = sum(slot(p) is not None for p in order) + (ready is not None)
    if not kernel_mesh():
        total = lax.psum_scatter(partial, BOTH, scatter_dimension=0, tiled=True)
        total = total.astype(jnp.float32)
        outs, keeps, adds = [None] * steps, [None] * groups, [0.0] * sums
        if ready is not None:
            outs[0] = ready
        for p in order:
            out, keeps[p], add = row_step(p, total[p * GROUP : (p + 1) * GROUP], extras)
            adds = [one + two for one, two in zip(adds, add)]
            if out is not None:
                outs[slot(p)] = out
        gathered = lax.all_gather(jnp.concatenate(outs), BOTH, axis=0, tiled=True)
        keeps = [jnp.concatenate(parts) for parts in zip(*keeps)]
        moved = [] if cargo is None else [exchange_plain(cargo)]
        return [gathered, *keeps, *adds, *moved]
    plan = dict(
        rows=rows,
        order=order,
        slot=slot,
        steps=steps,
        ready=int(ready is not None),
        extras=len(extras),
        cargo=int(cargo is not None),
        kept=kept,
        sums=sums,
    )
    low = partial.dtype
    vmem = pl.BlockSpec(memory_space=pltpu.VMEM)
    load = [] if cargo is None else [cargo]
    copies = 31 * (groups + steps)
    shapes = [jax.ShapeDtypeStruct((32 * steps * GROUP, width), low)]
    shapes += [jax.ShapeDtypeStruct((rows, width), jnp.float32)] * kept
    shapes += [jax.ShapeDtypeStruct((1, width), jnp.float32)] * sums
    shapes += [jax.ShapeDtypeStruct(swapped(value.shape), value.dtype) for value in load]
    buffers = [pltpu.VMEM((count, rows, width), low) for count in (16, 16, 4, 8, 3)]
    semaphores = [pltpu.SemaphoreType.DMA((count,)) for count in (copies, copies, 16 * groups, steps)]
    semaphores += [pltpu.SemaphoreType.DMA((7,))] * 2 * len(load)
    semaphores += [pltpu.SemaphoreType.DMA] * len(load)
    return pl.pallas_call(
        functools.partial(relay_kernel, plan, row_step),
        out_shape=shapes,
        in_specs=[ANY] * (1 + plan["ready"]) + [vmem] * len(extras) + [ANY] * len(load),
        out_specs=[ANY] + [vmem] * (kept + sums) + [ANY] * len(load),
        scratch_shapes=buffers + [pltpu.VMEM((steps, GROUP, width), low)] + semaphores,
        compiler_params=comm_params(ident),
    )(partial, *([] if ready is None else [ready]), *extras, *load)


def exchange_plain(value):
    count = lax.axis_size("dp")
    if len(value.shape) == 3:
        moved = lax.all_to_all(value, "dp", split_axis=0, concat_axis=0, tiled=True)
        return jnp.moveaxis(moved, 0, 1).reshape(value.shape[1], -1)
    parts = jnp.moveaxis(value.reshape(value.shape[0], count, -1), 1, 0)
    return lax.all_to_all(parts, "dp", split_axis=0, concat_axis=0, tiled=True)


def small_gather_kernel(x_ref, o_ref, send_sem, recv_sem, own_sem):
    data_index, model_index = lax.axis_index("dp"), lax.axis_index("mp")
    me = data_index * 4 + model_index
    own = pltpu.make_async_copy(x_ref, o_ref.at[me], own_sem)
    own.start()
    peers = [lax.rem(me + shift, 32) for shift in range(1, 32)]
    barrier = pltpu.get_barrier_semaphore()
    for peer in peers:
        pl.semaphore_signal(
            barrier, inc=1, device_id=(peer // 4, peer % 4), device_id_type=MESH
        )
    pl.semaphore_wait(barrier, 31)
    sent = []
    for index, peer in enumerate(peers):
        copy = pltpu.make_async_remote_copy(
            src_ref=x_ref,
            dst_ref=o_ref.at[me],
            send_sem=send_sem.at[index],
            recv_sem=recv_sem.at[index],
            device_id=(peer // 4, peer % 4),
            device_id_type=MESH,
        )
        copy.start()
        sent.append(copy)
    for index in range(31):
        here = o_ref.at[lax.rem(me + 31 - index, 32)]
        pltpu.make_async_copy(here, here, recv_sem.at[index]).wait()
    own.wait()
    for copy in sent:
        copy.wait_send()


def gather_small(value, ident):
    if not kernel_mesh():
        return lax.all_gather(value, BOTH)
    vmem = pl.BlockSpec(memory_space=pltpu.VMEM)
    return pl.pallas_call(
        small_gather_kernel,
        out_shape=jax.ShapeDtypeStruct((32,) + value.shape, value.dtype),
        in_specs=[vmem],
        out_specs=vmem,
        scratch_shapes=[
            pltpu.SemaphoreType.DMA((31,)),
            pltpu.SemaphoreType.DMA((31,)),
            pltpu.SemaphoreType.DMA,
        ],
        compiler_params=comm_params(ident),
    )(value)


def greet(peers):
    barrier = pltpu.get_barrier_semaphore()
    for peer in peers:
        pl.semaphore_signal(barrier, inc=1, device_id=peer, device_id_type=MESH)
    pl.semaphore_wait(barrier, len(peers))


def exchange_kernel(count, whole, *refs):
    ins, outs = refs[: len(whole)], refs[len(whole) : 2 * len(whole)]
    send_sem, recv_sem, own_sem = refs[2 * len(whole) :]
    me, model_index = lax.axis_index("dp"), lax.axis_index("mp")
    peers = [lax.rem(me + shift, count) for shift in range(1, count)]
    greet([(peer, model_index) for peer in peers])
    owns, sent = [], []
    for array, keep in enumerate(whole):
        own = pltpu.make_async_copy(
            ins[array] if keep else ins[array].at[me], outs[array].at[me], own_sem.at[array]
        )
        own.start()
        owns.append(own)
        for shift in range(count - 1):
            copy = pltpu.make_async_remote_copy(
                src_ref=ins[array] if keep else ins[array].at[peers[shift]],
                dst_ref=outs[array].at[me],
                send_sem=send_sem.at[array, shift],
                recv_sem=recv_sem.at[array, shift],
                device_id=(peers[shift], model_index),
                device_id_type=MESH,
            )
            copy.start()
            sent.append(copy)
    for own in owns:
        own.wait()
    for array in range(len(whole)):
        for shift in range(count - 1):
            source = lax.rem(me + count - 1 - shift, count)
            here = outs[array].at[source]
            pltpu.make_async_copy(here, here, recv_sem.at[array, shift]).wait()
    for copy in sent:
        copy.wait_send()


def exchange(values, whole, ident):
    count = lax.axis_size("dp")
    if not kernel_mesh():
        return [
            lax.all_gather(value, "dp")
            if keep
            else lax.all_to_all(value, "dp", split_axis=0, concat_axis=0, tiled=True)
            for value, keep in zip(values, whole)
        ]
    shapes = [
        jax.ShapeDtypeStruct(((count,) if keep else ()) + value.shape, value.dtype)
        for value, keep in zip(values, whole)
    ]
    return pl.pallas_call(
        functools.partial(exchange_kernel, count, tuple(whole)),
        out_shape=shapes,
        in_specs=[ANY] * len(values),
        out_specs=[ANY] * len(values),
        scratch_shapes=[
            pltpu.SemaphoreType.DMA((len(values), count - 1)),
            pltpu.SemaphoreType.DMA((len(values), count - 1)),
            pltpu.SemaphoreType.DMA((len(values),)),
        ],
        compiler_params=comm_params(ident),
    )(*values)


def norm_fwd(values, gain):
    row_scale = lax.rsqrt(jnp.mean(values * values, axis=-1, keepdims=True) + EPS_NORM)
    unit_rows = values * row_scale
    return (unit_rows * gain, unit_rows, row_scale)


def norm_back(unit_rows, row_scale, gain, gradient):
    weighted = gradient * gain
    back_rows = row_scale * (
        weighted - unit_rows * jnp.mean(weighted * unit_rows, axis=-1, keepdims=True)
    )
    return (back_rows, jnp.sum(gradient * unit_rows, axis=0))


def rotary(places, width):
    half_width = width // 2
    frequency = jnp.exp(
        jnp.arange(half_width, dtype=jnp.float32) * (-math.log(10000.0) / half_width)
    )
    angles = places.astype(jnp.float32)[:, None] * frequency[None, :]
    return (jnp.cos(angles), jnp.sin(angles))


def rotate_pairs(values, cosine, sine_table):
    half_width = values.shape[-1] // 2
    front_half = values[..., :half_width]
    back_half = values[..., half_width:]
    return jnp.concatenate(
        [
            front_half * cosine - back_half * sine_table,
            back_half * cosine + front_half * sine_table,
        ],
        axis=-1,
    )


def dot(left, right, left_dim=1, right_dim=0):
    return lax.dot_general(
        left, right, (((left_dim,), (right_dim,)), ((), ())), preferred_element_type=jnp.float32
    )


def placed(value, order):
    return with_layout_constraint(value, Layout(major_to_minor=order))


def adam_update(weight, moment_one, moment_two, gradient, rate, decay):
    moment_one = BETA_ONE * moment_one + (1.0 - BETA_ONE) * gradient
    moment_two = BETA_TWO * moment_two + (1.0 - BETA_TWO) * gradient * gradient
    ratio = (
        moment_one
        / (1.0 - BETA_ONE**STEP)
        / (jnp.sqrt(moment_two / (1.0 - BETA_TWO**STEP)) + ADAM_EPS)
    )
    return (weight - rate * (ratio + decay * weight), moment_one, moment_two)


def body(
    token_ids,
    target_ids,
    exit_mask,
    table,
    table_first,
    table_second,
    qkv_weight,
    qkv_first,
    qkv_second,
    out_weight,
    out_first,
    out_second,
    gate_up_weight,
    gate_up_first,
    gate_up_second,
    down_weight,
    down_first,
    down_second,
    gains,
    gains_first,
    gains_second,
):
    low = jnp.bfloat16
    data_size, model_size = lax.axis_size("dp"), lax.axis_size("mp")
    data_index, model_index = lax.axis_index("dp"), lax.axis_index("mp")
    devices = data_size * model_size
    block_rows = token_ids.shape[0]
    tokens = block_rows * data_size
    width = table.shape[1]
    width_here = qkv_weight.shape[0]
    heads_here = qkv_weight.shape[2] // HEAD_DIM
    hidden_here = down_weight.shape[0] // data_size
    vocab_here = table.shape[0]
    device_index = data_index * model_size + model_index
    vocab_ids = device_index * vocab_here + jnp.arange(vocab_here, dtype=jnp.int32)
    score_scale = 1.0 / math.sqrt(HEAD_DIM)

    sharers = data_size // heads_here
    shares = sharers // 2
    share_slots = data_size // shares * R_DEV
    exit_here = data_index % sharers % 2
    share_here = data_index % sharers // 2
    slots_here = R_DEV // model_size
    rows_here = block_rows // model_size

    ints, gain_low = exchange(
        [
            jnp.concatenate([token_ids[None], target_ids[None], exit_mask]),
            jnp.pad(gains.astype(low), ((0, 13), (0, 0))),
        ],
        (True, True),
        0,
    )
    gain_rows = jnp.moveaxis(gain_low[:, :3], 0, 1).reshape(3, width).astype(jnp.float32)
    all_ids = ints[:, 0].reshape(tokens)
    mask_blocks = jnp.moveaxis(ints[:, 2:], 0, 1)
    slot_ids = jnp.arange(R_DEV, dtype=jnp.int32)
    slot_ranks = jnp.cumsum(mask_blocks, axis=2) - 1
    pick_int = (
        (slot_ranks[:, :, None, :] == slot_ids[:, None]) & (mask_blocks[:, :, None, :] == 1)
    ).astype(jnp.int32)
    pick_low = pick_int.astype(low)
    token_places = jnp.arange(tokens, dtype=jnp.int32)
    slot_targets = jnp.sum(pick_int * ints[:, 1][None, :, None, :], axis=3).reshape(2, -1)
    slot_places = jnp.sum(
        pick_int * token_places.reshape(1, data_size, 1, block_rows), axis=3
    ).reshape(2, -1)
    live = (slot_ids < jnp.sum(mask_blocks, axis=2)[:, :, None]).astype(jnp.float32).reshape(2, -1)
    counts = jnp.sum(live, axis=1)

    head_rows = jnp.moveaxis(
        qkv_weight.astype(low).reshape(width_here, 3, heads_here, HEAD_DIM), 0, 3
    )
    head_rows = jnp.concatenate(
        [
            jnp.moveaxis(head_rows, 0, 1).reshape(heads_here, 3 * HEAD_DIM, width_here),
            out_weight.astype(low).reshape(heads_here, HEAD_DIM, width_here),
        ],
        axis=1,
    )
    hidden_rows = jnp.moveaxis(
        gate_up_weight.astype(low).reshape(width_here, 2, data_size, hidden_here), 0, 3
    )
    hidden_rows = jnp.concatenate(
        [
            jnp.moveaxis(hidden_rows, 0, 1).reshape(data_size, 2 * hidden_here, width_here),
            down_weight.astype(low).reshape(data_size, hidden_here, width_here),
        ],
        axis=1,
    )

    table_low = table.astype(low)
    id_hits = (all_ids[:, None] == vocab_ids[None, :]).astype(low)
    resid_low, head_rows = relay(
        dot(id_hits, table_low).astype(low),
        lambda p, total, extras: (total.astype(low), (), ()),
        1,
        cargo=jnp.repeat(head_rows, sharers, axis=0),
    )
    qkv_head, out_head = head_rows[: 3 * HEAD_DIM], head_rows[3 * HEAD_DIM :]
    attn_low = norm_fwd(resid_low.astype(jnp.float32), gain_rows[0])[0].astype(low)

    projected = dot(attn_low, qkv_head, 1, 1)
    cosine, sine_table = rotary(token_places, HEAD_DIM)
    query_low = rotate_pairs(projected[:, :HEAD_DIM], cosine, sine_table).astype(low)
    key_low = rotate_pairs(projected[:, HEAD_DIM : 2 * HEAD_DIM], cosine, sine_table).astype(low)
    value_low = projected[:, 2 * HEAD_DIM :].astype(low)
    pick_share = lax.dynamic_slice_in_dim(
        lax.dynamic_index_in_dim(pick_low, exit_here, 0, keepdims=False),
        share_here * (data_size // shares),
        data_size // shares,
        0,
    )
    query_share = lax.dynamic_slice_in_dim(
        query_low.reshape(data_size, block_rows, HEAD_DIM),
        share_here * (data_size // shares),
        data_size // shares,
        0,
    )
    query_slots = (
        jnp.einsum("brt,btd->brd", pick_share, query_share, preferred_element_type=jnp.float32)
        .astype(low)
        .reshape(share_slots, HEAD_DIM)
    )

    def share_of(per_slot):
        return lax.dynamic_slice(per_slot, (exit_here, share_here * share_slots), (1, share_slots))[
            0
        ]

    places_share, live_share = share_of(slot_places), share_of(live)
    scores = dot(query_slots, key_low, 1, 1) * score_scale
    allowed = token_places[None, :] <= places_share[:, None]
    scores = jnp.where(allowed, scores, NEG)
    weights = jnp.exp(scores - jnp.max(scores, axis=-1, keepdims=True))
    probs = weights / jnp.sum(weights, axis=-1, keepdims=True)
    probs_low = probs.astype(low)
    attn_out = (dot(probs_low, value_low) * live_share[:, None]).astype(low)

    def spread(per_share):
        if shares > 1:
            full = jnp.zeros((data_size * R_DEV, width), per_share.dtype)
            per_share = lax.dynamic_update_slice_in_dim(
                full, per_share, share_here * share_slots, 0
            )
        exits = jnp.arange(2, dtype=jnp.int32)[None, :, None, None]
        rows = per_share.reshape(devices, 1, slots_here, width)
        return jnp.where(exits == exit_here, rows, 0).reshape(-1, width)

    block_low = lax.dynamic_slice_in_dim(resid_low, data_index * block_rows, block_rows, 0)
    pick_here = lax.dynamic_slice(
        pick_low,
        (0, data_index, model_index * slots_here, 0),
        (2, 1, slots_here, block_rows),
    ).reshape(2 * slots_here, block_rows)

    def first_step(p, total, extras):
        resid = extras[0][p * GROUP : (p + 1) * GROUP] + total
        gain = 2 if p == 0 else 1
        return (norm_fwd(resid, extras[1][gain : gain + 1])[0].astype(low), (resid,), ())

    first_rows, resid_one, hidden_rows = relay(
        spread(dot(attn_out, out_head).astype(low)),
        first_step,
        2,
        extras=[dot(pick_here, block_low), gain_rows],
        kept=1,
        cargo=hidden_rows,
    )
    first_rows = first_rows.reshape(devices, 2, slots_here, width)
    exit_rows_one = first_rows[:, 0].reshape(-1, width)
    mlp_low = first_rows[:, 1].reshape(-1, width)

    gate_up_head, down_head = hidden_rows[: 2 * hidden_here], hidden_rows[2 * hidden_here :]
    gate_up = dot(mlp_low, gate_up_head, 1, 1)
    gate_part, up_part = gate_up[:, :hidden_here], gate_up[:, hidden_here:]
    gate_sigma = jax.nn.sigmoid(gate_part)
    hidden_low = (gate_part * gate_sigma * up_part).astype(low)

    def second_step(p, total, extras):
        resid = extras[0][GROUP : 2 * GROUP] + total
        return (norm_fwd(resid, extras[1][2:3])[0].astype(low), (resid,), ())

    exit_rows_two, resid_two = relay(
        dot(hidden_low, down_head).astype(low), second_step, 3, extras=[resid_one, gain_rows], kept=1
    )

    exit_rows = (exit_rows_one, exit_rows_two)
    logits = [dot(rows, table_low, 1, 1) for rows in exit_rows]
    hits = [slot_targets[e][:, None] == vocab_ids[None, :] for e in range(2)]
    tops = [jnp.max(values, axis=1) for values in logits]
    masses = [jnp.sum(jnp.exp(values - top[:, None]), axis=1) for values, top in zip(logits, tops)]
    found = [jnp.sum(jnp.where(hit, values, 0.0), axis=1) for hit, values in zip(hits, logits)]
    stats = jnp.concatenate(tops + masses + found).reshape(-1, 128)
    stats = gather_small(stats, 4).reshape(devices, 3, 2, -1)
    row_top = jnp.max(stats[:, 0], axis=0)
    row_mass = jnp.sum(stats[:, 1] * jnp.exp(stats[:, 0] - row_top), axis=0)
    row_lse = row_top + jnp.log(row_mass)
    entropy = row_lse - jnp.sum(stats[:, 2], axis=0)
    loss_sums = jnp.sum(entropy * live, axis=1)
    row_weight = live * (jnp.array(EXIT_SCALE, jnp.float32) / counts)[:, None]
    grad_logits = [
        (
            row_weight[e][:, None]
            * (jnp.exp(logits[e] - row_lse[e][:, None]) - hits[e].astype(jnp.float32))
        ).astype(low)
        for e in range(2)
    ]
    table_head = dot(grad_logits[0], exit_rows_one, 0, 0) + dot(grad_logits[1], exit_rows_two, 0, 0)
    row_terms = jnp.stack(
        [
            dot(grad, table_low).astype(low).reshape(devices, slots_here, width)
            for grad in grad_logits
        ],
        axis=1,
    )

    def head_step(p, total, extras):
        values = extras[0][:GROUP] if p == 0 else extras[1][...]
        gain = extras[2][2:3]
        _, unit, scale = norm_fwd(values, gain)
        back, gain_grad = norm_back(unit, scale, gain, total)
        return (None if p == 0 else back.astype(low), (back,), (gain_grad[None],))

    dtwo_low, dexits, final_grad = relay(
        row_terms.reshape(-1, width),
        head_step,
        5,
        extras=[resid_one, resid_two, gain_rows],
        kept=1,
        sums=1,
        order=[1, 0],
        slot=lambda p: None if p == 0 else 0,
    )
    down_local = dot(hidden_low, dtwo_low, 0, 0)
    dhidden = dot(dtwo_low, down_head, 1, 1)
    dgate = dhidden * up_part * gate_sigma * (1.0 + gate_part * (1.0 - gate_sigma))
    dup_part = dhidden * gate_part * gate_sigma
    dgate_up = jnp.concatenate([dgate, dup_part], axis=1).astype(low)
    gate_up_local = dot(dgate_up, mlp_low, 0, 0)

    def mlp_step(p, total, extras):
        gain = extras[2][1:2]
        _, unit, scale = norm_fwd(extras[0][GROUP : 2 * GROUP], gain)
        back, gain_grad = norm_back(unit, scale, gain, total)
        return ((extras[1][GROUP : 2 * GROUP] + back).astype(low), (), (gain_grad[None],))

    done_low, mlp_grad, hidden_parts = relay(
        dot(dgate_up, gate_up_head).astype(low),
        mlp_step,
        6,
        extras=[resid_one, dexits, gain_rows],
        sums=1,
        slot=lambda p: 1,
        ready=dexits[:GROUP].astype(low),
        cargo=jnp.concatenate([gate_up_local.astype(low), down_local.astype(low)]),
    )
    done_low = done_low.reshape(devices, 2, slots_here, width)

    done_share = lax.dynamic_slice(
        lax.dynamic_index_in_dim(done_low, exit_here, 1, keepdims=False).reshape(-1, width),
        (share_here * share_slots, 0),
        (share_slots, width),
    )
    out_local = dot(attn_out, done_share, 0, 0)
    dattn_low = dot(done_share, out_head, 1, 1).astype(low)
    dprobs = dot(dattn_low, value_low, 1, 1)
    delta = jnp.sum(probs * dprobs, axis=-1, keepdims=True)
    dscores = (probs * (dprobs - delta)).astype(low)
    cosine_share, sine_share = rotary(places_share, HEAD_DIM)
    dquery = rotate_pairs(dot(dscores, key_low) * score_scale, cosine_share, -sine_share).astype(
        low
    )
    dquery_share = jnp.einsum(
        "brt,brd->btd",
        pick_share,
        dquery.reshape(-1, R_DEV, HEAD_DIM),
        preferred_element_type=jnp.float32,
    ).astype(low)
    if shares > 1:
        dquery_share = lax.dynamic_update_slice_in_dim(
            jnp.zeros((data_size, block_rows, HEAD_DIM), low),
            dquery_share,
            share_here * (data_size // shares),
            0,
        )
    dkey = rotate_pairs(dot(dscores, query_slots, 0, 0) * score_scale, cosine, -sine_table)
    dvalue = dot(probs_low, dattn_low, 0, 0)
    dprojected = jnp.concatenate(
        [dquery_share.reshape(tokens, HEAD_DIM), dkey.astype(low), dvalue.astype(low)], axis=1
    )
    qkv_local = dot(dprojected, attn_low, 0, 0)

    resid_here = lax.dynamic_slice_in_dim(resid_low, device_index * rows_here, rows_here, 0)
    done_block = lax.dynamic_slice_in_dim(done_low, data_index * model_size, model_size, 0)
    pick_block = lax.dynamic_slice(
        pick_low,
        (0, data_index, 0, model_index * rows_here),
        (2, 1, R_DEV, rows_here),
    ).reshape(2, model_size, slots_here, rows_here)
    dresid_here = jnp.einsum(
        "emst,mesd->td", pick_block, done_block, preferred_element_type=jnp.float32
    )

    def zero_step(p, total, extras):
        at = slice(p * GROUP, (p + 1) * GROUP)
        gain = extras[2][:1]
        _, unit, scale = norm_fwd(extras[0][at], gain)
        back, gain_grad = norm_back(unit, scale, gain, total)
        return ((extras[1][at] + back).astype(low), (), (gain_grad[None],))

    dzero_low, attn_grad, head_parts = relay(
        dot(dprojected, qkv_head).astype(low),
        zero_step,
        7,
        extras=[resid_here.astype(jnp.float32), dresid_here, gain_rows],
        sums=1,
        cargo=jnp.concatenate([qkv_local.astype(low), out_local.astype(low)]),
    )
    table_grad = table_head + dot(id_hits, dzero_low, 0, 0)

    gain_sums = jnp.sum(
        gather_small(
            jnp.concatenate([attn_grad, mlp_grad, final_grad]).reshape(-1, 128), 8
        ).reshape(devices, 3, width),
        axis=0,
    )
    head_grad = jnp.sum(
        head_parts.reshape(heads_here, sharers, 4, HEAD_DIM, width_here).astype(jnp.float32), axis=1
    )
    qkv_grad = placed(jnp.transpose(head_grad[:, :3], (3, 1, 0, 2)).reshape(qkv_weight.shape), (1, 0, 2))
    out_grad = head_grad[:, 3].reshape(out_weight.shape)
    hidden_parts = hidden_parts.astype(jnp.float32)
    gate_up_grad = hidden_parts[:, : 2 * hidden_here].reshape(
        data_size, 2, hidden_here, width_here
    )
    gate_up_grad = placed(
        jnp.transpose(gate_up_grad, (3, 1, 0, 2)).reshape(gate_up_weight.shape), (0, 1, 2)
    )
    down_grad = hidden_parts[:, 2 * hidden_here :].reshape(down_weight.shape)
    gain_grad = lax.dynamic_slice_in_dim(gain_sums, data_index * width_here, width_here, 1)

    squares = (
        jnp.sum(table_grad * table_grad)
        + jnp.sum(qkv_grad * qkv_grad)
        + jnp.sum(out_grad * out_grad)
        + jnp.sum(gate_up_grad * gate_up_grad)
        + jnp.sum(down_grad * down_grad)
    )
    square_parts = gather_small(jnp.full((8, 128), squares), 9)[:, 0, 0]
    grad_norm = jnp.sqrt(jnp.sum(square_parts) + jnp.sum(gain_sums * gain_sums))
    factor = jnp.minimum(1.0, CLIP / (grad_norm + 1e-06))
    table_new = adam_update(
        table, table_first, table_second, table_grad * factor, RATE_MATRIX, DECAY
    )
    qkv_new = adam_update(qkv_weight, qkv_first, qkv_second, qkv_grad * factor, RATE_MATRIX, DECAY)
    out_new = adam_update(out_weight, out_first, out_second, out_grad * factor, RATE_MATRIX, DECAY)
    gate_up_new = adam_update(
        gate_up_weight, gate_up_first, gate_up_second, gate_up_grad * factor, RATE_MATRIX, DECAY
    )
    down_new = adam_update(
        down_weight, down_first, down_second, down_grad * factor, RATE_MATRIX, DECAY
    )
    gains_new = adam_update(gains, gains_first, gains_second, gain_grad * factor, RATE_GAIN, 0.0)
    return (
        loss_sums,
        counts,
        grad_norm,
        *table_new,
        *qkv_new,
        *out_new,
        *gate_up_new,
        *down_new,
        *gains_new,
    )


def solution(mesh):
    rows, sides, cols, gain = P(BOTH, None), P("dp", None, "mp"), P("mp", "dp"), P(None, "dp")
    state = (rows,) * 3 + (sides,) * 3 + (cols,) * 3 + (sides,) * 3 + (cols,) * 3 + (gain,) * 3
    return jax.shard_map(
        body,
        mesh=mesh,
        in_specs=(P("dp"), P("dp"), P(None, "dp")) + state,
        out_specs=(P(), P(), P()) + state,
        check_vma=False,
    )
```

time: 1030 us -> 810 us (0.79)
  Pallas kernels: 712 us -> 537 us
  local copies, waits for them, and re-layouts: 87.5 us -> 44.6 us
    pallas_call x3 -> x1, Pallas kernels: 198 us -> 9.58 us  [exchange(): pl.pallas_call(functools.partial(exchange_kernel, count, tuple(whole)), o...]
    unnamed x224 -> x161, local copies, waits for them, and re-layouts: 52.3 us -> 14.6 us
    pallas_call x15 -> x9, Pallas kernels: 514 us -> 527 us  [the longest x6 486 us: relay(): pl.pallas_call(functools.partial(relay_kernel, plan, row_step), out_shape...]
where the time goes in v2:
time: 810 us; the launch traced here: 801 us
  Pallas kernels  537 us (66%)
  other arithmetic  109 us (13%)
  matrix products  103 us (13%)
  local copies, waits for them, and re-layouts  44.6 us (6%)
    pallas_call x6, Pallas kernels, relay(): pl.pallas_call(functools.partial(relay_kernel, plan, row_step), out_shape...  486 us
    dot_general x27, matrix products, dot(): lax.dot_general(left, right, (((left_dim,), (right_dim,)), ((), ())), pre...  98.7 us
    sub x6, other arithmetic, adam_update(): return (weight - rate * (ratio + decay * weight), moment_one, moment_two)  44.3 us
    pallas_call x3, Pallas kernels, gather_small(): pl.pallas_call(small_gather_kernel, out_shape=jax.ShapeDtypeStruct((32,)...  41.5 us

profile of v2, /device:TPU:0, one launch (start us, length us, event | category | flops | bytes accessed | tf_op | source)
XLA Modules:
  0.0 801.3 jit_solution(6928051872908989901)
XLA Ops:
  3.3 9.6 %shard_map.373 = (s32[8,4,256]{2,1,0:T(4,128)}, bf16[8,16,256]{2,1,0:T(8,128)(2,1)}) custom-call(s32[4,256]{1,0:T(4,128)} %pad_add_fusion.refs_0_, bf16[16,256]{1,0:T(8,128)(2,1)} %pad.4.refs_1_), custom_call_target="tpu_custom_call" | custom-call | tf_op jit(solution)/shard_map/pallas_call | solution.py:507
  15.8 5.9 convert_element_type.179
  21.8 13.6 %fusion.8.refs_0_ = bf16[2048,2048]{1,0:T(8,128)(2,1)} fusion(bf16[1000,2048]{1,0:T(8,128)(2,1)} %convert_element_type.179, s32[1000]{0:T(1024)S(1)} %iota_add_fusion, s32[2048]{0:T(1024)S(1)} %bitcast.200), kind=kOutput, calls=%fused_computation.15 | convolution fusion | flops 8394850304 | bytes 12496800 | tf_op jit(solution)/shard_map/dot_general | solution.py:558
  37.3 113.8 %shard_map.374 = (bf16[2048,2048]{1,0:T(8,128)(2,1)}, bf16[512,2048]{1,0:T(8,128)(2,1)}) custom-call(bf16[2048,2048]{1,0:T(8,128)(2,1)} %fusion.8.refs_0_, bf16[8,512,256]{2,1,0:T(8,128)(2,1)} %bitcast.146), custom_call_target="tpu_custom_call" | custom-call | tf_op jit(solution)/shard_map/pallas_call | solution.py:383
  152.6 5.2 fusion
  158.3 5.1 fusion.19
  163.5 3.5 fusion.68
  192.1 3.6 copy.118
  198.8 88.3 %shard_map.375 = (bf16[1024,2048]{1,0:T(8,128)(2,1)}, f32[32,2048]{1,0:T(8,128)}, bf16[528,2048]{1,0:T(8,128)(2,1)}) custom-call(bf16[1024,2048]{1,0:T(8,128)(2,1)} %bitcast_select_fusion.refs_0_, f32[32,2048]{1,0:T(8,128)} %fusion.38.refs_1_, f32[3,2048]{1,0:T(4,128)} %bitcast.168, bf16[8,528,256]{2,1,0:T(8,128)(2,1)} %pad_maximum_fusion.1.refs_3_), custom_call_target="tpu_custom_call" | custom-call | tf_op jit(solution)/shard_map/pallas_call | solution.py:383
  287.1 2.9 fusion.126
  290.5 4.3 fusion.132
  299.5 38.6 %shard_map.376 = (bf16[512,2048]{1,0:T(8,128)(2,1)}, f32[16,2048]{1,0:T(8,128)}) custom-call(bf16[512,2048]{1,0:T(8,128)(2,1)} %convolution_convert_fusion.3.refs_0_, f32[32,2048]{1,0:T(8,128)} %get-tuple-element.45.refs_1_.refs_2_, f32[3,2048]{1,0:T(4,128)} %bitcast.169), custom_call_target="tpu_custom_call" | custom-call | tf_op jit(solution)/shard_map/pallas_call | solution.py:383
  338.1 5.8 fusion.133
  344.1 3.2 fusion.25
  349.1 12.4 %shard_map.377 = f32[32,24,128]{2,1,0:T(8,128)} custom-call(f32[24,128]{1,0:T(8,128)} %concatenate.79.x_ref), custom_call_target="tpu_custom_call" | custom-call | tf_op jit(solution)/shard_map/pallas_call | solution.py:438
  363.7 5.0 convolution_convert_fusion.1
  368.7 2.8 convolution_convert_fusion.2
  373.9 47.1 %shard_map.378 = (bf16[512,2048]{1,0:T(8,128)(2,1)}, f32[32,2048]{1,0:T(8,128)}, f32[1,2048]{1,0:T(1,128)}) custom-call(bf16[1024,2048]{1,0:T(8,128)(2,1)} %bitcast.143, f32[32,2048]{1,0:T(8,128)} %get-tuple-element.45.refs_1_.refs_2_, f32[16,2048]{1,0:T(8,128)} %get-tuple-element.47.refs_2_, f32[3,2048]{1,0:T(4,128)} %bitcast.170), custom_call_target="tpu_custom_call" | custom-call | tf_op jit(solution)/shard_map/pallas_call | solution.py:383
  431.7 81.6 %shard_map.379 = (bf16[1024,2048]{1,0:T(8,128)(2,1)}, f32[1,2048]{1,0:T(1,128)}, bf16[8,528,256]{2,1,0:T(8,128)(2,1)}) custom-call(bf16[512,2048]{1,0:T(8,128)(2,1)} %convolution_convert_fusion.5.refs_0_, bf16[16,2048]{1,0:T(8,128)(2,1)} %slice.262.refs_1_, f32[32,2048]{1,0:T(8,128)} %get-tuple-element.45.refs_1_.refs_2_, ...), custom_call_target="tpu_custom_call" | custom-call | tf_op jit(solution)/shard_map/pallas_call | solution.py:383
  523.2 3.0 fusion.60
  529.4 9.7 %convolution_convert_fusion.refs_0_ = bf16[2048,2048]{1,0:T(8,128)(2,1)} fusion(bf16[512,2048]{1,0:T(8,128)(2,1)} %get-tuple-element.42, bf16[2048,128]{0,1:T(8,128)(2,1)} %convolution_convert_fusion.10, bf16[2048,64]{0,1:T(8,128)(2,1)} %get-tuple-element.96, bf16[2048,64]{0,1:T(8,128)(2,1)} %get-tuple-element.95, bf16[2048,128]{0,1:T(8,128)(2,1)} %copy.125), kind=kOutput, calls=%fused_computation.16 | convolution fusion | flops 3231711232 | bytes 11534336 | tf_op jit(solution)/shard_map/dot_general | solution.py:558
  545.3 7.0 convolution_convert_fusion.6
  553.8 116.5 %shard_map.380 = (bf16[2048,2048]{1,0:T(8,128)(2,1)}, f32[1,2048]{1,0:T(1,128)}, bf16[8,512,256]{2,1,0:T(8,128)(2,1)}) custom-call(bf16[2048,2048]{1,0:T(8,128)(2,1)} %convolution_convert_fusion.refs_0_, f32[64,2048]{1,0:T(8,128)} %dynamic-slice_convert_fusion.refs_1_, f32[64,2048]{1,0:T(8,128)} %convolution_bitcast_fusion.refs_2_, f32[3,2048]{1,0:T(4,128)} %bitcast.172, ...), custom_call_target="tpu_custom_call" | custom-call | tf_op jit(solution)/shard_map/pallas_call | solution.py:383
  670.3 11.5 %fusion.3 = f32[1000,2048]{1,0:T(8,128)S(1)} fusion(bf16[2048,2048]{1,0:T(8,128)(2,1)} %get-tuple-element.51, s32[1000]{0:T(1024)S(1)} %iota_add_fusion, s32[2048]{0:T(1024)S(1)} %bitcast.201), kind=kOutput, calls=%fused_computation.6 | convolution fusion | flops 8390656000 | bytes 16592800 | tf_op jit(solution)/shard_map/dot_general | solution.py:558
  684.4 5.8 multiply_reduce_fusion
  701.9 4.3 copy.129
  706.2 3.6 multiply_reduce_fusion.2
  716.7 9.9 %shard_map.381 = f32[32,8,128]{2,1,0:T(8,128)} custom-call(f32[8,128]{1,0:T(8,128)} %broadcast_in_dim.82.x_ref), custom_call_target="tpu_custom_call" | custom-call | tf_op jit(solution)/shard_map/pallas_call | solution.py:438
  728.8 19.2 %shard_map.382 = f32[32,48,128]{2,1,0:T(8,128)} custom-call(f32[48,128]{1,0:T(8,128)} %reshape.293.x_ref), custom_call_target="tpu_custom_call" | custom-call | tf_op jit(solution)/shard_map/pallas_call | solution.py:438
  751.2 22.2 %multiply_subtract_fusion = (f32[1000,2048]{1,0:T(8,128)}, f32[1000,2048]{1,0:T(8,128)}, f32[1000,2048]{1,0:T(8,128)}) fusion(f32[1000,2048]{1,0:T(8,128)} %param.25, f32[1000,2048]{1,0:T(8,128)} %get-tuple-element.118, f32[]{:T(128)S(6)} %min.3, f32[1000,2048]{1,0:T(8,128)} %param.26, f32[1000,2048]{1,0:T(8,128)} %param.27), kind=kLoop, calls=%fused_computation.11 | loop fusion | flops 32768000 | bytes 57344004 | tf_op jit(solution)/shard_map/sub | solution.py:575
  773.4 6.1 multiply_subtract_fusion.2
  783.0 11.2 %multiply_subtract_fusion.1 = (f32[256,2,1408]{2,1,0:T(2,128)}, f32[256,2,1408]{2,1,0:T(2,128)}, f32[256,2,1408]{2,1,0:T(2,128)}) fusion(f32[256,2,1408]{2,1,0:T(2,128)S(1)} %copy-done.10, f32[256,2,1408]{2,1,0:T(2,128)S(1)} %copy.129, f32[]{:T(128)S(6)} %min.3, f32[256,2,1408]{2,1,0:T(2,128)S(1)} %copy-done.20, f32[256,2,1408]{2,1,0:T(2,128)S(1)} %copy-done.21), kind=kLoop, calls=%fused_computation.38 | loop fusion | flops 11534336 | bytes 20185092 | tf_op jit(solution)/shard_map/sub | solution.py:575
  (278 shorter events, 111.1 us)
Async XLA Ops:
  15.8 5.9 copy-start.52
  21.8 13.6 %copy-start.72 = (s32[8,1,256]{2,1,0:T(1,128)}, s32[8,1,256]{2,1,0:T(1,128)S(1)}, u32[]{:S(2)}) copy-start(s32[8,1,256]{2,1,0:T(1,128)S(1)} %get-tuple-element.102) | copy-start | bytes 24580
  21.8 13.6 %copy-start.23 = (f32[512,256]{1,0:T(8,128)S(1)}, f32[512,256]{1,0:T(8,128)}, u32[]{:S(2)}) copy-start(f32[512,256]{1,0:T(8,128)} %param.31) | copy-start | bytes 1572868
  21.8 13.7 %copy-start.16 = (f32[256,3,512]{2,0,1:T(8,128)S(1)}, f32[256,3,512]{2,0,1:T(8,128)}, u32[]{:S(2)}) copy-start(f32[256,3,512]{2,0,1:T(8,128)} %param.28) | copy-start | bytes 4718596
  152.6 5.3 copy-start.67
  152.6 5.8 copy-start.11
  157.8 5.7 copy-start.69
  163.5 17.1 %copy-start.18 = (f32[2048,384]{0,1:T(8,128)}, f32[2048,384]{0,1:T(8,128)S(1)}, u32[]{:S(2)}) copy-start(f32[2048,384]{0,1:T(8,128)S(1)} %fusion.19) | copy-start | bytes 9437188
  163.5 6.5 copy-start.74
  186.7 5.4 copy-start.9
  338.1 5.8 copy-start.55
  344.0 19.6 %copy-start.60 = (f32[2,512]{1,0:T(2,128)S(1)}, f32[2,512]{1,0:T(2,128)}, u32[]{:S(2)}) copy-start(f32[2,512]{1,0:T(2,128)} %get-tuple-element.83) | copy-start | bytes 12292
  344.1 19.6 %copy-start.6 = (f32[512,1000]{0,1:T(8,128)S(1)}, f32[512,1000]{0,1:T(8,128)}, u32[]{:S(2)}) copy-start(f32[512,1000]{0,1:T(8,128)} %get-tuple-element.114) | copy-start | bytes 6144004
  363.7 5.1 copy-start.53
  363.7 5.0 copy-start.5
  373.9 47.1 %copy-start.39 = (f32[512,352]{0,1:T(8,128)S(1)}, f32[512,352]{0,1:T(8,128)}, u32[]{:S(2)}) copy-start(f32[512,352]{0,1:T(8,128)} %copy-done.38) | copy-start | bytes 2162692
  529.4 13.8 %copy-start.37 = (bf16[512,128]{1,0:T(8,128)(2,1)S(1)}, bf16[512,128]{1,0:T(8,128)(2,1)}, u32[]{:S(2)}) copy-start(bf16[512,128]{1,0:T(8,128)(2,1)} %copy-done.36) | copy-start | bytes 393220
  553.8 116.5 %copy-start.73 = (s32[8,1,256]{2,1,0:T(1,128)S(1)}, s32[8,1,256]{2,1,0:T(1,128)}, u32[]{:S(2)}) copy-start(s32[8,1,256]{2,1,0:T(1,128)} %copy-done.72) | copy-start | bytes 24580
  670.3 11.5 %copy-start.15 = (f32[512,1000]{0,1:T(8,128)S(1)}, f32[512,1000]{0,1:T(8,128)}, u32[]{:S(2)}) copy-start(f32[512,1000]{0,1:T(8,128)} %get-tuple-element.112) | copy-start | bytes 6144004
  670.3 11.5 %copy-start.28 = (bf16[32,1,16,2048]{3,2,1,0:T(8,128)(2,1)S(1)}, bf16[32,1,16,2048]{3,2,1,0:T(8,128)(2,1)}, u32[]{:S(2)}) copy-start(bf16[32,1,16,2048]{3,2,1,0:T(8,128)(2,1)} %copy-done.27) | copy-start | bytes 6291460
  670.3 11.5 %copy-start.54 = (f32[1,512]{1,0:T(1,128)S(1)}, f32[1,512]{1,0:T(1,128)}, u32[]{:S(2)}) copy-start(f32[1,512]{1,0:T(1,128)} %copy-done.53) | copy-start | bytes 6148
  684.4 5.8 copy-start.25
  693.7 6.4 copy-start.7
  710.4 17.7 %copy-start.64 = (f32[1,2048]{1,0:T(1,128)S(1)}, f32[1,2048]{1,0:T(1,128)}, u32[]{:S(2)}) copy-start(f32[1,2048]{1,0:T(1,128)} %get-tuple-element.56) | copy-start | bytes 24580
  710.5 17.7 %copy-start.65 = (f32[1,2048]{1,0:T(1,128)S(1)}, f32[1,2048]{1,0:T(1,128)}, u32[]{:S(2)}) copy-start(f32[1,2048]{1,0:T(1,128)} %get-tuple-element.55) | copy-start | bytes 24580
  710.5 17.7 %copy-start.66 = (f32[1,2048]{1,0:T(1,128)S(1)}, f32[1,2048]{1,0:T(1,128)}, u32[]{:S(2)}) copy-start(f32[1,2048]{1,0:T(1,128)} %get-tuple-element.54) | copy-start | bytes 24580
  773.4 7.2 copy-start.24
  773.4 7.3 copy-start.40
  773.4 7.3 copy-start.41
  773.4 8.7 %copy-start.20 = (f32[256,2,1408]{2,1,0:T(2,128)S(1)}, f32[256,2,1408]{2,1,0:T(2,128)}, u32[]{:S(2)}) copy-start(f32[256,2,1408]{2,1,0:T(2,128)} %param.35) | copy-start | bytes 8650756
  773.4 8.7 %copy-start.21 = (f32[256,2,1408]{2,1,0:T(2,128)S(1)}, f32[256,2,1408]{2,1,0:T(2,128)}, u32[]{:S(2)}) copy-start(f32[256,2,1408]{2,1,0:T(2,128)} %param.36) | copy-start | bytes 8650756
  783.0 12.8 %copy-start.35 = (f32[1408,256]{1,0:T(8,128)S(1)}, f32[1408,256]{1,0:T(8,128)}, u32[]{:S(2)}) copy-start(f32[1408,256]{1,0:T(8,128)} %param.39) | copy-start | bytes 4325380
  (47 other events, 128.6 us)

commit v3 on v2

--- a/solution.py
+++ b/solution.py
@@ -42,7 +42,7 @@
 
 
 class Links:
-    def __init__(self, send_sem, recv_sem, cargo):
+    def __init__(self, send_sem, recv_sem):
         data_index, model_index = lax.axis_index("dp"), lax.axis_index("mp")
         z, y, x, c = data_index // 2, data_index % 2, model_index // 2, model_index % 2
         self.c = c
@@ -54,8 +54,6 @@
         self.c_side = (data_index, x * 2 + 1 - c)
         self.send_sem, self.recv_sem, self.sent, self.slots = send_sem, recv_sem, [], {}
         peers = self.z_side[1:] + [self.x_side, self.y_side, self.c_side]
-        if cargo:
-            peers += [(zd * 2 + 1 - y, model_index) for zd in self.zs[1:]]
         barrier = pltpu.get_barrier_semaphore()
         for peer in peers:
             pl.semaphore_signal(barrier, inc=1, device_id=peer, device_id_type=MESH)
@@ -88,51 +86,6 @@
     def finish(self):
         for copy in self.sent:
             copy.wait_send()
-
-
-class Cargo:
-    def __init__(self, source, target, send_sem, recv_sem, own_sem):
-        self.me, self.model_index = lax.axis_index("dp"), lax.axis_index("mp")
-        self.source, self.target = source, target
-        self.send_sem, self.recv_sem, self.own_sem, self.sent = send_sem, recv_sem, own_sem, []
-
-    def block(self, ref, index):
-        if len(ref.shape) == 3:
-            return ref.at[index]
-        size = ref.shape[1] // 8
-        return ref.at[:, pl.ds(pl.multiple_of(index * size, size), size)]
-
-    def start(self):
-        self.own = pltpu.make_async_copy(
-            self.block(self.source, self.me), self.block(self.target, self.me), self.own_sem
-        )
-        self.own.start()
-        for shift in (4, 3, 5, 2, 6, 1, 7):
-            peer = lax.rem(self.me + shift, 8)
-            copy = pltpu.make_async_remote_copy(
-                src_ref=self.block(self.source, peer),
-                dst_ref=self.block(self.target, self.me),
-                send_sem=self.send_sem.at[shift - 1],
-                recv_sem=self.recv_sem.at[shift - 1],
-                device_id=(peer, self.model_index),
-                device_id_type=MESH,
-            )
-            copy.start()
-            self.sent.append(copy)
-
-    def finish(self):
-        self.own.wait()
-        for shift in range(1, 8):
-            here = self.block(self.target, lax.rem(self.me + 8 - shift, 8))
-            pltpu.make_async_copy(here, here, self.recv_sem.at[shift - 1]).wait()
-        for copy in self.sent:
-            copy.wait_send()
-
-
-def swapped(shape):
-    if len(shape) == 3:
-        return (shape[1], shape[0] * shape[2])
-    return (8, shape[0], shape[1] // 8)
 
 
 class Gather:
@@ -284,22 +237,17 @@
     (partial,) = take(1)
     ready = take(plan["ready"])
     extras = take(plan["extras"])
-    cargo_in = take(plan["cargo"])
     (gathered,) = take(1)
     kept = take(plan["kept"])
     sums = take(plan["sums"])
-    cargo_out = take(plan["cargo"])
     buffers = take(5)
     held, send_sem, recv_sem, load_sem, own_sem = take(5)
     order, steps = plan["order"], plan["steps"]
-    link = Links(send_sem, recv_sem, plan["cargo"])
-    cargo = Cargo(*cargo_in, *cargo_out, *refs) if cargo_in else None
+    link = Links(send_sem, recv_sem)
     gather = Gather(link, gathered, steps, own_sem)
     if ready:
         gather.begin(0, ready[0])
     scatter = Scatter(link, partial, plan["rows"], order, buffers, load_sem)
-    if cargo:
-        cargo.start()
     ticks = len(order) + 7
     agenda = [[] for _ in range(ticks)]
     if ready:
@@ -330,13 +278,9 @@
             step(index)
     gather.finish()
     link.finish()
-    if cargo:
-        cargo.finish()
-
-
-def relay(
-    partial, row_step, ident, extras=(), kept=0, sums=0, order=None, slot=None, ready=None, cargo=None
-):
+
+
+def relay(partial, row_step, ident, extras=(), kept=0, sums=0, order=None, slot=None, ready=None):
     rows, width = partial.shape[0] // (lax.axis_size("dp") * lax.axis_size("mp")), partial.shape[1]
     groups = rows // GROUP
     order = list(range(groups)) if order is None else order
@@ -355,8 +299,7 @@
                 outs[slot(p)] = out
         gathered = lax.all_gather(jnp.concatenate(outs), BOTH, axis=0, tiled=True)
         keeps = [jnp.concatenate(parts) for parts in zip(*keeps)]
-        moved = [] if cargo is None else [exchange_plain(cargo)]
-        return [gathered, *keeps, *adds, *moved]
+        return [gathered, *keeps, *adds]
     plan = dict(
         rows=rows,
         order=order,
@@ -364,33 +307,33 @@
         steps=steps,
         ready=int(ready is not None),
         extras=len(extras),
-        cargo=int(cargo is not None),
         kept=kept,
         sums=sums,
     )
     low = partial.dtype
     vmem = pl.BlockSpec(memory_space=pltpu.VMEM)
-    load = [] if cargo is None else [cargo]
     copies = 31 * (groups + steps)
     shapes = [jax.ShapeDtypeStruct((32 * steps * GROUP, width), low)]
     shapes += [jax.ShapeDtypeStruct((rows, width), jnp.float32)] * kept
     shapes += [jax.ShapeDtypeStruct((1, width), jnp.float32)] * sums
-    shapes += [jax.ShapeDtypeStruct(swapped(value.shape), value.dtype) for value in load]
     buffers = [pltpu.VMEM((count, rows, width), low) for count in (16, 16, 4, 8, 3)]
     semaphores = [pltpu.SemaphoreType.DMA((count,)) for count in (copies, copies, 16 * groups, steps)]
-    semaphores += [pltpu.SemaphoreType.DMA((7,))] * 2 * len(load)
-    semaphores += [pltpu.SemaphoreType.DMA] * len(load)
     return pl.pallas_call(
         functools.partial(relay_kernel, plan, row_step),
         out_shape=shapes,
-        in_specs=[ANY] * (1 + plan["ready"]) + [vmem] * len(extras) + [ANY] * len(load),
-        out_specs=[ANY] + [vmem] * (kept + sums) + [ANY] * len(load),
+        in_specs=[ANY] * (1 + plan["ready"]) + [vmem] * len(extras),
+        out_specs=[ANY] + [vmem] * (kept + sums),
         scratch_shapes=buffers + [pltpu.VMEM((steps, GROUP, width), low)] + semaphores,
         compiler_params=comm_params(ident),
-    )(partial, *([] if ready is None else [ready]), *extras, *load)
-
-
-def exchange_plain(value):
+        cost_estimate=pl.CostEstimate(flops=1, bytes_accessed=1, transcendentals=0),
+    )(partial, *([] if ready is None else [ready]), *extras)
+
+
+def after(value, *first):
+    return lax.optimization_barrier((value, *first))[0]
+
+
+def swap_blocks(value):
     count = lax.axis_size("dp")
     if len(value.shape) == 3:
         moved = lax.all_to_all(value, "dp", split_axis=0, concat_axis=0, tiled=True)
@@ -516,6 +459,222 @@
         ],
         compiler_params=comm_params(ident),
     )(*values)
+
+
+def turned(values, cosine, sine_table):
+    return values * cosine + pltpu.roll(values, HEAD_DIM // 2, 1) * sine_table
+
+
+def softmax_rows(query, keys, places):
+    scores = dot(query, keys, 1, 1) * (1.0 / math.sqrt(HEAD_DIM))
+    columns = lax.broadcasted_iota(jnp.int32, scores.shape, 1)
+    scores = jnp.where(columns <= places, scores, NEG)
+    weights = jnp.exp(scores - jnp.max(scores, axis=-1, keepdims=True))
+    return weights / jnp.sum(weights, axis=-1, keepdims=True)
+
+
+def attend_kernel(
+    exit_ref,
+    resid_ref,
+    gain_ref,
+    head_ref,
+    cosine_ref,
+    sine_ref,
+    pick_ref,
+    place_ref,
+    live_ref,
+    attn_ref,
+    query_ref,
+    key_ref,
+    value_ref,
+    out_ref,
+    partial_ref,
+):
+    block, blocks = pl.program_id(0), key_ref.shape[0] // resid_ref.shape[0]
+    rows, slots = resid_ref.shape[0], pick_ref.shape[1]
+    low = jnp.bfloat16
+    attn = norm_fwd(resid_ref[...].astype(jnp.float32), gain_ref[...])[0].astype(low)
+    attn_ref[...] = attn
+    projected = dot(attn, head_ref[: 3 * HEAD_DIM], 1, 1)
+    cosine, sine_table = cosine_ref[...], sine_ref[...]
+    query = turned(projected[:, :HEAD_DIM], cosine, sine_table).astype(low)
+    at = pl.ds(pl.multiple_of(block * rows, rows), rows)
+    key_ref[at] = turned(projected[:, HEAD_DIM : 2 * HEAD_DIM], cosine, sine_table).astype(low)
+    value_ref[at] = projected[:, 2 * HEAD_DIM :].astype(low)
+    at = pl.ds(pl.multiple_of(block * slots, slots), slots)
+    query_ref[at] = dot(pick_ref[0], query).astype(low)
+
+    @pl.when(block == blocks - 1)
+    def _():
+        exit_here = exit_ref[0]
+        step = 2 * slots
+        for index in range(blocks // 2):
+            reach = (index + 1) * 2 * rows
+            at = slice(index * step, (index + 1) * step)
+            probs = softmax_rows(query_ref[at], key_ref[:reach], place_ref[at]).astype(low)
+            out = (dot(probs, value_ref[:reach]) * live_ref[at]).astype(low)
+            out_ref[at] = out
+            share = dot(out, head_ref[3 * HEAD_DIM :]).astype(low)
+            groups = step // partial_ref.shape[2]
+            at = slice(index * groups, (index + 1) * groups)
+            share = share.reshape(groups, 1, -1, share.shape[1])
+            partial_ref[at, pl.ds(exit_here, 1)] = share
+            partial_ref[at, pl.ds(1 - exit_here, 1)] = jnp.zeros_like(share)
+
+
+def attend_back_kernel(
+    exit_ref,
+    done_ref,
+    head_ref,
+    out_ref,
+    query_ref,
+    key_ref,
+    value_ref,
+    cosine_ref,
+    sine_ref,
+    slot_cosine_ref,
+    slot_sine_ref,
+    pick_ref,
+    place_ref,
+    attn_ref,
+    partial_ref,
+    parts_ref,
+    key_sum,
+    value_sum,
+    turned_ref,
+    head_sum,
+):
+    block, blocks = pl.program_id(0), key_ref.shape[0] // attn_ref.shape[0]
+    rows, slots = attn_ref.shape[0], pick_ref.shape[1]
+    low = jnp.bfloat16
+    scale = 1.0 / math.sqrt(HEAD_DIM)
+
+    @pl.when(block == 0)
+    def _():
+        key_sum[...] = jnp.zeros_like(key_sum)
+        value_sum[...] = jnp.zeros_like(value_sum)
+        step = 2 * slots
+        width = done_ref.shape[-1]
+        done = done_ref[...].reshape(-1, width)
+        parts_ref[3 * HEAD_DIM :] = dot(out_ref[...], done, 0, 0).astype(low)
+        dout = dot(done, head_ref[3 * HEAD_DIM :], 1, 1).astype(low)
+        for index in range(blocks // 2):
+            reach = (index + 1) * 2 * rows
+            at = slice(index * step, (index + 1) * step)
+            probs = softmax_rows(query_ref[at], key_ref[:reach], place_ref[at])
+            dprobs = dot(dout[at], value_ref[:reach], 1, 1)
+            delta = jnp.sum(probs * dprobs, axis=-1, keepdims=True)
+            dscores = (probs * (dprobs - delta)).astype(low)
+            dquery = dot(dscores, key_ref[:reach]) * scale
+            dquery = turned(dquery, slot_cosine_ref[at], -slot_sine_ref[at]).astype(low)
+            for half in (0, 1):
+                where = 2 * index + half
+                turned_ref[where * rows : (where + 1) * rows, :HEAD_DIM] = dot(
+                    pick_ref[where], dquery[half * slots : (half + 1) * slots], 0, 0
+                ).astype(low)
+            key_sum[:reach] += dot(dscores, query_ref[at], 0, 0)
+            value_sum[:reach] += dot(probs.astype(low), dout[at], 0, 0)
+        dkey = turned(key_sum[...] * scale, cosine_ref[...], -sine_ref[...])
+        turned_ref[:, HEAD_DIM : 2 * HEAD_DIM] = dkey.astype(low)
+        turned_ref[:, 2 * HEAD_DIM :] = value_sum[...].astype(low)
+
+    at = pl.ds(pl.multiple_of(block * rows, rows), rows)
+    dprojected = turned_ref[at]
+    partial_ref[...] = dot(dprojected, head_ref[: 3 * HEAD_DIM]).astype(low)
+    term = dot(dprojected, attn_ref[...], 0, 0)
+
+    @pl.when(block == 0)
+    def _():
+        head_sum[...] = term
+
+    @pl.when(block > 0)
+    def _():
+        head_sum[...] += term
+
+    @pl.when(block == blocks - 1)
+    def _():
+        parts_ref[: 3 * HEAD_DIM] = head_sum[...].astype(low)
+
+
+def local_params():
+    return dict(
+        compiler_params=pltpu.CompilerParams(vmem_limit_bytes=VMEM_LIMIT),
+        cost_estimate=pl.CostEstimate(flops=1, bytes_accessed=1, transcendentals=0),
+    )
+
+
+def whole_spec(value):
+    return pl.BlockSpec(value.shape, lambda b, e: (0,) * len(value.shape))
+
+
+def attend(exit_here, resid, gain, head, cosine, sine_table, pick, places, live, slots_here):
+    (tokens, width), (blocks, slots, rows) = resid.shape, pick.shape
+    low = resid.dtype
+    devices = blocks * slots // slots_here
+    by_block = lambda columns: pl.BlockSpec((rows, columns), lambda b, e: (b, 0))
+    outs = [
+        jax.ShapeDtypeStruct(shape, low)
+        for shape in (
+            (tokens, width),
+            (blocks * slots, HEAD_DIM),
+            (tokens, HEAD_DIM),
+            (tokens, HEAD_DIM),
+            (blocks * slots, HEAD_DIM),
+            (devices, 2, slots_here, width),
+        )
+    ]
+    return pl.pallas_call(
+        attend_kernel,
+        out_shape=outs,
+        grid_spec=pltpu.PrefetchScalarGridSpec(
+            num_scalar_prefetch=1,
+            grid=(blocks,),
+            in_specs=[
+                by_block(width),
+                whole_spec(gain),
+                whole_spec(head),
+                by_block(HEAD_DIM),
+                by_block(HEAD_DIM),
+                pl.BlockSpec((1, slots, rows), lambda b, e: (b, 0, 0)),
+                whole_spec(places),
+                whole_spec(live),
+            ],
+            out_specs=[by_block(width)] + [whole_spec(out) for out in outs[1:]],
+        ),
+        **local_params(),
+    )(exit_here, resid, gain, head, cosine, sine_table, pick, places, live)
+
+
+def attend_back(
+    exit_here, done, head, out, query, key, value, cosine, sine_table, slot_turns, pick, places, attn
+):
+    (tokens, width), (blocks, slots, rows) = attn.shape, pick.shape
+    low = attn.dtype
+    devices, _, slots_here, _ = done.shape
+    by_block = pl.BlockSpec((rows, width), lambda b, e: (b, 0))
+    inner = [head, out, query, key, value, cosine, sine_table, *slot_turns, pick, places]
+    parts = jax.ShapeDtypeStruct((4 * HEAD_DIM, width), low)
+    return pl.pallas_call(
+        attend_back_kernel,
+        out_shape=[jax.ShapeDtypeStruct((tokens, width), low), parts],
+        grid_spec=pltpu.PrefetchScalarGridSpec(
+            num_scalar_prefetch=1,
+            grid=(blocks,),
+            in_specs=[
+                pl.BlockSpec((devices, 1, slots_here, width), lambda b, e: (0, e[0], 0, 0))
+            ]
+            + [whole_spec(value) for value in inner]
+            + [by_block],
+            out_specs=[by_block, whole_spec(parts)],
+            scratch_shapes=[
+                pltpu.VMEM((tokens, HEAD_DIM), jnp.float32),
+                pltpu.VMEM((tokens, HEAD_DIM), jnp.float32),
+                pltpu.VMEM((tokens, 3 * HEAD_DIM), low),
+                pltpu.VMEM((3 * HEAD_DIM, width), jnp.float32),
+            ],
+        ),
+        **local_params(),
+    )(exit_here, done, *inner, attn)
 
 
 def norm_fwd(values, gain):
@@ -667,63 +826,88 @@
         axis=1,
     )
 
+    head_rows = swap_blocks(after(jnp.repeat(head_rows, sharers, axis=0), ints))
+
     table_low = table.astype(low)
     id_hits = (all_ids[:, None] == vocab_ids[None, :]).astype(low)
-    resid_low, head_rows = relay(
+    (resid_low,) = relay(
         dot(id_hits, table_low).astype(low),
         lambda p, total, extras: (total.astype(low), (), ()),
         1,
-        cargo=jnp.repeat(head_rows, sharers, axis=0),
-    )
-    qkv_head, out_head = head_rows[: 3 * HEAD_DIM], head_rows[3 * HEAD_DIM :]
-    attn_low = norm_fwd(resid_low.astype(jnp.float32), gain_rows[0])[0].astype(low)
-
-    projected = dot(attn_low, qkv_head, 1, 1)
-    cosine, sine_table = rotary(token_places, HEAD_DIM)
-    query_low = rotate_pairs(projected[:, :HEAD_DIM], cosine, sine_table).astype(low)
-    key_low = rotate_pairs(projected[:, HEAD_DIM : 2 * HEAD_DIM], cosine, sine_table).astype(low)
-    value_low = projected[:, 2 * HEAD_DIM :].astype(low)
+    )
+    hidden_rows = swap_blocks(after(hidden_rows, resid_low))
     pick_share = lax.dynamic_slice_in_dim(
         lax.dynamic_index_in_dim(pick_low, exit_here, 0, keepdims=False),
         share_here * (data_size // shares),
         data_size // shares,
         0,
     )
-    query_share = lax.dynamic_slice_in_dim(
-        query_low.reshape(data_size, block_rows, HEAD_DIM),
-        share_here * (data_size // shares),
-        data_size // shares,
-        0,
-    )
-    query_slots = (
-        jnp.einsum("brt,btd->brd", pick_share, query_share, preferred_element_type=jnp.float32)
-        .astype(low)
-        .reshape(share_slots, HEAD_DIM)
-    )
-
     def share_of(per_slot):
         return lax.dynamic_slice(per_slot, (exit_here, share_here * share_slots), (1, share_slots))[
             0
         ]
 
     places_share, live_share = share_of(slot_places), share_of(live)
-    scores = dot(query_slots, key_low, 1, 1) * score_scale
-    allowed = token_places[None, :] <= places_share[:, None]
-    scores = jnp.where(allowed, scores, NEG)
-    weights = jnp.exp(scores - jnp.max(scores, axis=-1, keepdims=True))
-    probs = weights / jnp.sum(weights, axis=-1, keepdims=True)
-    probs_low = probs.astype(low)
-    attn_out = (dot(probs_low, value_low) * live_share[:, None]).astype(low)
-
-    def spread(per_share):
-        if shares > 1:
-            full = jnp.zeros((data_size * R_DEV, width), per_share.dtype)
-            per_share = lax.dynamic_update_slice_in_dim(
-                full, per_share, share_here * share_slots, 0
-            )
-        exits = jnp.arange(2, dtype=jnp.int32)[None, :, None, None]
-        rows = per_share.reshape(devices, 1, slots_here, width)
-        return jnp.where(exits == exit_here, rows, 0).reshape(-1, width)
+    cosine, sine_table = rotary(token_places, HEAD_DIM)
+    cosine_share, sine_share = rotary(places_share, HEAD_DIM)
+
+    def turns(cosines, sines):
+        return (
+            jnp.concatenate([cosines, cosines], axis=1),
+            jnp.concatenate([-sines, sines], axis=1),
+        )
+
+    if kernel_mesh():
+        attn_low, query_slots, key_low, value_low, attn_out, out_partial = attend(
+            exit_here[None],
+            resid_low,
+            gain_rows[:1],
+            head_rows,
+            *turns(cosine, sine_table),
+            pick_share,
+            places_share[:, None],
+            live_share[:, None],
+            slots_here,
+        )
+        out_partial = out_partial.reshape(-1, width)
+    else:
+        qkv_head, out_head = head_rows[: 3 * HEAD_DIM], head_rows[3 * HEAD_DIM :]
+        attn_low = norm_fwd(resid_low.astype(jnp.float32), gain_rows[0])[0].astype(low)
+
+        projected = dot(attn_low, qkv_head, 1, 1)
+        query_low = rotate_pairs(projected[:, :HEAD_DIM], cosine, sine_table).astype(low)
+        key_low = rotate_pairs(projected[:, HEAD_DIM : 2 * HEAD_DIM], cosine, sine_table).astype(low)
+        value_low = projected[:, 2 * HEAD_DIM :].astype(low)
+        query_share = lax.dynamic_slice_in_dim(
+            query_low.reshape(data_size, block_rows, HEAD_DIM),
+            share_here * (data_size // shares),
+            data_size // shares,
+            0,
+        )
+        query_slots = (
+            jnp.einsum("brt,btd->brd", pick_share, query_share, preferred_element_type=jnp.float32)
+            .astype(low)
+            .reshape(share_slots, HEAD_DIM)
+        )
+
+        scores = dot(query_slots, key_low, 1, 1) * score_scale
+        allowed = token_places[None, :] <= places_share[:, None]
+        scores = jnp.where(allowed, scores, NEG)
+        weights = jnp.exp(scores - jnp.max(scores, axis=-1, keepdims=True))
+        probs = weights / jnp.sum(weights, axis=-1, keepdims=True)
+        probs_low = probs.astype(low)
+        attn_out = (dot(probs_low, value_low) * live_share[:, None]).astype(low)
+
+        def spread(per_share):
+            if shares > 1:
+                full = jnp.zeros((data_size * R_DEV, width), per_share.dtype)
+                per_share = lax.dynamic_update_slice_in_dim(
+                    full, per_share, share_here * share_slots, 0
+                )
+            exits = jnp.arange(2, dtype=jnp.int32)[None, :, None, None]
+            rows = per_share.reshape(devices, 1, slots_here, width)
+            return jnp.where(exits == exit_here, rows, 0).reshape(-1, width)
+        out_partial = spread(dot(attn_out, out_head).astype(low))
 
     block_low = lax.dynamic_slice_in_dim(resid_low, data_index * block_rows, block_rows, 0)
     pick_here = lax.dynamic_slice(
@@ -737,13 +921,12 @@
         gain = 2 if p == 0 else 1
         return (norm_fwd(resid, extras[1][gain : gain + 1])[0].astype(low), (resid,), ())
 
-    first_rows, resid_one, hidden_rows = relay(
-        spread(dot(attn_out, out_head).astype(low)),
+    first_rows, resid_one = relay(
+        out_partial,
         first_step,
         2,
         extras=[dot(pick_here, block_low), gain_rows],
         kept=1,
-        cargo=hidden_rows,
     )
     first_rows = first_rows.reshape(devices, 2, slots_here, width)
     exit_rows_one = first_rows[:, 0].reshape(-1, width)
@@ -823,7 +1006,7 @@
         back, gain_grad = norm_back(unit, scale, gain, total)
         return ((extras[1][GROUP : 2 * GROUP] + back).astype(low), (), (gain_grad[None],))
 
-    done_low, mlp_grad, hidden_parts = relay(
+    done_low, mlp_grad = relay(
         dot(dgate_up, gate_up_head).astype(low),
         mlp_step,
         6,
@@ -831,43 +1014,60 @@
         sums=1,
         slot=lambda p: 1,
         ready=dexits[:GROUP].astype(low),
-        cargo=jnp.concatenate([gate_up_local.astype(low), down_local.astype(low)]),
-    )
+    )
+    hidden_parts = jnp.concatenate([gate_up_local.astype(low), down_local.astype(low)])
+    hidden_parts = swap_blocks(after(hidden_parts, done_low))
     done_low = done_low.reshape(devices, 2, slots_here, width)
 
-    done_share = lax.dynamic_slice(
-        lax.dynamic_index_in_dim(done_low, exit_here, 1, keepdims=False).reshape(-1, width),
-        (share_here * share_slots, 0),
-        (share_slots, width),
-    )
-    out_local = dot(attn_out, done_share, 0, 0)
-    dattn_low = dot(done_share, out_head, 1, 1).astype(low)
-    dprobs = dot(dattn_low, value_low, 1, 1)
-    delta = jnp.sum(probs * dprobs, axis=-1, keepdims=True)
-    dscores = (probs * (dprobs - delta)).astype(low)
-    cosine_share, sine_share = rotary(places_share, HEAD_DIM)
-    dquery = rotate_pairs(dot(dscores, key_low) * score_scale, cosine_share, -sine_share).astype(
-        low
-    )
-    dquery_share = jnp.einsum(
-        "brt,brd->btd",
-        pick_share,
-        dquery.reshape(-1, R_DEV, HEAD_DIM),
-        preferred_element_type=jnp.float32,
-    ).astype(low)
-    if shares > 1:
-        dquery_share = lax.dynamic_update_slice_in_dim(
-            jnp.zeros((data_size, block_rows, HEAD_DIM), low),
-            dquery_share,
-            share_here * (data_size // shares),
-            0,
-        )
-    dkey = rotate_pairs(dot(dscores, query_slots, 0, 0) * score_scale, cosine, -sine_table)
-    dvalue = dot(probs_low, dattn_low, 0, 0)
-    dprojected = jnp.concatenate(
-        [dquery_share.reshape(tokens, HEAD_DIM), dkey.astype(low), dvalue.astype(low)], axis=1
-    )
-    qkv_local = dot(dprojected, attn_low, 0, 0)
+    if kernel_mesh():
+        zero_partial, head_parts = attend_back(
+            exit_here[None],
+            done_low,
+            head_rows,
+            attn_out,
+            query_slots,
+            key_low,
+            value_low,
+            *turns(cosine, sine_table),
+            turns(cosine_share, sine_share),
+            pick_share,
+            places_share[:, None],
+            attn_low,
+        )
+    else:
+        done_share = lax.dynamic_slice(
+            lax.dynamic_index_in_dim(done_low, exit_here, 1, keepdims=False).reshape(-1, width),
+            (share_here * share_slots, 0),
+            (share_slots, width),
+        )
+        out_local = dot(attn_out, done_share, 0, 0)
+        dattn_low = dot(done_share, out_head, 1, 1).astype(low)
+        dprobs = dot(dattn_low, value_low, 1, 1)
+        delta = jnp.sum(probs * dprobs, axis=-1, keepdims=True)
+        dscores = (probs * (dprobs - delta)).astype(low)
+        dquery = rotate_pairs(dot(dscores, key_low) * score_scale, cosine_share, -sine_share).astype(
+            low
+        )
+        dquery_share = jnp.einsum(
+            "brt,brd->btd",
+            pick_share,
+            dquery.reshape(-1, R_DEV, HEAD_DIM),
+            preferred_element_type=jnp.float32,
+        ).astype(low)
+        if shares > 1:
+            dquery_share = lax.dynamic_update_slice_in_dim(
+                jnp.zeros((data_size, block_rows, HEAD_DIM), low),
+                dquery_share,
+                share_here * (data_size // shares),
+                0,
+            )
+        dkey = rotate_pairs(dot(dscores, query_slots, 0, 0) * score_scale, cosine, -sine_table)
+        dvalue = dot(probs_low, dattn_low, 0, 0)
+        dprojected = jnp.concatenate(
+            [dquery_share.reshape(tokens, HEAD_DIM), dkey.astype(low), dvalue.astype(low)], axis=1
+        )
+        head_parts = jnp.concatenate([dot(dprojected, attn_low, 0, 0).astype(low), out_local.astype(low)])
+        zero_partial = dot(dprojected, qkv_head).astype(low)
 
     resid_here = lax.dynamic_slice_in_dim(resid_low, device_index * rows_here, rows_here, 0)
     done_block = lax.dynamic_slice_in_dim(done_low, data_index * model_size, model_size, 0)
@@ -887,22 +1087,16 @@
         back, gain_grad = norm_back(unit, scale, gain, total)
         return ((extras[1][at] + back).astype(low), (), (gain_grad[None],))
 
-    dzero_low, attn_grad, head_parts = relay(
-        dot(dprojected, qkv_head).astype(low),
+    dzero_low, attn_grad = relay(
+        after(zero_partial, head_parts, hidden_parts),
         zero_step,
         7,
         extras=[resid_here.astype(jnp.float32), dresid_here, gain_rows],
         sums=1,
-        cargo=jnp.concatenate([qkv_local.astype(low), out_local.astype(low)]),
-    )
+    )
+    head_parts = swap_blocks(after(head_parts, dzero_low))
     table_grad = table_head + dot(id_hits, dzero_low, 0, 0)
 
-    gain_sums = jnp.sum(
-        gather_small(
-            jnp.concatenate([attn_grad, mlp_grad, final_grad]).reshape(-1, 128), 8
-        ).reshape(devices, 3, width),
-        axis=0,
-    )
     head_grad = jnp.sum(
         head_parts.reshape(heads_here, sharers, 4, HEAD_DIM, width_here).astype(jnp.float32), axis=1
     )
@@ -916,8 +1110,6 @@
         jnp.transpose(gate_up_grad, (3, 1, 0, 2)).reshape(gate_up_weight.shape), (0, 1, 2)
     )
     down_grad = hidden_parts[:, 2 * hidden_here :].reshape(down_weight.shape)
-    gain_grad = lax.dynamic_slice_in_dim(gain_sums, data_index * width_here, width_here, 1)
-
     squares = (
         jnp.sum(table_grad * table_grad)
         + jnp.sum(qkv_grad * qkv_grad)
@@ -925,8 +1117,16 @@
         + jnp.sum(gate_up_grad * gate_up_grad)
         + jnp.sum(down_grad * down_grad)
     )
-    square_parts = gather_small(jnp.full((8, 128), squares), 9)[:, 0, 0]
-    grad_norm = jnp.sqrt(jnp.sum(square_parts) + jnp.sum(gain_sums * gain_sums))
+    parts = jnp.concatenate(
+        [
+            jnp.concatenate([attn_grad, mlp_grad, final_grad]).reshape(-1, 128),
+            jnp.full((8, 128), squares),
+        ]
+    )
+    parts = jnp.sum(gather_small(parts, 8), axis=0)
+    gain_sums = parts[:-8].reshape(3, width)
+    gain_grad = lax.dynamic_slice_in_dim(gain_sums, data_index * width_here, width_here, 1)
+    grad_norm = jnp.sqrt(parts[-1, 0] + jnp.sum(gain_sums * gain_sums))
     factor = jnp.minimum(1.0, CLIP / (grad_norm + 1e-06))
     table_new = adam_update(
         table, table_first, table_second, table_grad * factor, RATE_MATRIX, DECAY

time: 810 us -> 735 us (0.907)
  the two profiles are of different devices: /device:TPU:0 before, /device:TPU:15 now
where the time goes in v3:
time: 735 us; the launch traced here: 725 us
  Pallas kernels  456 us (62%)
  other arithmetic  94.5 us (13%)
  matrix products  66.9 us (9%)
  local copies, waits for them, and re-layouts  55.6 us (8%)
  starting transfers between devices  22.3 us (3%)
  waiting for transfers between devices  22.2 us (3%)
  between operations  7.48 us (1%)
    pallas_call x6, Pallas kernels, relay(): pl.pallas_call(functools.partial(relay_kernel, plan, row_step), out_shape...  359 us
    dot_general x15, matrix products, dot(): lax.dot_general(left, right, (((left_dim,), (right_dim,)), ((), ())), pre...  64.8 us
    sub x6, other arithmetic, adam_update(): return (weight - rate * (ratio + decay * weight), moment_one, moment_two)  47.2 us
    pallas_call x2, Pallas kernels, gather_small(): pl.pallas_call(small_gather_kernel, out_shape=jax.ShapeDtypeStruct((32,)...  46.2 us
    pallas_call x1, Pallas kernels, attend_back(): pl.pallas_call(attend_back_kernel, out_shape=[jax.ShapeDtypeStruct((token...  23.6 us
    all_to_all x2, waiting for transfers between devices, swap_blocks(): return lax.all_to_all(parts, 'dp', split_axis=0, concat_axis=0, tiled=True)  22.2 us
    pallas_call x1, Pallas kernels, attend(): pl.pallas_call(attend_kernel, out_shape=outs, grid_spec=pltpu.PrefetchSca...  19.6 us
    unnamed x111, local copies, waits for them, and re-layouts  16 us
  transfers between devices with their start and end apart: 4, of which 2 were waited for; matrix products, arithmetic and copies ran while one was open for 13% of the time, Pallas kernels for 27%

profile of v3, /device:TPU:15, one launch (start us, length us, event | category | flops | bytes accessed | tf_op | source)
XLA Modules:
  0.0 724.6 jit_solution(4356267087429359082)
XLA Ops:
  5.4 6.8 shard_map.373
  13.7 5.7 all-to-all-start
  19.4 4.0 convert_element_type.116
  25.4 11.4 %fusion.5.refs_0_ = bf16[2048,2048]{1,0:T(8,128)(2,1)} fusion(bf16[1000,2048]{1,0:T(8,128)(2,1)S(1)} %convert_element_type.116, s32[1000]{0:T(1024)S(1)} %iota_add_fusion, s32[2048]{0:T(1024)S(1)} %bitcast.212), kind=kOutput, calls=%fused_computation.10 | convolution fusion | flops 8394850304 | bytes 12496800 | tf_op jit(solution)/shard_map/dot_general | solution.py:717
  36.8 93.8 %shard_map.374.resid_ref = bf16[2048,2048]{1,0:T(8,128)(2,1)} custom-call(bf16[2048,2048]{1,0:T(8,128)(2,1)} %fusion.5.refs_0_), custom_call_target="tpu_custom_call" | custom-call | flops 1 | bytes 1 | tf_op jit(solution)/shard_map/pallas_call | solution.py:321
  143.3 6.1 all-to-all-start.1
  156.1 3.7 fusion.30
  165.0 19.6 %shard_map.375 = (bf16[2048,2048]{1,0:T(8,128)(2,1)}, bf16[512,128]{1,0:T(8,128)(2,1)}, bf16[2048,128]{1,0:T(8,128)(2,1)}, bf16[2048,128]{1,0:T(8,128)(2,1)}, bf...) custom-call(s32[1]{0:T(128)} %bitcast.3.exit_ref, bf16[2048,2048]{1,0:T(8,128)(2,1)} %shard_map.374.resid_ref, ...), custom_call_target="tpu_custom_call" | custom-call | flops 1 | bytes 1 | tf_op jit(solution)/shard_map/pallas_call | solution.py:626
  184.6 56.3 %shard_map.376 = (bf16[1024,2048]{1,0:T(8,128)(2,1)}, f32[32,2048]{1,0:T(8,128)}) custom-call(bf16[1024,2048]{1,0:T(8,128)(2,1)} %bitcast.173, f32[32,2048]{1,0:T(8,128)} %fusion.24.refs_1_, f32[3,2048]{1,0:T(4,128)} %bitcast.187), custom_call_target="tpu_custom_call" | custom-call | flops 1 | bytes 1 | tf_op jit(solution)/shard_map/pallas_call | solution.py:321
  241.0 4.2 fusion.57
  246.5 3.7 fusion.63
  256.6 38.5 %shard_map.377 = (bf16[512,2048]{1,0:T(8,128)(2,1)}, f32[16,2048]{1,0:T(8,128)}) custom-call(bf16[512,2048]{1,0:T(8,128)(2,1)} %convolution_convert_fusion.2.refs_0_, f32[32,2048]{1,0:T(8,128)} %get-tuple-element.53.refs_1_.refs_2_, f32[3,2048]{1,0:T(4,128)} %bitcast.188), custom_call_target="tpu_custom_call" | custom-call | flops 1 | bytes 1 | tf_op jit(solution)/shard_map/pallas_call | solution.py:321
  295.1 4.1 fusion.64
  303.7 16.2 %shard_map.378 = f32[32,24,128]{2,1,0:T(8,128)} custom-call(f32[24,128]{1,0:T(8,128)} %concatenate.63.x_ref), custom_call_target="tpu_custom_call" | custom-call | tf_op jit(solution)/shard_map/pallas_call | solution.py:381
  322.0 5.6 convolution_convert_fusion
  332.8 43.3 %shard_map.379 = (bf16[512,2048]{1,0:T(8,128)(2,1)}, f32[32,2048]{1,0:T(8,128)}, f32[1,2048]{1,0:T(1,128)}) custom-call(bf16[1024,2048]{1,0:T(8,128)(2,1)} %bitcast.156, f32[32,2048]{1,0:T(8,128)} %get-tuple-element.53.refs_1_.refs_2_, f32[16,2048]{1,0:T(8,128)} %get-tuple-element.55.refs_2_, f32[3,2048]{1,0:T(4,128)} %bitcast.189), custom_call_target="tpu_custom_call" | custom-call | flops 1 | bytes 1 | tf_op jit(solution)/shard_map/pallas_call | solution.py:321
  384.5 40.9 %shard_map.380 = (bf16[1024,2048]{1,0:T(8,128)(2,1)}, f32[1,2048]{1,0:T(1,128)}) custom-call(bf16[512,2048]{1,0:T(8,128)(2,1)} %convolution_convert_fusion.3.refs_0_, bf16[16,2048]{1,0:T(8,128)(2,1)} %slice.187.refs_1_, f32[32,2048]{1,0:T(8,128)} %get-tuple-element.53.refs_1_.refs_2_, f32[32,2048]{1,0:T(8,128)} %get-tuple-element.57.refs_3_, f32[3,2048]{1,0:T(4,128)} %bitcast.190), custom_call_target="tpu_custom_call" | custom-call | flops 1 | bytes 1 | tf_op jit(solution)/shard_map/pallas_call | solution.py:321
  427.1 4.4 all-to-all-start.2
  436.1 23.6 %shard_map.381 = (bf16[2048,2048]{1,0:T(8,128)(2,1)}, bf16[512,2048]{1,0:T(8,128)(2,1)}) custom-call(s32[1]{0:T(128)} %bitcast.3.exit_ref, bf16[32,2,16,2048]{3,2,1,0:T(8,128)(2,1)} %bitcast.171, bf16[512,2048]{1,0:T(8,128)(2,1)} %bitcast.155, bf16[512,128]{1,0:T(8,128)(2,1)} %get-tuple-element.59.out_ref, bf16[512,128]{1,0:T(8,128)(2,1)} %get-tuple-element.60.query_ref, ...), custom_call_target="tpu_custom_call" | custom-call | flops 1 | bytes 1 | tf_op jit(solution)/shard_map/pallas_call | solution.py:657
  461.8 8.1 %fusion.46 = f32[1000,2048]{1,0:T(8,128)} fusion(bf16[512,2048]{1,0:T(8,128)(2,1)} %bitcast.182, f32[512,1000]{0,1:T(8,128)} %get-tuple-element.128, f32[512]{0:T(512)S(1)} %bitcast.202, f32[512]{0:T(512)S(1)} %bitcast.200, s32[512]{0:T(512)S(1)} %eq.76, s32[1000]{0:T(1024)S(1)} %iota_add_fusion), kind=kOutput, calls=%fused_computation.139 | convolution fusion | flops 2100224000 | bytes 12347296 | tf_op jit(solution)/shard_map/dot_general | solution.py:717
  469.9 8.7 %all-to-all-done.2 = bf16[8,528,256]{2,1,0:T(8,128)(2,1)S(1)} async-done(((bf16[8,528,256]{2,1,0:T(8,128)(2,1)}), bf16[8,528,256]{2,1,0:T(8,128)(2,1)S(1)}, u32[]{:S(2)}, u32[]{:S(2)}) %all-to-all-start.2) | async-done | bytes 2162720 | tf_op jit(solution)/shard_map/all_to_all | solution.py:342
  478.6 86.7 %shard_map.382 = (bf16[2048,2048]{1,0:T(8,128)(2,1)}, f32[1,2048]{1,0:T(1,128)}) custom-call(bf16[2048,2048]{1,0:T(8,128)(2,1)} %get-tuple-element.67.refs_0_, f32[64,2048]{1,0:T(8,128)} %dynamic-slice_convert_fusion.refs_1_, f32[64,2048]{1,0:T(8,128)} %convolution_bitcast_fusion.refs_2_, f32[3,2048]{1,0:T(4,128)} %bitcast.191), custom_call_target="tpu_custom_call" | custom-call | flops 1 | bytes 1 | tf_op jit(solution)/shard_map/pallas_call | solution.py:321
  569.1 6.2 all-to-all-start.3
  577.4 4.3 copy.161
  590.3 11.5 %fusion = f32[1000,2048]{1,0:T(8,128)S(1)} fusion(bf16[2048,2048]{1,0:T(8,128)(2,1)} %get-tuple-element.71, s32[1000]{0:T(1024)S(1)} %iota_add_fusion, s32[2048]{0:T(1024)S(1)} %bitcast.213), kind=kOutput, calls=%fused_computation.1 | convolution fusion | flops 8390656000 | bytes 16592800 | tf_op jit(solution)/shard_map/dot_general | solution.py:717
  601.8 5.8 multiply_reduce_fusion
  607.6 13.4 %all-to-all-done.3 = bf16[8,512,256]{2,1,0:T(8,128)(2,1)} async-done(((bf16[8,512,256]{2,1,0:T(8,128)(2,1)}), bf16[8,512,256]{2,1,0:T(8,128)(2,1)}, u32[]{:S(2)}, u32[]{:S(2)}) %all-to-all-start.3) | async-done | bytes 2097184 | tf_op jit(solution)/shard_map/all_to_all | solution.py:342
  637.5 30.0 %shard_map.383 = f32[32,56,128]{2,1,0:T(8,128)} custom-call(f32[56,128]{1,0:T(8,128)} %concatenate.69.x_ref), custom_call_target="tpu_custom_call" | custom-call | tf_op jit(solution)/shard_map/pallas_call | solution.py:381
  675.0 6.1 multiply_subtract_fusion.2
  682.1 10.9 %multiply_subtract_fusion.1 = (f32[256,2,1408]{2,1,0:T(2,128)}, f32[256,2,1408]{2,1,0:T(2,128)}, f32[256,2,1408]{2,1,0:T(2,128)}) fusion(f32[256,2,1408]{2,1,0:T(2,128)S(1)} %copy-done.9, f32[256,2,1408]{2,1,0:T(2,128)S(1)} %copy.161, f32[]{:T(128)S(6)} %min.3, f32[256,2,1408]{2,1,0:T(2,128)S(1)} %copy-done.18, f32[256,2,1408]{2,1,0:T(2,128)S(1)} %copy-done.19), kind=kLoop, calls=%fused_computation.23 | loop fusion | flops 11534336 | bytes 20185092 | tf_op jit(solution)/shard_map/sub | solution.py:734
  693.0 22.6 %multiply_subtract_fusion = (f32[1000,2048]{1,0:T(8,128)}, f32[1000,2048]{1,0:T(8,128)}, f32[1000,2048]{1,0:T(8,128)}) fusion(f32[1000,2048]{1,0:T(8,128)} %param.25, f32[1000,2048]{1,0:T(8,128)} %get-tuple-element.132, f32[]{:T(128)S(6)} %min.3, f32[1000,2048]{1,0:T(8,128)} %param.26, f32[1000,2048]{1,0:T(8,128)} %param.27), kind=kLoop, calls=%fused_computation.6 | loop fusion | flops 32768000 | bytes 57344004 | tf_op jit(solution)/shard_map/sub | solution.py:734
  718.4 4.3 multiply_subtract_fusion.3
  (216 shorter events, 106.8 us)
Async XLA Ops:
  13.7 5.7 copy-start.35
  13.7 129.6 %all-to-all-start = ((bf16[8,512,256]{2,1,0:T(8,128)(2,1)}), bf16[8,512,256]{2,1,0:T(8,128)(2,1)}, u32[]{:S(2)}, u32[]{:S(2)}) async-start(bf16[8,512,256]{2,1,0:T(8,128)(2,1)} %bitcast.11), calls=%async_computation | async-start | bytes 4194304 | tf_op jit(solution)/shard_map/all_to_all | solution.py:339
  36.8 98.8 %copy-start.8 = (f32[256,2,1408]{2,1,0:T(2,128)S(1)}, f32[256,2,1408]{2,1,0:T(2,128)}, u32[]{:S(2)}) copy-start(f32[256,2,1408]{2,1,0:T(2,128)} %param.34) | copy-start | bytes 8650756
  141.9 9.8 %copy-start.49 = (f32[2]{0:T(128)}, f32[2]{0:T(128)S(1)}, u32[]{:S(2)}) copy-start(f32[2]{0:T(128)S(1)} %convert_reduce_fusion.1) | copy-start | bytes 28
  143.3 8.4 %copy-start.50 = (f32[2]{0:T(128)S(1)}, f32[2]{0:T(128)}, u32[]{:S(2)}) copy-start(f32[2]{0:T(128)} %constant.158.clone) | copy-start | bytes 28
  143.3 106.9 %all-to-all-start.1 = ((bf16[8,528,256]{2,1,0:T(8,128)(2,1)}), bf16[8,528,256]{2,1,0:T(8,128)(2,1)S(1)}, u32[]{:S(2)}, u32[]{:S(2)}) async-start(bf16[8,528,256]{2,1,0:T(8,128)(2,1)} %pad_maximum_fusion.1), calls=%async_computation.1 | async-start | bytes 4325376 | tf_op jit(solution)/shard_map/all_to_all | solution.py:339
  152.9 7.0 copy-start.45
  153.1 6.8 copy-start.31
  241.0 5.6 copy-start.1
  254.5 40.6 %copy-start.2 = (bf16[1000,2048]{1,0:T(8,128)(2,1)S(1)}, bf16[1000,2048]{1,0:T(8,128)(2,1)}, u32[]{:S(2)}) copy-start(bf16[1000,2048]{1,0:T(8,128)(2,1)} %copy-done) | copy-start | bytes 12288004
  295.1 5.4 copy-start.11
  322.0 5.6 copy-start.3
  322.0 5.6 copy-start.12
  332.8 43.3 %copy-start.16 = (bf16[8,22,8,256]{3,2,0,1:T(8,128)(2,1)S(1)}, bf16[8,22,8,256]{3,2,0,1:T(8,128)(2,1)}, u32[]{:S(2)}) copy-start(bf16[8,22,8,256]{3,2,0,1:T(8,128)(2,1)} %copy-done.15) | copy-start | bytes 2162692
  332.8 43.3 %copy-start.33 = (f32[512,352]{0,1:T(8,128)S(1)}, f32[512,352]{0,1:T(8,128)}, u32[]{:S(2)}) copy-start(f32[512,352]{0,1:T(8,128)} %copy-done.32) | copy-start | bytes 2162692
  427.1 5.2 copy-start.37
  427.1 5.2 copy-start.46
  427.1 51.5 %all-to-all-start.2 = ((bf16[8,528,256]{2,1,0:T(8,128)(2,1)}), bf16[8,528,256]{2,1,0:T(8,128)(2,1)S(1)}, u32[]{:S(2)}, u32[]{:S(2)}) async-start(bf16[8,528,256]{2,1,0:T(8,128)(2,1)} %bitcast.161), calls=%async_computation.2 | async-start | bytes 4325376 | tf_op jit(solution)/shard_map/all_to_all | solution.py:342
  478.6 96.7 %copy-start.4 = (bf16[8,528,256]{2,1,0:T(8,128)(2,1)}, bf16[8,528,256]{2,1,0:T(8,128)(2,1)S(1)}, u32[]{:S(2)}) copy-start(bf16[8,528,256]{2,1,0:T(8,128)(2,1)S(1)} %all-to-all-done.2) | copy-start | bytes 6488068
  478.6 86.7 %copy-start.38 = (f32[1,2048]{1,0:T(1,128)S(1)}, f32[1,2048]{1,0:T(1,128)}, u32[]{:S(2)}) copy-start(f32[1,2048]{1,0:T(1,128)} %get-tuple-element.70) | copy-start | bytes 24580
  478.6 86.7 %copy-start.39 = (f32[1,2048]{1,0:T(1,128)S(1)}, f32[1,2048]{1,0:T(1,128)}, u32[]{:S(2)}) copy-start(f32[1,2048]{1,0:T(1,128)} %get-tuple-element.69) | copy-start | bytes 24580
  569.1 51.9 %all-to-all-start.3 = ((bf16[8,512,256]{2,1,0:T(8,128)(2,1)}), bf16[8,512,256]{2,1,0:T(8,128)(2,1)}, u32[]{:S(2)}, u32[]{:S(2)}) async-start(bf16[8,512,256]{2,1,0:T(8,128)(2,1)} %bitcast.163), calls=%async_computation.3 | async-start | bytes 4194304 | tf_op jit(solution)/shard_map/all_to_all | solution.py:342
  586.7 15.0 %slice-start = ((s8[8192000]{0:T(1024)(128)(4,1)}), s8[4194304]{0:T(1024)(128)(4,1)S(1)}, s32[]{:S(2)}) async-start(s8[8192000]{0:T(1024)(128)(4,1)} %bitcast.166), calls=%async_computation.4 | async-start | bytes 8388608
  590.3 11.5 %copy-start.6 = (f32[512,1000]{0,1:T(8,128)S(1)}, f32[512,1000]{0,1:T(8,128)}, u32[]{:S(2)}) copy-start(f32[512,1000]{0,1:T(8,128)} %copy-done.5) | copy-start | bytes 6144004
  590.3 11.5 %slice-start.1 = ((s8[8192000]{0:T(1024)(128)(4,1)}), s8[3997696]{0:T(1024)(128)(4,1)S(1)}, s32[]{:S(2)}) async-start(s8[8192000]{0:T(1024)(128)(4,1)} %bitcast.166), calls=%async_computation.5 | async-start | bytes 7995392
  590.3 11.5 %copy-start.25 = (bf16[512,2048]{1,0:T(8,128)(2,1)S(1)}, bf16[512,2048]{1,0:T(8,128)(2,1)}, u32[]{:S(2)}) copy-start(bf16[512,2048]{1,0:T(8,128)(2,1)} %get-tuple-element.54) | copy-start | bytes 6291460
  675.0 6.2 copy-start.9
  675.0 6.1 copy-start.18
  675.0 7.1 copy-start.19
  693.0 22.7 %copy-start.20 = (f32[512,256]{1,0:T(8,128)S(1)}, f32[512,256]{1,0:T(8,128)}, u32[]{:S(2)}) copy-start(f32[512,256]{1,0:T(8,128)} %param.31) | copy-start | bytes 1572868
  693.0 22.7 %copy-start.34 = (f32[512,256]{1,0:T(8,128)S(1)}, f32[512,256]{1,0:T(8,128)}, u32[]{:S(2)}) copy-start(f32[512,256]{1,0:T(8,128)} %param.32) | copy-start | bytes 1572868
  693.0 25.3 %copy-start.28 = (f32[1408,256]{1,0:T(8,128)S(1)}, f32[1408,256]{1,0:T(8,128)}, u32[]{:S(2)}) copy-start(f32[1408,256]{1,0:T(8,128)} %param.38) | copy-start | bytes 4325380
  (25 other events, 66.4 us)

commit v4 on v3

--- a/solution.py
+++ b/solution.py
@@ -5,7 +5,6 @@
 import jax.numpy as jnp
 from jax import lax
 from jax.experimental import pallas as pl
-from jax.experimental.layout import Layout, with_layout_constraint
 from jax.experimental.pallas import tpu as pltpu
 from jax.sharding import PartitionSpec as P
 
@@ -29,6 +28,9 @@
 VMEM_LIMIT = 60 * 1024 * 1024
 ANY = pl.BlockSpec(memory_space=pl.ANY)
 GROUP = 16
+CARGO_CUTS = 2
+CARGO_EARLY = 4
+CARGO_LATE = 2
 
 
 def kernel_mesh():
@@ -42,7 +44,7 @@
 
 
 class Links:
-    def __init__(self, send_sem, recv_sem):
+    def __init__(self, send_sem, recv_sem, cargo=False):
         data_index, model_index = lax.axis_index("dp"), lax.axis_index("mp")
         z, y, x, c = data_index // 2, data_index % 2, model_index // 2, model_index % 2
         self.c = c
@@ -54,6 +56,8 @@
         self.c_side = (data_index, x * 2 + 1 - c)
         self.send_sem, self.recv_sem, self.sent, self.slots = send_sem, recv_sem, [], {}
         peers = self.z_side[1:] + [self.x_side, self.y_side, self.c_side]
+        if cargo:
+            peers += [(zd * 2 + 1 - y, model_index) for zd in self.zs[1:]]
         barrier = pltpu.get_barrier_semaphore()
         for peer in peers:
             pl.semaphore_signal(barrier, inc=1, device_id=peer, device_id_type=MESH)
@@ -88,15 +92,57 @@
             copy.wait_send()
 
 
+class Cargo:
+    def __init__(self, source, target, send_sem, recv_sem, own_sem):
+        self.me, self.model_index = lax.axis_index("dp"), lax.axis_index("mp")
+        self.source, self.target = source, target
+        self.send_sem, self.recv_sem, self.sent = send_sem, recv_sem, []
+        self.own = pltpu.make_async_copy(source.at[self.me], target.at[self.me], own_sem)
+        self.own.start()
+        size = source.shape[1] // CARGO_CUTS
+        cuts = [pl.ds(cut * size, size) for cut in range(CARGO_CUTS)]
+        self.cuts = [(shift, cut) for cut in cuts for shift in (4, 3, 5, 2, 6, 1, 7)]
+
+    def load(self, count):
+        for _ in range(count):
+            index = len(self.sent)
+            if index == len(self.cuts):
+                return
+            shift, cut = self.cuts[index]
+            peer = lax.rem(self.me + shift, 8)
+            copy = pltpu.make_async_remote_copy(
+                src_ref=self.source.at[peer, cut],
+                dst_ref=self.target.at[self.me, cut],
+                send_sem=self.send_sem.at[index],
+                recv_sem=self.recv_sem.at[index],
+                device_id=(peer, self.model_index),
+                device_id_type=MESH,
+            )
+            copy.start()
+            self.sent.append(copy)
+
+    def finish(self):
+        self.load(len(self.cuts))
+        self.own.wait()
+        for index, (shift, cut) in enumerate(self.cuts):
+            here = self.target.at[lax.rem(self.me + 8 - shift, 8), cut]
+            pltpu.make_async_copy(here, here, self.recv_sem.at[index]).wait()
+        for copy in self.sent:
+            copy.wait_send()
+
+
 class Gather:
-    def __init__(self, link, out, steps, own_sem):
-        self.link, self.out, self.steps, self.own_sem = link, out, steps, own_sem
+    def __init__(self, link, outs, steps, own_sem):
+        self.link, self.outs, self.steps, self.own_sem = link, outs, steps, own_sem
         self.owns = []
 
     def spot(self, g, d, group, core=0):
-        rows = self.steps * GROUP
-        start = self.link.first_row(rows, d, group, core) + g * GROUP
-        return self.out.at[pl.ds(pl.multiple_of(start, GROUP), GROUP)]
+        if len(self.outs) > 1:
+            out, start = self.outs[g], self.link.first_row(GROUP, d, group, core)
+        else:
+            out, start = self.outs[0], self.link.first_row(self.steps * GROUP, d, group, core)
+            start = start + g * GROUP
+        return out.at[pl.ds(pl.multiple_of(start, GROUP), GROUP)]
 
     def send(self, g, source, device, here, there):
         self.link.send(source, self.spot(g, *here), device, ("gather", g, *there))
@@ -158,8 +204,8 @@
 
 
 class Scatter:
-    def __init__(self, link, partial, rows, order, buffers, own_sem):
-        self.link, self.partial, self.rows = link, partial, rows
+    def __init__(self, link, partials, rows, order, buffers, own_sem):
+        self.link, self.partials, self.rows = link, partials, rows
         self.mine, self.core, self.corner, self.side, self.column = buffers
         self.owns = {}
         for p in order:
@@ -172,8 +218,12 @@
                 self.send(p, self.spot(p, d, group, 1), self.core, k, link.c_side, "core")
 
     def spot(self, p, d, group, core=0):
-        start = self.link.first_row(self.rows, d, group, core) + p * GROUP
-        return self.partial.at[pl.ds(pl.multiple_of(start, GROUP), GROUP)]
+        if len(self.partials) > 1:
+            partial, start = self.partials[p], self.link.first_row(GROUP, d, group, core)
+        else:
+            partial, start = self.partials[0], self.link.first_row(self.rows, d, group, core)
+            start = start + p * GROUP
+        return partial.at[pl.ds(pl.multiple_of(start, GROUP), GROUP)]
 
     def send(self, p, source, buffer, k, device, name):
         self.link.send(source, buffer.at[k, pl.ds(p * GROUP, GROUP)], device, (name, p, k))
@@ -234,20 +284,23 @@
         del refs[:count]
         return taken
 
-    (partial,) = take(1)
+    partials = take(plan["partials"])
     ready = take(plan["ready"])
     extras = take(plan["extras"])
-    (gathered,) = take(1)
+    cargo_in = take(plan["cargo"])
+    gathered = take(plan["outs"])
     kept = take(plan["kept"])
     sums = take(plan["sums"])
+    cargo_out = take(plan["cargo"])
     buffers = take(5)
     held, send_sem, recv_sem, load_sem, own_sem = take(5)
     order, steps = plan["order"], plan["steps"]
-    link = Links(send_sem, recv_sem)
+    link = Links(send_sem, recv_sem, plan["cargo"])
     gather = Gather(link, gathered, steps, own_sem)
     if ready:
         gather.begin(0, ready[0])
-    scatter = Scatter(link, partial, plan["rows"], order, buffers, load_sem)
+    scatter = Scatter(link, partials, plan["rows"], order, buffers, load_sem)
+    cargo = Cargo(*cargo_in, *cargo_out, *refs) if cargo_in else None
     ticks = len(order) + 7
     agenda = [[] for _ in range(ticks)]
     if ready:
@@ -273,21 +326,40 @@
         if plan["slot"](p) is not None:
             for tick, step in enumerate((gather.first, gather.second, gather.third)):
                 agenda[q + 4 + tick].append((step, plan["slot"](p)))
-    for tick in agenda:
+    for number, tick in enumerate(agenda):
+        if cargo:
+            cargo.load(CARGO_EARLY if number < 4 else CARGO_LATE)
         for step, index in tick:
             step(index)
     gather.finish()
     link.finish()
-
-
-def relay(partial, row_step, ident, extras=(), kept=0, sums=0, order=None, slot=None, ready=None):
-    rows, width = partial.shape[0] // (lax.axis_size("dp") * lax.axis_size("mp")), partial.shape[1]
+    if cargo:
+        cargo.finish()
+
+
+def relay(
+    partials,
+    row_step,
+    ident,
+    extras=(),
+    kept=0,
+    sums=0,
+    order=None,
+    slot=None,
+    ready=None,
+    split=False,
+    cargo=None,
+):
+    devices, width = lax.axis_size("dp") * lax.axis_size("mp"), partials[0].shape[1]
+    rows = sum(partial.shape[0] for partial in partials) // devices
     groups = rows // GROUP
     order = list(range(groups)) if order is None else order
     slot = slot or (lambda p: p)
     steps = sum(slot(p) is not None for p in order) + (ready is not None)
     if not kernel_mesh():
-        total = lax.psum_scatter(partial, BOTH, scatter_dimension=0, tiled=True)
+        total = jnp.concatenate(
+            [lax.psum_scatter(part, BOTH, scatter_dimension=0, tiled=True) for part in partials]
+        )
         total = total.astype(jnp.float32)
         outs, keeps, adds = [None] * steps, [None] * groups, [0.0] * sums
         if ready is not None:
@@ -297,10 +369,15 @@
             adds = [one + two for one, two in zip(adds, add)]
             if out is not None:
                 outs[slot(p)] = out
-        gathered = lax.all_gather(jnp.concatenate(outs), BOTH, axis=0, tiled=True)
+        outs = outs if split else [jnp.concatenate(outs)]
+        gathered = [lax.all_gather(out, BOTH, axis=0, tiled=True) for out in outs]
         keeps = [jnp.concatenate(parts) for parts in zip(*keeps)]
-        return [gathered, *keeps, *adds]
+        moved = [] if cargo is None else [swap_blocks(cargo)]
+        return [*gathered, *keeps, *adds, *moved]
     plan = dict(
+        partials=len(partials),
+        outs=steps if split else 1,
+        cargo=int(cargo is not None),
         rows=rows,
         order=order,
         slot=slot,
@@ -310,23 +387,30 @@
         kept=kept,
         sums=sums,
     )
-    low = partial.dtype
+    low = partials[0].dtype
+    load = [] if cargo is None else [cargo]
     vmem = pl.BlockSpec(memory_space=pltpu.VMEM)
     copies = 31 * (groups + steps)
-    shapes = [jax.ShapeDtypeStruct((32 * steps * GROUP, width), low)]
+    out_rows = [devices * GROUP] * steps if split else [devices * steps * GROUP]
+    shapes = [jax.ShapeDtypeStruct((count, width), low) for count in out_rows]
     shapes += [jax.ShapeDtypeStruct((rows, width), jnp.float32)] * kept
     shapes += [jax.ShapeDtypeStruct((1, width), jnp.float32)] * sums
+    shapes += [jax.ShapeDtypeStruct(value.shape, value.dtype) for value in load]
     buffers = [pltpu.VMEM((count, rows, width), low) for count in (16, 16, 4, 8, 3)]
     semaphores = [pltpu.SemaphoreType.DMA((count,)) for count in (copies, copies, 16 * groups, steps)]
+    if load:
+        semaphores += [pltpu.SemaphoreType.DMA((7 * CARGO_CUTS,))] * 2 + [pltpu.SemaphoreType.DMA]
     return pl.pallas_call(
         functools.partial(relay_kernel, plan, row_step),
         out_shape=shapes,
-        in_specs=[ANY] * (1 + plan["ready"]) + [vmem] * len(extras),
-        out_specs=[ANY] + [vmem] * (kept + sums),
+        in_specs=[ANY] * (len(partials) + plan["ready"])
+        + [vmem] * len(extras)
+        + [ANY] * len(load),
+        out_specs=[ANY] * len(out_rows) + [vmem] * (kept + sums) + [ANY] * len(load),
         scratch_shapes=buffers + [pltpu.VMEM((steps, GROUP, width), low)] + semaphores,
         compiler_params=comm_params(ident),
         cost_estimate=pl.CostEstimate(flops=1, bytes_accessed=1, transcendentals=0),
-    )(partial, *([] if ready is None else [ready]), *extras)
+    )(*partials, *([] if ready is None else [ready]), *extras, *load)
 
 
 def after(value, *first):
@@ -334,12 +418,7 @@
 
 
 def swap_blocks(value):
-    count = lax.axis_size("dp")
-    if len(value.shape) == 3:
-        moved = lax.all_to_all(value, "dp", split_axis=0, concat_axis=0, tiled=True)
-        return jnp.moveaxis(moved, 0, 1).reshape(value.shape[1], -1)
-    parts = jnp.moveaxis(value.reshape(value.shape[0], count, -1), 1, 0)
-    return lax.all_to_all(parts, "dp", split_axis=0, concat_axis=0, tiled=True)
+    return lax.all_to_all(value, "dp", split_axis=0, concat_axis=0, tiled=True)
 
 
 def small_gather_kernel(x_ref, o_ref, send_sem, recv_sem, own_sem):
@@ -465,6 +544,14 @@
     return values * cosine + pltpu.roll(values, HEAD_DIM // 2, 1) * sine_table
 
 
+def to_column(row):
+    return jnp.broadcast_to(row, (row.shape[1], row.shape[1])).T[:, :1]
+
+
+def to_row(column):
+    return jnp.broadcast_to(column, (column.shape[0], column.shape[0])).T[:1]
+
+
 def softmax_rows(query, keys, places):
     scores = dot(query, keys, 1, 1) * (1.0 / math.sqrt(HEAD_DIM))
     columns = lax.broadcasted_iota(jnp.int32, scores.shape, 1)
@@ -478,8 +565,8 @@
     resid_ref,
     gain_ref,
     head_ref,
-    cosine_ref,
-    sine_ref,
+    inner_ref,
+    outer_ref,
     pick_ref,
     place_ref,
     live_ref,
@@ -488,21 +575,37 @@
     key_ref,
     value_ref,
     out_ref,
+    turn_ref,
+    slot_turn_ref,
     partial_ref,
 ):
     block, blocks = pl.program_id(0), key_ref.shape[0] // resid_ref.shape[0]
     rows, slots = resid_ref.shape[0], pick_ref.shape[1]
+    parts, columns = head_ref.shape[0], head_ref.shape[2]
     low = jnp.bfloat16
     attn = norm_fwd(resid_ref[...].astype(jnp.float32), gain_ref[...])[0].astype(low)
     attn_ref[...] = attn
-    projected = dot(attn, head_ref[: 3 * HEAD_DIM], 1, 1)
-    cosine, sine_table = cosine_ref[...], sine_ref[...]
+    projected = jnp.zeros((rows, 3 * HEAD_DIM), jnp.float32)
+    for part in range(parts):
+        piece = attn[:, part * columns : (part + 1) * columns]
+        projected = projected + dot(piece, head_ref[part, : 3 * HEAD_DIM], 1, 1)
+    inner_cos, inner_sin = inner_ref[0], inner_ref[1]
+    outer_cos, outer_sin = outer_ref[0, pl.ds(block, 1)], outer_ref[1, pl.ds(block, 1)]
+    sign = jnp.where(lax.broadcasted_iota(jnp.int32, inner_cos.shape, 1) < HEAD_DIM // 2, -1.0, 1.0)
+    cosine = inner_cos * outer_cos - inner_sin * outer_sin
+    sine_table = (inner_sin * outer_cos + inner_cos * outer_sin) * sign
+    at = pl.ds(pl.multiple_of(block * rows, rows), rows)
+    turn_ref[0, at], turn_ref[1, at] = cosine, sine_table
     query = turned(projected[:, :HEAD_DIM], cosine, sine_table).astype(low)
-    at = pl.ds(pl.multiple_of(block * rows, rows), rows)
     key_ref[at] = turned(projected[:, HEAD_DIM : 2 * HEAD_DIM], cosine, sine_table).astype(low)
     value_ref[at] = projected[:, 2 * HEAD_DIM :].astype(low)
     at = pl.ds(pl.multiple_of(block * slots, slots), slots)
     query_ref[at] = dot(pick_ref[0], query).astype(low)
+    pick_wide = pick_ref[0].astype(jnp.float32)
+    for index, table in enumerate((cosine, sine_table)):
+        slot_turn_ref[index, at] = jnp.dot(
+            pick_wide, table, precision=lax.Precision.HIGHEST, preferred_element_type=jnp.float32
+        )
 
     @pl.when(block == blocks - 1)
     def _():
@@ -511,15 +614,19 @@
         for index in range(blocks // 2):
             reach = (index + 1) * 2 * rows
             at = slice(index * step, (index + 1) * step)
-            probs = softmax_rows(query_ref[at], key_ref[:reach], place_ref[at]).astype(low)
-            out = (dot(probs, value_ref[:reach]) * live_ref[at]).astype(low)
+            row = slice(index, index + 1)
+            places, live = to_column(place_ref[row]), to_column(live_ref[row])
+            probs = softmax_rows(query_ref[at], key_ref[:reach], places).astype(low)
+            out = (dot(probs, value_ref[:reach]) * live).astype(low)
             out_ref[at] = out
-            share = dot(out, head_ref[3 * HEAD_DIM :]).astype(low)
             groups = step // partial_ref.shape[2]
             at = slice(index * groups, (index + 1) * groups)
-            share = share.reshape(groups, 1, -1, share.shape[1])
-            partial_ref[at, pl.ds(exit_here, 1)] = share
-            partial_ref[at, pl.ds(1 - exit_here, 1)] = jnp.zeros_like(share)
+            for part in range(parts):
+                share = dot(out, head_ref[part, 3 * HEAD_DIM :]).astype(low)
+                share = share.reshape(groups, 1, -1, columns)
+                lanes = slice(part * columns, (part + 1) * columns)
+                partial_ref[at, pl.ds(exit_here, 1), :, lanes] = share
+                partial_ref[at, pl.ds(1 - exit_here, 1), :, lanes] = jnp.zeros_like(share)
 
 
 def attend_back_kernel(
@@ -530,10 +637,8 @@
     query_ref,
     key_ref,
     value_ref,
-    cosine_ref,
-    sine_ref,
-    slot_cosine_ref,
-    slot_sine_ref,
+    turn_ref,
+    slot_turn_ref,
     pick_ref,
     place_ref,
     attn_ref,
@@ -546,6 +651,7 @@
 ):
     block, blocks = pl.program_id(0), key_ref.shape[0] // attn_ref.shape[0]
     rows, slots = attn_ref.shape[0], pick_ref.shape[1]
+    parts, columns = head_ref.shape[0], head_ref.shape[2]
     low = jnp.bfloat16
     scale = 1.0 / math.sqrt(HEAD_DIM)
 
@@ -556,17 +662,22 @@
         step = 2 * slots
         width = done_ref.shape[-1]
         done = done_ref[...].reshape(-1, width)
-        parts_ref[3 * HEAD_DIM :] = dot(out_ref[...], done, 0, 0).astype(low)
-        dout = dot(done, head_ref[3 * HEAD_DIM :], 1, 1).astype(low)
+        dout = jnp.zeros((done.shape[0], HEAD_DIM), jnp.float32)
+        for part in range(parts):
+            piece = done[:, part * columns : (part + 1) * columns]
+            parts_ref[part, 3 * HEAD_DIM :] = dot(out_ref[...], piece, 0, 0).astype(low)
+            dout = dout + dot(piece, head_ref[part, 3 * HEAD_DIM :], 1, 1)
+        dout = dout.astype(low)
         for index in range(blocks // 2):
             reach = (index + 1) * 2 * rows
             at = slice(index * step, (index + 1) * step)
-            probs = softmax_rows(query_ref[at], key_ref[:reach], place_ref[at])
+            places = to_column(place_ref[index : index + 1])
+            probs = softmax_rows(query_ref[at], key_ref[:reach], places)
             dprobs = dot(dout[at], value_ref[:reach], 1, 1)
             delta = jnp.sum(probs * dprobs, axis=-1, keepdims=True)
             dscores = (probs * (dprobs - delta)).astype(low)
             dquery = dot(dscores, key_ref[:reach]) * scale
-            dquery = turned(dquery, slot_cosine_ref[at], -slot_sine_ref[at]).astype(low)
+            dquery = turned(dquery, slot_turn_ref[0, at], -slot_turn_ref[1, at]).astype(low)
             for half in (0, 1):
                 where = 2 * index + half
                 turned_ref[where * rows : (where + 1) * rows, :HEAD_DIM] = dot(
@@ -574,13 +685,15 @@
                 ).astype(low)
             key_sum[:reach] += dot(dscores, query_ref[at], 0, 0)
             value_sum[:reach] += dot(probs.astype(low), dout[at], 0, 0)
-        dkey = turned(key_sum[...] * scale, cosine_ref[...], -sine_ref[...])
+        dkey = turned(key_sum[...] * scale, turn_ref[0], -turn_ref[1])
         turned_ref[:, HEAD_DIM : 2 * HEAD_DIM] = dkey.astype(low)
         turned_ref[:, 2 * HEAD_DIM :] = value_sum[...].astype(low)
 
     at = pl.ds(pl.multiple_of(block * rows, rows), rows)
     dprojected = turned_ref[at]
-    partial_ref[...] = dot(dprojected, head_ref[: 3 * HEAD_DIM]).astype(low)
+    for part in range(parts):
+        lanes = slice(part * columns, (part + 1) * columns)
+        partial_ref[:, lanes] = dot(dprojected, head_ref[part, : 3 * HEAD_DIM]).astype(low)
     term = dot(dprojected, attn_ref[...], 0, 0)
 
     @pl.when(block == 0)
@@ -593,7 +706,9 @@
 
     @pl.when(block == blocks - 1)
     def _():
-        parts_ref[: 3 * HEAD_DIM] = head_sum[...].astype(low)
+        for part in range(parts):
+            lanes = slice(part * columns, (part + 1) * columns)
+            parts_ref[part, : 3 * HEAD_DIM] = head_sum[:, lanes].astype(low)
 
 
 def local_params():
@@ -607,21 +722,20 @@
     return pl.BlockSpec(value.shape, lambda b, e: (0,) * len(value.shape))
 
 
-def attend(exit_here, resid, gain, head, cosine, sine_table, pick, places, live, slots_here):
+def attend(exit_here, resid, gain, head, inner, outer, pick, places, live, slots_here):
     (tokens, width), (blocks, slots, rows) = resid.shape, pick.shape
     low = resid.dtype
     devices = blocks * slots // slots_here
-    by_block = lambda columns: pl.BlockSpec((rows, columns), lambda b, e: (b, 0))
+    by_block = pl.BlockSpec((rows, width), lambda b, e: (b, 0))
     outs = [
-        jax.ShapeDtypeStruct(shape, low)
-        for shape in (
-            (tokens, width),
-            (blocks * slots, HEAD_DIM),
-            (tokens, HEAD_DIM),
-            (tokens, HEAD_DIM),
-            (blocks * slots, HEAD_DIM),
-            (devices, 2, slots_here, width),
-        )
+        jax.ShapeDtypeStruct((tokens, width), low),
+        jax.ShapeDtypeStruct((blocks * slots, HEAD_DIM), low),
+        jax.ShapeDtypeStruct((tokens, HEAD_DIM), low),
+        jax.ShapeDtypeStruct((tokens, HEAD_DIM), low),
+        jax.ShapeDtypeStruct((blocks * slots, HEAD_DIM), low),
+        jax.ShapeDtypeStruct((2, tokens, HEAD_DIM), jnp.float32),
+        jax.ShapeDtypeStruct((2, blocks * slots, HEAD_DIM), jnp.float32),
+        jax.ShapeDtypeStruct((devices, 2, slots_here, width), low),
     ]
     return pl.pallas_call(
         attend_kernel,
@@ -630,30 +744,28 @@
             num_scalar_prefetch=1,
             grid=(blocks,),
             in_specs=[
-                by_block(width),
+                by_block,
                 whole_spec(gain),
                 whole_spec(head),
-                by_block(HEAD_DIM),
-                by_block(HEAD_DIM),
+                whole_spec(inner),
+                whole_spec(outer),
                 pl.BlockSpec((1, slots, rows), lambda b, e: (b, 0, 0)),
                 whole_spec(places),
                 whole_spec(live),
             ],
-            out_specs=[by_block(width)] + [whole_spec(out) for out in outs[1:]],
+            out_specs=[by_block] + [whole_spec(out) for out in outs[1:]],
         ),
         **local_params(),
-    )(exit_here, resid, gain, head, cosine, sine_table, pick, places, live)
-
-
-def attend_back(
-    exit_here, done, head, out, query, key, value, cosine, sine_table, slot_turns, pick, places, attn
-):
+    )(exit_here, resid, gain, head, inner, outer, pick, places, live)
+
+
+def attend_back(exit_here, done, head, out, query, key, value, turn, slot_turn, pick, places, attn):
     (tokens, width), (blocks, slots, rows) = attn.shape, pick.shape
     low = attn.dtype
     devices, _, slots_here, _ = done.shape
     by_block = pl.BlockSpec((rows, width), lambda b, e: (b, 0))
-    inner = [head, out, query, key, value, cosine, sine_table, *slot_turns, pick, places]
-    parts = jax.ShapeDtypeStruct((4 * HEAD_DIM, width), low)
+    inner = [head, out, query, key, value, turn, slot_turn, pick, places]
+    parts = jax.ShapeDtypeStruct(head.shape, low)
     return pl.pallas_call(
         attend_back_kernel,
         out_shape=[jax.ShapeDtypeStruct((tokens, width), low), parts],
@@ -677,6 +789,244 @@
     )(exit_here, done, *inner, attn)
 
 
+def local(kernel, outs, *values, scratch=()):
+    vmem = pl.BlockSpec(memory_space=pltpu.VMEM)
+    return pl.pallas_call(
+        kernel,
+        out_shape=[jax.ShapeDtypeStruct(shape, dtype) for shape, dtype in outs],
+        in_specs=[vmem] * len(values),
+        out_specs=[vmem] * len(outs),
+        scratch_shapes=list(scratch),
+        **local_params(),
+    )(*values)
+
+
+def pack_head_kernel(qkv_ref, out_ref, packed_ref):
+    heads = out_ref.shape[0] // HEAD_DIM
+    sharers = packed_ref.shape[0] // heads
+    low = packed_ref.dtype
+    for head in range(heads):
+        lanes = slice(head * HEAD_DIM, (head + 1) * HEAD_DIM)
+        for c in range(4):
+            block = out_ref[lanes] if c == 3 else qkv_ref[c, :, lanes].T
+            for sharer in range(sharers):
+                packed_ref[head * sharers + sharer, c * HEAD_DIM : (c + 1) * HEAD_DIM] = block.astype(
+                    low
+                )
+
+
+def pack_hidden_kernel(gate_up_ref, down_ref, packed_ref, turned_ref):
+    parts, hidden = packed_ref.shape[0], packed_ref.shape[1] // 3
+    low = packed_ref.dtype
+    for c in range(2):
+        for start in range(0, gate_up_ref.shape[2], 128):
+            lanes = slice(start, start + 128)
+            turned_ref[lanes] = gate_up_ref[:, c, lanes].T
+        for part in range(parts):
+            packed_ref[part, c * hidden : (c + 1) * hidden] = turned_ref[
+                part * hidden : (part + 1) * hidden
+            ].astype(low)
+    for part in range(parts):
+        packed_ref[part, 2 * hidden :] = down_ref[part * hidden : (part + 1) * hidden].astype(low)
+
+
+def square_row(value):
+    return jnp.sum(value * value, axis=0, keepdims=True)
+
+
+def unpack_head_kernel(one_ref, two_ref, qkv_ref, out_ref, square_ref):
+    heads = out_ref.shape[0] // HEAD_DIM
+    sharers = one_ref.shape[0] // heads
+    squares = jnp.zeros(square_ref.shape, jnp.float32)
+    for head in range(heads):
+        lanes = slice(head * HEAD_DIM, (head + 1) * HEAD_DIM)
+        for c in range(4):
+            parts_ref = one_ref if c < 2 else two_ref
+            rows = slice(c % 2 * HEAD_DIM, (c % 2 + 1) * HEAD_DIM)
+            total = parts_ref[head * sharers, rows].astype(jnp.float32)
+            for sharer in range(1, sharers):
+                total = total + parts_ref[head * sharers + sharer, rows].astype(jnp.float32)
+            squares = squares + square_row(total)
+            if c == 3:
+                out_ref[lanes] = total
+            else:
+                qkv_ref[c, :, lanes] = total.T
+    square_ref[...] = squares
+
+
+def unpack_hidden_kernel(parts_ref, gate_up_ref, down_ref, square_ref, turned_ref):
+    parts, hidden = parts_ref.shape[0], parts_ref.shape[1] // 3
+    squares = jnp.zeros(square_ref.shape, jnp.float32)
+    for c in range(3):
+        target = down_ref if c == 2 else turned_ref
+        for part in range(parts):
+            block = parts_ref[part, c * hidden : (c + 1) * hidden].astype(jnp.float32)
+            squares = squares + square_row(block)
+            target[part * hidden : (part + 1) * hidden] = block
+        if c < 2:
+            for start in range(0, gate_up_ref.shape[2], 128):
+                lanes = slice(start, start + 128)
+                gate_up_ref[:, c, lanes] = turned_ref[lanes].T
+    square_ref[...] = squares
+
+
+def hidden_kernel(rows_ref, weight_ref, gate_ref, up_ref, hidden_ref, partial_ref):
+    parts, columns = weight_ref.shape[0], weight_ref.shape[2]
+    hidden = weight_ref.shape[1] // 3
+    low = jnp.bfloat16
+    gate = jnp.zeros(gate_ref.shape, jnp.float32)
+    up = jnp.zeros(gate_ref.shape, jnp.float32)
+    for part in range(parts):
+        piece = rows_ref[:, part * columns : (part + 1) * columns]
+        gate = gate + dot(piece, weight_ref[part, :hidden], 1, 1)
+        up = up + dot(piece, weight_ref[part, hidden : 2 * hidden], 1, 1)
+    gate_ref[...], up_ref[...] = gate, up
+    value = (gate * jax.nn.sigmoid(gate) * up).astype(low)
+    hidden_ref[...] = value
+    for part in range(parts):
+        partial_ref[:, part * columns : (part + 1) * columns] = dot(
+            value, weight_ref[part, 2 * hidden :]
+        ).astype(low)
+
+
+def hidden_back_kernel(
+    dtwo_ref, rows_ref, weight_ref, gate_ref, up_ref, hidden_ref, partial_ref, parts_ref
+):
+    parts, columns = weight_ref.shape[0], weight_ref.shape[2]
+    hidden = weight_ref.shape[1] // 3
+    low = jnp.bfloat16
+    dhidden = jnp.zeros(gate_ref.shape, jnp.float32)
+    for part in range(parts):
+        piece = dtwo_ref[:, part * columns : (part + 1) * columns]
+        dhidden = dhidden + dot(piece, weight_ref[part, 2 * hidden :], 1, 1)
+        parts_ref[part, 2 * hidden :] = dot(hidden_ref[...], piece, 0, 0).astype(low)
+    gate, up = gate_ref[...], up_ref[...]
+    sigma = jax.nn.sigmoid(gate)
+    dgate = (dhidden * up * sigma * (1.0 + gate * (1.0 - sigma))).astype(low)
+    dup = (dhidden * gate * sigma).astype(low)
+    for part in range(parts):
+        lanes = slice(part * columns, (part + 1) * columns)
+        partial_ref[:, lanes] = (
+            dot(dgate, weight_ref[part, :hidden]) + dot(dup, weight_ref[part, hidden : 2 * hidden])
+        ).astype(low)
+        parts_ref[part, :hidden] = dot(dgate, rows_ref[:, lanes], 0, 0).astype(low)
+        parts_ref[part, hidden : 2 * hidden] = dot(dup, rows_ref[:, lanes], 0, 0).astype(low)
+
+
+def embed_kernel(base_ref, ids_ref, table_ref, partial_ref, low_ref, hits_ref):
+    @pl.when(pl.program_id(0) == 0)
+    def _():
+        entries = base_ref[0] + lax.broadcasted_iota(jnp.int32, (1, table_ref.shape[0]), 1)
+        hits_ref[...] = jnp.where(ids_ref[...] == entries, 1.0, 0.0).astype(hits_ref.dtype)
+
+    table_low = table_ref[...].astype(low_ref.dtype)
+    low_ref[...] = table_low
+    partial_ref[...] = dot(hits_ref[...], table_low).astype(partial_ref.dtype)
+
+
+def embed(base, ids, table):
+    (entries, width), tokens, low = table.shape, ids.shape[0], jnp.bfloat16
+    columns = 256
+    by_columns = lambda rows: pl.BlockSpec((rows, columns), lambda b, e: (0, b))
+    return pl.pallas_call(
+        embed_kernel,
+        out_shape=[
+            jax.ShapeDtypeStruct((tokens, width), low),
+            jax.ShapeDtypeStruct((entries, width), low),
+        ],
+        grid_spec=pltpu.PrefetchScalarGridSpec(
+            num_scalar_prefetch=1,
+            grid=(width // columns,),
+            in_specs=[whole_spec(ids), by_columns(entries)],
+            out_specs=[by_columns(tokens), by_columns(entries)],
+            scratch_shapes=[pltpu.VMEM((tokens, entries), low)],
+        ),
+        **local_params(),
+    )(base, ids, table)
+
+
+def logits_kernel(one_ref, two_ref, table_ref, target_ref, entry_ref, logits_ref, stats_ref):
+    slots, step, lanes = one_ref.shape[0], 256, stats_ref.shape[1]
+    for e, rows_ref in enumerate((one_ref, two_ref)):
+        for start in range(0, slots, step):
+            values = dot(rows_ref[start : start + step], table_ref[...], 1, 1)
+            logits_ref[e * slots + start : e * slots + start + step] = values
+            top = jnp.max(values, axis=1, keepdims=True)
+            mass = jnp.sum(jnp.exp(values - top), axis=1, keepdims=True)
+            for part in range(0, step, lanes):
+                row = (e * slots + start + part) // lanes
+                at = slice(part, part + lanes)
+                hit = to_column(target_ref[row : row + 1]) == entry_ref[...]
+                found = jnp.sum(jnp.where(hit, values[at], 0.0), axis=1, keepdims=True)
+                for stat, column in enumerate((top[at], mass[at], found)):
+                    index = stat * (2 * slots // lanes) + row
+                    stats_ref[index : index + 1] = to_row(column)
+
+
+def head_grad_kernel(
+    logits_ref, lse_ref, weight_ref, target_ref, entry_ref, table_ref, one_ref, two_ref, *terms
+):
+    slots, lanes, step = one_ref.shape[0], lse_ref.shape[1], 256
+    low = jnp.bfloat16
+    for e, grad_ref in enumerate((one_ref, two_ref)):
+        for start in range(0, slots, lanes):
+            row = (e * slots + start) // lanes
+            lse, weight, target = (
+                to_column(ref[row : row + 1]) for ref in (lse_ref, weight_ref, target_ref)
+            )
+            values = logits_ref[row * lanes : (row + 1) * lanes]
+            hit = jnp.where(target == entry_ref[...], 1.0, 0.0)
+            grad_ref[start : start + lanes] = (weight * (jnp.exp(values - lse) - hit)).astype(low)
+        for start in range(0, slots, step):
+            at = slice(start, start + step)
+            terms[e][at] = dot(grad_ref[at], table_ref[...]).astype(low)
+
+
+def table_grad_kernel(
+    base_ref, ids_ref, one_ref, two_ref, rows_one, rows_two, dzero_ref, grad_ref, square_ref, left_ref
+):
+    slots = one_ref.shape[0]
+
+    @pl.when(pl.program_id(0) == 0)
+    def _():
+        entries = base_ref[0] + lax.broadcasted_iota(jnp.int32, (left_ref.shape[0], 1), 0)
+        left_ref[:, :slots] = one_ref[...].T
+        left_ref[:, slots : 2 * slots] = two_ref[...].T
+        hits = jnp.where(ids_ref[...] == entries, 1.0, 0.0)
+        left_ref[:, 2 * slots :] = hits.astype(left_ref.dtype)
+
+    grad = (
+        dot(left_ref[:, :slots], rows_one[...])
+        + dot(left_ref[:, slots : 2 * slots], rows_two[...])
+        + dot(left_ref[:, 2 * slots :], dzero_ref[...])
+    )
+    grad_ref[...] = grad
+    square_ref[...] = square_row(grad)
+
+
+def table_gradient(base, ids, grads, rows, dzero):
+    slots, entries = grads[0].shape
+    tokens, width = dzero.shape
+    columns = 256
+    by_columns = lambda count: pl.BlockSpec((count, columns), lambda b, e: (0, b))
+    return pl.pallas_call(
+        table_grad_kernel,
+        out_shape=[
+            jax.ShapeDtypeStruct((entries, width), jnp.float32),
+            jax.ShapeDtypeStruct((1, width), jnp.float32),
+        ],
+        grid_spec=pltpu.PrefetchScalarGridSpec(
+            num_scalar_prefetch=1,
+            grid=(width // columns,),
+            in_specs=[whole_spec(ids), whole_spec(grads[0]), whole_spec(grads[1])]
+            + [by_columns(slots), by_columns(slots), by_columns(tokens)],
+            out_specs=[by_columns(entries), by_columns(1)],
+            scratch_shapes=[pltpu.VMEM((entries, 2 * slots + tokens), dzero.dtype)],
+        ),
+        **local_params(),
+    )(base, ids, *grads, *rows, dzero)
+
+
 def norm_fwd(values, gain):
     row_scale = lax.rsqrt(jnp.mean(values * values, axis=-1, keepdims=True) + EPS_NORM)
     unit_rows = values * row_scale
@@ -717,10 +1067,6 @@
     return lax.dot_general(
         left, right, (((left_dim,), (right_dim,)), ((), ())), preferred_element_type=jnp.float32
     )
-
-
-def placed(value, order):
-    return with_layout_constraint(value, Layout(major_to_minor=order))
 
 
 def adam_update(weight, moment_one, moment_two, gradient, rate, decay):
@@ -805,37 +1151,60 @@
     live = (slot_ids < jnp.sum(mask_blocks, axis=2)[:, :, None]).astype(jnp.float32).reshape(2, -1)
     counts = jnp.sum(live, axis=1)
 
-    head_rows = jnp.moveaxis(
-        qkv_weight.astype(low).reshape(width_here, 3, heads_here, HEAD_DIM), 0, 3
-    )
-    head_rows = jnp.concatenate(
-        [
-            jnp.moveaxis(head_rows, 0, 1).reshape(heads_here, 3 * HEAD_DIM, width_here),
-            out_weight.astype(low).reshape(heads_here, HEAD_DIM, width_here),
-        ],
-        axis=1,
-    )
-    hidden_rows = jnp.moveaxis(
-        gate_up_weight.astype(low).reshape(width_here, 2, data_size, hidden_here), 0, 3
-    )
-    hidden_rows = jnp.concatenate(
-        [
-            jnp.moveaxis(hidden_rows, 0, 1).reshape(data_size, 2 * hidden_here, width_here),
-            down_weight.astype(low).reshape(data_size, hidden_here, width_here),
-        ],
-        axis=1,
-    )
-
-    head_rows = swap_blocks(after(jnp.repeat(head_rows, sharers, axis=0), ints))
-
-    table_low = table.astype(low)
-    id_hits = (all_ids[:, None] == vocab_ids[None, :]).astype(low)
-    (resid_low,) = relay(
-        dot(id_hits, table_low).astype(low),
-        lambda p, total, extras: (total.astype(low), (), ()),
-        1,
-    )
+    packed = kernel_mesh()
+    head_shape = (data_size, 4 * HEAD_DIM, width_here)
+    hidden_shape = (data_size, 3 * hidden_here, width_here)
+    if packed:
+        (head_rows,) = local(
+            pack_head_kernel,
+            [(head_shape, low)],
+            jnp.transpose(qkv_weight, (1, 0, 2)),
+            out_weight,
+        )
+    else:
+        head_rows = jnp.moveaxis(
+            qkv_weight.astype(low).reshape(width_here, 3, heads_here, HEAD_DIM), 0, 3
+        )
+        head_rows = jnp.concatenate(
+            [
+                jnp.moveaxis(head_rows, 0, 1).reshape(heads_here, 3 * HEAD_DIM, width_here),
+                out_weight.astype(low).reshape(heads_here, HEAD_DIM, width_here),
+            ],
+            axis=1,
+        )
+        head_rows = jnp.repeat(head_rows, sharers, axis=0)
+    head_rows = swap_blocks(after(head_rows, ints))
+
+    base = (device_index * vocab_here)[None]
+    if packed:
+        id_rows, table_low = embed(base, all_ids[:, None], table)
+    else:
+        table_low = table.astype(low)
+        id_hits = (all_ids[:, None] == vocab_ids[None, :]).astype(low)
+        id_rows = dot(id_hits, table_low).astype(low)
+    if packed:
+        (hidden_rows,) = local(
+            pack_hidden_kernel,
+            [(hidden_shape, low)],
+            gate_up_weight,
+            down_weight,
+            scratch=[pltpu.VMEM((gate_up_weight.shape[2], width_here), jnp.float32)],
+        )
+    else:
+        hidden_rows = jnp.moveaxis(
+            gate_up_weight.astype(low).reshape(width_here, 2, data_size, hidden_here), 0, 3
+        )
+        hidden_rows = jnp.concatenate(
+            [
+                jnp.moveaxis(hidden_rows, 0, 1).reshape(data_size, 2 * hidden_here, width_here),
+                down_weight.astype(low).reshape(data_size, hidden_here, width_here),
+            ],
+            axis=1,
+        )
+    (resid_low,) = relay([after(id_rows, hidden_rows)], lambda p, total, extras: (total.astype(low), (), ()), 1)
+
     hidden_rows = swap_blocks(after(hidden_rows, resid_low))
+
     pick_share = lax.dynamic_slice_in_dim(
         lax.dynamic_index_in_dim(pick_low, exit_here, 0, keepdims=False),
         share_here * (data_size // shares),
@@ -848,30 +1217,29 @@
         ]
 
     places_share, live_share = share_of(slot_places), share_of(live)
-    cosine, sine_table = rotary(token_places, HEAD_DIM)
-    cosine_share, sine_share = rotary(places_share, HEAD_DIM)
-
-    def turns(cosines, sines):
-        return (
-            jnp.concatenate([cosines, cosines], axis=1),
-            jnp.concatenate([-sines, sines], axis=1),
-        )
-
-    if kernel_mesh():
-        attn_low, query_slots, key_low, value_low, attn_out, out_partial = attend(
+    if packed:
+
+        def turns(places):
+            return jnp.stack([jnp.concatenate([part, part], axis=1) for part in rotary(places, HEAD_DIM)])
+
+        attn_low, query_slots, key_low, value_low, attn_out, turn, slot_turn, out_partial = attend(
             exit_here[None],
             resid_low,
             gain_rows[:1],
             head_rows,
-            *turns(cosine, sine_table),
+            turns(token_places[:block_rows]),
+            turns(token_places[::block_rows]),
             pick_share,
-            places_share[:, None],
-            live_share[:, None],
+            places_share.reshape(-1, 2 * R_DEV),
+            live_share.reshape(-1, 2 * R_DEV),
             slots_here,
         )
         out_partial = out_partial.reshape(-1, width)
     else:
+        head_rows = jnp.moveaxis(head_rows, 0, 1).reshape(4 * HEAD_DIM, width)
         qkv_head, out_head = head_rows[: 3 * HEAD_DIM], head_rows[3 * HEAD_DIM :]
+        cosine, sine_table = rotary(token_places, HEAD_DIM)
+        cosine_share, sine_share = rotary(places_share, HEAD_DIM)
         attn_low = norm_fwd(resid_low.astype(jnp.float32), gain_rows[0])[0].astype(low)
 
         projected = dot(attn_low, qkv_head, 1, 1)
@@ -921,38 +1289,65 @@
         gain = 2 if p == 0 else 1
         return (norm_fwd(resid, extras[1][gain : gain + 1])[0].astype(low), (resid,), ())
 
-    first_rows, resid_one = relay(
-        out_partial,
+    exit_rows_one, mlp_low, resid_one = relay(
+        [out_partial],
         first_step,
         2,
         extras=[dot(pick_here, block_low), gain_rows],
         kept=1,
-    )
-    first_rows = first_rows.reshape(devices, 2, slots_here, width)
-    exit_rows_one = first_rows[:, 0].reshape(-1, width)
-    mlp_low = first_rows[:, 1].reshape(-1, width)
-
-    gate_up_head, down_head = hidden_rows[: 2 * hidden_here], hidden_rows[2 * hidden_here :]
-    gate_up = dot(mlp_low, gate_up_head, 1, 1)
-    gate_part, up_part = gate_up[:, :hidden_here], gate_up[:, hidden_here:]
-    gate_sigma = jax.nn.sigmoid(gate_part)
-    hidden_low = (gate_part * gate_sigma * up_part).astype(low)
+        split=True,
+    )
+
+    slots = mlp_low.shape[0]
+    if packed:
+        gate_part, up_part, hidden_low, mlp_partial = local(
+            hidden_kernel,
+            [
+                ((slots, hidden_here), jnp.float32),
+                ((slots, hidden_here), jnp.float32),
+                ((slots, hidden_here), low),
+                ((slots, width), low),
+            ],
+            mlp_low,
+            hidden_rows,
+        )
+    else:
+        hidden_rows = jnp.moveaxis(hidden_rows, 0, 1).reshape(3 * hidden_here, width)
+        gate_up_head, down_head = hidden_rows[: 2 * hidden_here], hidden_rows[2 * hidden_here :]
+        gate_up = dot(mlp_low, gate_up_head, 1, 1)
+        gate_part, up_part = gate_up[:, :hidden_here], gate_up[:, hidden_here:]
+        gate_sigma = jax.nn.sigmoid(gate_part)
+        hidden_low = (gate_part * gate_sigma * up_part).astype(low)
+        mlp_partial = dot(hidden_low, down_head).astype(low)
 
     def second_step(p, total, extras):
         resid = extras[0][GROUP : 2 * GROUP] + total
         return (norm_fwd(resid, extras[1][2:3])[0].astype(low), (resid,), ())
 
     exit_rows_two, resid_two = relay(
-        dot(hidden_low, down_head).astype(low), second_step, 3, extras=[resid_one, gain_rows], kept=1
+        [mlp_partial], second_step, 3, extras=[resid_one, gain_rows], kept=1
     )
 
     exit_rows = (exit_rows_one, exit_rows_two)
-    logits = [dot(rows, table_low, 1, 1) for rows in exit_rows]
-    hits = [slot_targets[e][:, None] == vocab_ids[None, :] for e in range(2)]
-    tops = [jnp.max(values, axis=1) for values in logits]
-    masses = [jnp.sum(jnp.exp(values - top[:, None]), axis=1) for values, top in zip(logits, tops)]
-    found = [jnp.sum(jnp.where(hit, values, 0.0), axis=1) for hit, values in zip(hits, logits)]
-    stats = jnp.concatenate(tops + masses + found).reshape(-1, 128)
+    if packed:
+        target_rows, entry_row = slot_targets.reshape(-1, 128), vocab_ids[None]
+        logits, stats = local(
+            logits_kernel,
+            [((2 * slots, vocab_here), jnp.float32), ((3 * 2 * slots // 128, 128), jnp.float32)],
+            *exit_rows,
+            table_low,
+            target_rows,
+            entry_row,
+        )
+    else:
+        logits = [dot(rows, table_low, 1, 1) for rows in exit_rows]
+        hits = [slot_targets[e][:, None] == vocab_ids[None, :] for e in range(2)]
+        tops = [jnp.max(values, axis=1) for values in logits]
+        masses = [
+            jnp.sum(jnp.exp(values - top[:, None]), axis=1) for values, top in zip(logits, tops)
+        ]
+        found = [jnp.sum(jnp.where(hit, values, 0.0), axis=1) for hit, values in zip(hits, logits)]
+        stats = jnp.concatenate(tops + masses + found).reshape(-1, 128)
     stats = gather_small(stats, 4).reshape(devices, 3, 2, -1)
     row_top = jnp.max(stats[:, 0], axis=0)
     row_mass = jnp.sum(stats[:, 1] * jnp.exp(stats[:, 0] - row_top), axis=0)
@@ -960,21 +1355,27 @@
     entropy = row_lse - jnp.sum(stats[:, 2], axis=0)
     loss_sums = jnp.sum(entropy * live, axis=1)
     row_weight = live * (jnp.array(EXIT_SCALE, jnp.float32) / counts)[:, None]
-    grad_logits = [
-        (
-            row_weight[e][:, None]
-            * (jnp.exp(logits[e] - row_lse[e][:, None]) - hits[e].astype(jnp.float32))
-        ).astype(low)
-        for e in range(2)
-    ]
-    table_head = dot(grad_logits[0], exit_rows_one, 0, 0) + dot(grad_logits[1], exit_rows_two, 0, 0)
-    row_terms = jnp.stack(
-        [
-            dot(grad, table_low).astype(low).reshape(devices, slots_here, width)
-            for grad in grad_logits
-        ],
-        axis=1,
-    )
+    if packed:
+        *grad_logits, one_terms, two_terms = local(
+            head_grad_kernel,
+            [((slots, vocab_here), low)] * 2 + [((slots, width), low)] * 2,
+            logits,
+            row_lse.reshape(-1, 128),
+            row_weight.reshape(-1, 128),
+            target_rows,
+            entry_row,
+            table_low,
+        )
+        row_terms = [one_terms, two_terms]
+    else:
+        grad_logits = [
+            (
+                row_weight[e][:, None]
+                * (jnp.exp(logits[e] - row_lse[e][:, None]) - hits[e].astype(jnp.float32))
+            ).astype(low)
+            for e in range(2)
+        ]
+        row_terms = [dot(grad, table_low).astype(low) for grad in grad_logits]
 
     def head_step(p, total, extras):
         values = extras[0][:GROUP] if p == 0 else extras[1][...]
@@ -984,7 +1385,7 @@
         return (None if p == 0 else back.astype(low), (back,), (gain_grad[None],))
 
     dtwo_low, dexits, final_grad = relay(
-        row_terms.reshape(-1, width),
+        row_terms,
         head_step,
         5,
         extras=[resid_one, resid_two, gain_rows],
@@ -993,12 +1394,27 @@
         order=[1, 0],
         slot=lambda p: None if p == 0 else 0,
     )
-    down_local = dot(hidden_low, dtwo_low, 0, 0)
-    dhidden = dot(dtwo_low, down_head, 1, 1)
-    dgate = dhidden * up_part * gate_sigma * (1.0 + gate_part * (1.0 - gate_sigma))
-    dup_part = dhidden * gate_part * gate_sigma
-    dgate_up = jnp.concatenate([dgate, dup_part], axis=1).astype(low)
-    gate_up_local = dot(dgate_up, mlp_low, 0, 0)
+    if packed:
+        dmlp_partial, hidden_parts = local(
+            hidden_back_kernel,
+            [((slots, width), low), (hidden_shape, low)],
+            dtwo_low,
+            mlp_low,
+            hidden_rows,
+            gate_part,
+            up_part,
+            hidden_low,
+        )
+    else:
+        down_local = dot(hidden_low, dtwo_low, 0, 0)
+        dhidden = dot(dtwo_low, down_head, 1, 1)
+        dgate = dhidden * up_part * gate_sigma * (1.0 + gate_part * (1.0 - gate_sigma))
+        dup_part = dhidden * gate_part * gate_sigma
+        dgate_up = jnp.concatenate([dgate, dup_part], axis=1).astype(low)
+        gate_up_local = dot(dgate_up, mlp_low, 0, 0)
+        dmlp_partial = dot(dgate_up, gate_up_head).astype(low)
+        hidden_parts = jnp.concatenate([gate_up_local.astype(low), down_local.astype(low)])
+        hidden_parts = jnp.moveaxis(hidden_parts.reshape(-1, data_size, width_here), 1, 0)
 
     def mlp_step(p, total, extras):
         gain = extras[2][1:2]
@@ -1007,7 +1423,7 @@
         return ((extras[1][GROUP : 2 * GROUP] + back).astype(low), (), (gain_grad[None],))
 
     done_low, mlp_grad = relay(
-        dot(dgate_up, gate_up_head).astype(low),
+        [dmlp_partial],
         mlp_step,
         6,
         extras=[resid_one, dexits, gain_rows],
@@ -1015,7 +1431,6 @@
         slot=lambda p: 1,
         ready=dexits[:GROUP].astype(low),
     )
-    hidden_parts = jnp.concatenate([gate_up_local.astype(low), down_local.astype(low)])
     hidden_parts = swap_blocks(after(hidden_parts, done_low))
     done_low = done_low.reshape(devices, 2, slots_here, width)
 
@@ -1028,10 +1443,10 @@
             query_slots,
             key_low,
             value_low,
-            *turns(cosine, sine_table),
-            turns(cosine_share, sine_share),
+            turn,
+            slot_turn,
             pick_share,
-            places_share[:, None],
+            places_share.reshape(-1, 2 * R_DEV),
             attn_low,
         )
     else:
@@ -1068,6 +1483,7 @@
         )
         head_parts = jnp.concatenate([dot(dprojected, attn_low, 0, 0).astype(low), out_local.astype(low)])
         zero_partial = dot(dprojected, qkv_head).astype(low)
+        head_parts = jnp.moveaxis(head_parts.reshape(-1, data_size, width_here), 1, 0)
 
     resid_here = lax.dynamic_slice_in_dim(resid_low, device_index * rows_here, rows_here, 0)
     done_block = lax.dynamic_slice_in_dim(done_low, data_index * model_size, model_size, 0)
@@ -1087,36 +1503,71 @@
         back, gain_grad = norm_back(unit, scale, gain, total)
         return ((extras[1][at] + back).astype(low), (), (gain_grad[None],))
 
-    dzero_low, attn_grad = relay(
-        after(zero_partial, head_parts, hidden_parts),
+    ride = 2 * HEAD_DIM
+    dzero_low, attn_grad, ridden = relay(
+        [after(zero_partial, hidden_parts)],
         zero_step,
         7,
         extras=[resid_here.astype(jnp.float32), dresid_here, gain_rows],
         sums=1,
-    )
-    head_parts = swap_blocks(after(head_parts, dzero_low))
-    table_grad = table_head + dot(id_hits, dzero_low, 0, 0)
-
-    head_grad = jnp.sum(
-        head_parts.reshape(heads_here, sharers, 4, HEAD_DIM, width_here).astype(jnp.float32), axis=1
-    )
-    qkv_grad = placed(jnp.transpose(head_grad[:, :3], (3, 1, 0, 2)).reshape(qkv_weight.shape), (1, 0, 2))
-    out_grad = head_grad[:, 3].reshape(out_weight.shape)
-    hidden_parts = hidden_parts.astype(jnp.float32)
-    gate_up_grad = hidden_parts[:, : 2 * hidden_here].reshape(
-        data_size, 2, hidden_here, width_here
-    )
-    gate_up_grad = placed(
-        jnp.transpose(gate_up_grad, (3, 1, 0, 2)).reshape(gate_up_weight.shape), (0, 1, 2)
-    )
-    down_grad = hidden_parts[:, 2 * hidden_here :].reshape(down_weight.shape)
-    squares = (
-        jnp.sum(table_grad * table_grad)
-        + jnp.sum(qkv_grad * qkv_grad)
-        + jnp.sum(out_grad * out_grad)
-        + jnp.sum(gate_up_grad * gate_up_grad)
-        + jnp.sum(down_grad * down_grad)
-    )
+        cargo=head_parts[:, :ride],
+    )
+    later = swap_blocks(after(head_parts[:, ride:], dzero_low))
+    if packed:
+        table_grad, squares = table_gradient(
+            base, all_ids[None, :], grad_logits, exit_rows, dzero_low
+        )
+        squares = jnp.sum(squares)
+    else:
+        table_grad = dot(id_hits, dzero_low, 0, 0)
+        for grad, rows in zip(grad_logits, exit_rows):
+            table_grad = table_grad + dot(grad, rows, 0, 0)
+        squares = jnp.sum(table_grad * table_grad)
+
+    square_shape = ((1, width_here), jnp.float32)
+    if packed:
+        qkv_grad, out_grad, head_squares = local(
+            unpack_head_kernel,
+            [
+                ((3, width_here, qkv_weight.shape[2]), jnp.float32),
+                (out_weight.shape, jnp.float32),
+                square_shape,
+            ],
+            ridden,
+            later,
+        )
+        qkv_grad = jnp.transpose(qkv_grad, (1, 0, 2))
+        gate_up_grad, down_grad, hidden_squares = local(
+            unpack_hidden_kernel,
+            [
+                (gate_up_weight.shape, jnp.float32),
+                (down_weight.shape, jnp.float32),
+                square_shape,
+            ],
+            hidden_parts,
+            scratch=[pltpu.VMEM((gate_up_weight.shape[2], width_here), jnp.float32)],
+        )
+        squares = squares + jnp.sum(head_squares) + jnp.sum(hidden_squares)
+    else:
+        head_grad = jnp.sum(
+            jnp.concatenate([ridden, later], axis=1).reshape(heads_here, sharers, 4, HEAD_DIM, width_here).astype(jnp.float32),
+            axis=1,
+        )
+        qkv_grad = jnp.transpose(head_grad[:, :3], (3, 1, 0, 2)).reshape(qkv_weight.shape)
+        out_grad = head_grad[:, 3].reshape(out_weight.shape)
+        hidden_parts = hidden_parts.astype(jnp.float32)
+        gate_up_grad = hidden_parts[:, : 2 * hidden_here].reshape(
+            data_size, 2, hidden_here, width_here
+        )
+        gate_up_grad = jnp.transpose(gate_up_grad, (3, 1, 0, 2)).reshape(gate_up_weight.shape)
+        down_grad = hidden_parts[:, 2 * hidden_here :].reshape(down_weight.shape)
+        squares = (
+            squares
+            + jnp.sum(qkv_grad * qkv_grad)
+            + jnp.sum(out_grad * out_grad)
+            + jnp.sum(gate_up_grad * gate_up_grad)
+            + jnp.sum(down_grad * down_grad)
+        )
     parts = jnp.concatenate(
         [
             jnp.concatenate([attn_grad, mlp_grad, final_grad]).reshape(-1, 128),

time: 735 us -> 688 us (0.936)
  the two profiles are of different devices: /device:TPU:15 before, /device:TPU:0 now
where the time goes in v4:
time: 688 us; the launch traced here: 675 us
  Pallas kernels  546 us (79%)
  other arithmetic  61.7 us (9%)
  waiting for transfers between devices  20.2 us (3%)
  local copies, waits for them, and re-layouts  18.5 us (3%)
  starting transfers between devices  18.2 us (3%)
    pallas_call x6, Pallas kernels, relay(): pl.pallas_call(functools.partial(relay_kernel, plan, row_step), out_shape...  371 us
    pallas_call x8, Pallas kernels, local(): pl.pallas_call(kernel, out_shape=[jax.ShapeDtypeStruct(shape, dtype) for...  51.8 us
    sub x6, other arithmetic, adam_update(): return (weight - rate * (ratio + decay * weight), moment_one, moment_two)  44 us
    pallas_call x2, Pallas kernels, gather_small(): pl.pallas_call(small_gather_kernel, out_shape=jax.ShapeDtypeStruct((32,)...  35.3 us
    pallas_call x1, Pallas kernels, attend_back(): pl.pallas_call(attend_back_kernel, out_shape=[jax.ShapeDtypeStruct((token...  23.2 us
    pallas_call x1, Pallas kernels, attend(): pl.pallas_call(attend_kernel, out_shape=outs, grid_spec=pltpu.PrefetchSca...  21.1 us
    all_to_all x4, waiting for transfers between devices, swap_blocks(): return lax.all_to_all(value, 'dp', split_axis=0, concat_axis=0, tiled=True)  20.2 us
    pallas_call x1, Pallas kernels, table_gradient(): pl.pallas_call(table_grad_kernel, out_shape=[jax.ShapeDtypeStruct((entrie...  19.2 us
  transfers between devices with their start and end apart: 4, of which 1 were waited for; matrix products, arithmetic and copies ran while one was open for 4% of the time, Pallas kernels for 35%

profile of v4, /device:TPU:0, one launch (start us, length us, event | category | flops | bytes accessed | tf_op | source)
XLA Modules:
  0.0 674.5 jit_solution(2769669700988802592)
XLA Ops:
  3.3 9.6 %shard_map.373 = (s32[8,4,256]{2,1,0:T(4,128)}, bf16[8,16,256]{2,1,0:T(8,128)(2,1)}) custom-call(s32[4,256]{1,0:T(4,128)} %pad_add_fusion.refs_0_, bf16[16,256]{1,0:T(8,128)(2,1)} %pad.5.refs_1_), custom_call_target="tpu_custom_call" | custom-call | tf_op jit(solution)/shard_map/pallas_call | solution.py:529
  12.9 3.1 shard_map.377
  16.0 5.4 all-to-all-start
  21.4 6.1 shard_map.375
  28.9 14.9 %shard_map.374 = (bf16[2048,2048]{1,0:T(8,128)(2,1)}, bf16[1000,2048]{1,0:T(8,128)(2,1)}) custom-call(s32[1]{0:T(128)} %bitcast.4.base_ref, s32[2048,1]{1,0:T(8,128)} %copy.59.ids_ref, f32[1000,2048]{1,0:T(8,128)} %table_ref.1), custom_call_target="tpu_custom_call" | custom-call | flops 1 | bytes 1 | tf_op jit(solution)/shard_map/pallas_call | solution.py:931
  43.9 89.5 %shard_map.376.resid_ref = bf16[2048,2048]{1,0:T(8,128)(2,1)} custom-call(bf16[2048,2048]{1,0:T(8,128)(2,1)} %get-tuple-element.76.refs_0_), custom_call_target="tpu_custom_call" | custom-call | flops 1 | bytes 1 | tf_op jit(solution)/shard_map/pallas_call | solution.py:403
  137.3 4.6 all-to-all-start.1
  151.1 2.2 fusion.5.refs_1_
  153.3 21.1 %shard_map.378 = (bf16[2048,2048]{1,0:T(8,128)(2,1)}, bf16[512,128]{1,0:T(8,128)(2,1)}, bf16[2048,128]{1,0:T(8,128)(2,1)}, bf16[2048,128]{1,0:T(8,128)(2,1)}, bf...) custom-call(s32[1]{0:T(128)} %bitcast.3.exit_ref, ...), custom_call_target="tpu_custom_call" | custom-call | flops 1 | bytes 1 | tf_op jit(solution)/shard_map/pallas_call | solution.py:740
  174.4 59.2 %shard_map.379 = (bf16[512,2048]{1,0:T(8,128)(2,1)}, bf16[512,2048]{1,0:T(8,128)(2,1)}, f32[32,2048]{1,0:T(8,128)}) custom-call(bf16[1024,2048]{1,0:T(8,128)(2,1)} %bitcast.74, f32[32,2048]{1,0:T(8,128)} %fusion.5.refs_1_, f32[3,2048]{1,0:T(4,128)} %bitcast.75), custom_call_target="tpu_custom_call" | custom-call | flops 1 | bytes 1 | tf_op jit(solution)/shard_map/pallas_call | solution.py:403
  235.0 5.4 shard_map.380
  240.4 39.0 %shard_map.381 = (bf16[512,2048]{1,0:T(8,128)(2,1)}, f32[16,2048]{1,0:T(8,128)}) custom-call(bf16[512,2048]{1,0:T(8,128)(2,1)} %get-tuple-element.83.refs_0_, f32[32,2048]{1,0:T(8,128)} %get-tuple-element.84.refs_1_.refs_2_, f32[3,2048]{1,0:T(4,128)} %bitcast.76), custom_call_target="tpu_custom_call" | custom-call | flops 1 | bytes 1 | tf_op jit(solution)/shard_map/pallas_call | solution.py:403
  279.4 10.1 %shard_map.382 = (f32[1024,1000]{1,0:T(8,128)}, f32[24,128]{1,0:T(8,128)}) custom-call(bf16[512,2048]{1,0:T(8,128)(2,1)} %get-tuple-element.80.one_ref.rows_one, bf16[512,2048]{1,0:T(8,128)(2,1)} %get-tuple-element.85.two_ref.rows_two, bf16[1000,2048]{1,0:T(8,128)(2,1)} %get-tuple-element.86.table_ref, s32[8,128]{1,0:T(8,128)} %reshape_reshape.3.target_ref, ...), custom_call_target="tpu_custom_call" | custom-call | flops 1 | bytes 1 | tf_op jit(solution)/shard_map/pallas_call | solution.py:794
  289.5 12.4 %shard_map.383 = f32[32,24,128]{2,1,0:T(8,128)} custom-call(f32[24,128]{1,0:T(8,128)} %get-tuple-element.87.x_ref), custom_call_target="tpu_custom_call" | custom-call | tf_op jit(solution)/shard_map/pallas_call | solution.py:460
  304.6 10.0 %shard_map.384 = (bf16[512,1000]{1,0:T(8,128)(2,1)}, bf16[512,1000]{1,0:T(8,128)(2,1)}, bf16[512,2048]{1,0:T(8,128)(2,1)}, bf16[512,2048]{1,0:T(8,128)(2,1)}) custom-call(f32[1024,1000]{1,0:T(8,128)} %get-tuple-element.88.logits_ref, f32[8,128]{1,0:T(8,128)} %add.196.lse_ref, f32[8,128]{1,0:T(8,128)} %compare_select_fusion.weight_ref, ...), custom_call_target="tpu_custom_call" | custom-call | flops 1 | bytes 1 | tf_op jit(solution)/shard_map/pallas_call | solution.py:794
  314.6 47.0 %shard_map.385 = (bf16[512,2048]{1,0:T(8,128)(2,1)}, f32[32,2048]{1,0:T(8,128)}, f32[1,2048]{1,0:T(1,128)}) custom-call(bf16[512,2048]{1,0:T(8,128)(2,1)} %get-tuple-element.89.refs_0_, bf16[512,2048]{1,0:T(8,128)(2,1)} %get-tuple-element.90.refs_1_, f32[32,2048]{1,0:T(8,128)} %get-tuple-element.84.refs_1_.refs_2_, f32[16,2048]{1,0:T(8,128)} %get-tuple-element.91.refs_3_, ...), custom_call_target="tpu_custom_call" | custom-call | flops 1 | bytes 1 | tf_op jit(solution)/shard_map/pallas_call | solution.py:403
  363.1 8.3 %shard_map.386 = (bf16[512,2048]{1,0:T(8,128)(2,1)}, bf16[8,528,256]{2,1,0:T(8,128)(2,1)}) custom-call(bf16[512,2048]{1,0:T(8,128)(2,1)} %get-tuple-element.92.dtwo_ref, bf16[512,2048]{1,0:T(8,128)(2,1)} %get-tuple-element.81.rows_ref, bf16[8,528,256]{2,1,0:T(8,128)(2,1)} %copy-done, f32[512,176]{1,0:T(8,128)} %get-tuple-element.93.gate_ref, ...), custom_call_target="tpu_custom_call" | custom-call | flops 1 | bytes 1 | tf_op jit(solution)/shard_map/pallas_call | solution.py:794
  371.5 40.4 %shard_map.387 = (bf16[1024,2048]{1,0:T(8,128)(2,1)}, f32[1,2048]{1,0:T(1,128)}) custom-call(bf16[512,2048]{1,0:T(8,128)(2,1)} %get-tuple-element.96.refs_0_, bf16[16,2048]{1,0:T(8,128)(2,1)} %slice.114.refs_1_, f32[32,2048]{1,0:T(8,128)} %get-tuple-element.84.refs_1_.refs_2_, f32[32,2048]{1,0:T(8,128)} %get-tuple-element.97.refs_3_, f32[3,2048]{1,0:T(4,128)} %bitcast.78), custom_call_target="tpu_custom_call" | custom-call | flops 1 | bytes 1 | tf_op jit(solution)/shard_map/pallas_call | solution.py:403
  411.9 4.0 all-to-all-start.2
  417.7 23.2 %shard_map.388 = (bf16[2048,2048]{1,0:T(8,128)(2,1)}, bf16[8,512,256]{2,1,0:T(8,128)(2,1)}) custom-call(s32[1]{0:T(128)} %bitcast.3.exit_ref, bf16[32,2,16,2048]{3,2,1,0:T(8,128)(2,1)} %bitcast.72, bf16[8,512,256]{2,1,0:T(8,128)(2,1)} %copy-done.1, bf16[512,128]{1,0:T(8,128)(2,1)} %get-tuple-element.99.out_ref, ...), custom_call_target="tpu_custom_call" | custom-call | flops 1 | bytes 1 | tf_op jit(solution)/shard_map/pallas_call | solution.py:769
  443.0 3.0 fusion.24
  446.0 20.1 %all-to-all-done.2.parts_ref = bf16[8,528,256]{2,1,0:T(8,128)(2,1)S(1)} async-done(((bf16[8,528,256]{2,1,0:T(8,128)(2,1)}), bf16[8,528,256]{2,1,0:T(8,128)(2,1)S(1)}, u32[]{:S(2)}, u32[]{:S(2)}) %all-to-all-start.2) | async-done | bytes 2162720 | tf_op jit(solution)/shard_map/all_to_all | solution.py:421
  466.2 95.6 %shard_map.389 = (bf16[2048,2048]{1,0:T(8,128)(2,1)}, f32[1,2048]{1,0:T(1,128)}, bf16[8,256,256]{2,1,0:T(8,128)(2,1)}) custom-call(bf16[2048,2048]{1,0:T(8,128)(2,1)} %get-tuple-element.109.refs_0_, f32[64,2048]{1,0:T(8,128)} %dynamic-slice_convert_fusion.refs_1_, f32[64,2048]{1,0:T(8,128)} %convolution_bitcast_fusion.refs_2_, f32[3,2048]{1,0:T(4,128)} %bitcast.79, ...), custom_call_target="tpu_custom_call" | custom-call | flops 1 | bytes 1 | tf_op jit(solution)/shard_map/pallas_call | solution.py:403
  561.8 4.1 all-to-all-start.3
  565.9 19.2 %shard_map.390 = (f32[1000,2048]{1,0:T(8,128)}, f32[1,2048]{1,0:T(1,128)}) custom-call(s32[1]{0:T(128)} %bitcast.4.base_ref, s32[1,2048]{1,0:T(1,128)} %bitcast.82, bf16[512,1000]{1,0:T(8,128)(2,1)} %get-tuple-element.114.one_ref, bf16[512,1000]{1,0:T(8,128)(2,1)} %get-tuple-element.115.two_ref, bf16[512,2048]{1,0:T(8,128)(2,1)} %get-tuple-element.80.one_ref.rows_one, ...), custom_call_target="tpu_custom_call" | custom-call | flops 1 | bytes 1 | tf_op jit(solution)/shard_map/pallas_call | solution.py:1012
  585.1 5.5 shard_map.392
  593.6 3.3 shard_map.391
  600.7 22.9 %shard_map.393 = f32[32,56,128]{2,1,0:T(8,128)} custom-call(f32[56,128]{1,0:T(8,128)} %concatenate.27.x_ref), custom_call_target="tpu_custom_call" | custom-call | tf_op jit(solution)/shard_map/pallas_call | solution.py:460
  627.4 22.8 %multiply_subtract_fusion = (f32[1000,2048]{1,0:T(8,128)}, f32[1000,2048]{1,0:T(8,128)}, f32[1000,2048]{1,0:T(8,128)}) fusion(f32[1000,2048]{1,0:T(8,128)} %table_ref.1, f32[1000,2048]{1,0:T(8,128)} %get-tuple-element.122, f32[]{:T(128)S(6)} %min.3, f32[1000,2048]{1,0:T(8,128)} %param.26, f32[1000,2048]{1,0:T(8,128)} %param.27), kind=kLoop, calls=%fused_computation.2 | loop fusion | flops 32768000 | bytes 57344004 | tf_op jit(solution)/shard_map/sub | solution.py:1080
  650.3 5.2 multiply_subtract_fusion.2
  658.5 11.1 %multiply_subtract_fusion.1 = (f32[256,2,1408]{2,1,0:T(2,128)}, f32[256,2,1408]{2,1,0:T(2,128)}, f32[256,2,1408]{2,1,0:T(2,128)}) fusion(f32[256,2,1408]{2,1,0:T(2,128)S(1)} %copy-done.2, f32[256,2,1408]{2,1,0:T(2,128)S(1)} %copy-done.9, f32[]{:T(128)S(6)} %min.3, f32[256,2,1408]{2,1,0:T(2,128)S(1)} %copy-done.7, f32[256,2,1408]{2,1,0:T(2,128)S(1)} %copy-done.8), kind=kLoop, calls=%fused_computation.6 | loop fusion | flops 11534336 | bytes 20185092 | tf_op jit(solution)/shard_map/sub | solution.py:1080
  669.7 2.8 multiply_subtract_fusion.3
  (138 shorter events, 37.4 us)
Async XLA Ops:
  16.0 120.0 %all-to-all-start = ((bf16[8,512,256]{2,1,0:T(8,128)(2,1)}), bf16[8,512,256]{2,1,0:T(8,128)(2,1)S(1)}, u32[]{:S(2)}, u32[]{:S(2)}) async-start(bf16[8,512,256]{2,1,0:T(8,128)(2,1)} %shard_map.377), calls=%async_computation | async-start | bytes 4194304 | tf_op jit(solution)/shard_map/all_to_all | solution.py:421
  21.4 6.1 copy-start.18
  27.6 16.3 %copy-start.19 = (s32[8,1,256]{2,1,0:T(1,128)}, s32[8,1,256]{2,1,0:T(1,128)S(1)}, u32[]{:S(2)}) copy-start(s32[8,1,256]{2,1,0:T(1,128)S(1)} %get-tuple-element.154) | copy-start | bytes 24580
  136.0 9.4 %copy-start.28 = (f32[2]{0:T(128)S(1)}, f32[2]{0:T(128)}, u32[]{:S(2)}) copy-start(f32[2]{0:T(128)} %constant.157.clone) | copy-start | bytes 28
  136.0 1.3 copy-start.1
  137.3 96.4 %all-to-all-start.1 = ((bf16[8,528,256]{2,1,0:T(8,128)(2,1)}), bf16[8,528,256]{2,1,0:T(8,128)(2,1)S(1)}, u32[]{:S(2)}, u32[]{:S(2)}) async-start(bf16[8,528,256]{2,1,0:T(8,128)(2,1)} %shard_map.375), calls=%async_computation.1 | async-start | bytes 4325376 | tf_op jit(solution)/shard_map/all_to_all | solution.py:421
  145.3 29.1 %copy-start.27 = (f32[2]{0:T(128)}, f32[2]{0:T(128)S(1)}, u32[]{:S(2)}) copy-start(f32[2]{0:T(128)S(1)} %convert_reduce_fusion) | copy-start | bytes 28
  233.7 1.3 copy-start
  411.9 54.3 %all-to-all-start.2 = ((bf16[8,528,256]{2,1,0:T(8,128)(2,1)}), bf16[8,528,256]{2,1,0:T(8,128)(2,1)S(1)}, u32[]{:S(2)}, u32[]{:S(2)}) async-start(bf16[8,528,256]{2,1,0:T(8,128)(2,1)} %get-tuple-element.108), calls=%async_computation.2 | async-start | bytes 4325376 | tf_op jit(solution)/shard_map/all_to_all | solution.py:421
  466.2 95.6 %copy-start.3 = (bf16[8,528,256]{2,1,0:T(8,128)(2,1)}, bf16[8,528,256]{2,1,0:T(8,128)(2,1)S(1)}, u32[]{:S(2)}) copy-start(bf16[8,528,256]{2,1,0:T(8,128)(2,1)S(1)} %all-to-all-done.2.parts_ref) | copy-start | bytes 6488068
  561.8 30.8 %all-to-all-start.3 = ((bf16[8,256,256]{2,1,0:T(8,128)(2,1)}), bf16[8,256,256]{2,1,0:T(8,128)(2,1)S(1)}, u32[]{:S(2)}, u32[]{:S(2)}) async-start(bf16[8,256,256]{2,1,0:T(8,128)(2,1)} %get-tuple-element.119), calls=%async_computation.3 | async-start | bytes 2097152 | tf_op jit(solution)/shard_map/all_to_all | solution.py:421
  585.1 5.5 copy-start.21
  585.1 5.5 copy-start.22
  585.1 5.5 copy-start.23
  585.1 5.5 copy-start.24
  627.4 22.9 %copy-start.4 = (f32[256,3,512]{2,0,1:T(8,128)S(1)}, f32[256,3,512]{2,0,1:T(8,128)}, u32[]{:S(2)}) copy-start(f32[256,3,512]{2,0,1:T(8,128)} %param.28) | copy-start | bytes 4718596
  627.4 22.8 %copy-start.11 = (f32[256,3,512]{2,0,1:T(8,128)S(1)}, f32[256,3,512]{2,0,1:T(8,128)}, u32[]{:S(2)}) copy-start(f32[256,3,512]{2,0,1:T(8,128)} %param.29) | copy-start | bytes 4718596
  650.2 5.3 copy-start.10
  650.2 5.2 copy-start.15
  650.3 5.2 copy-start.16
  650.3 5.2 copy-start.17
  650.3 6.7 copy-start.7
  650.3 6.6 copy-start.8
  650.3 7.3 %copy-start.9 = (f32[256,2,1408]{2,1,0:T(2,128)S(1)}, f32[256,2,1408]{2,1,0:T(2,128)}, u32[]{:S(2)}) copy-start(f32[256,2,1408]{2,1,0:T(2,128)} %get-tuple-element.125) | copy-start | bytes 8650756
  655.5 3.0 copy-start.2
  658.5 11.2 %copy-start.5 = (f32[1408,256]{1,0:T(8,128)S(1)}, f32[1408,256]{1,0:T(8,128)}, u32[]{:S(2)}) copy-start(f32[1408,256]{1,0:T(8,128)} %down_ref.1) | copy-start | bytes 4325380
  658.5 11.2 %copy-start.12 = (f32[1408,256]{1,0:T(8,128)S(1)}, f32[1408,256]{1,0:T(8,128)}, u32[]{:S(2)}) copy-start(f32[1408,256]{1,0:T(8,128)} %param.38) | copy-start | bytes 4325380
  658.5 11.2 %copy-start.13 = (f32[1408,256]{1,0:T(8,128)S(1)}, f32[1408,256]{1,0:T(8,128)}, u32[]{:S(2)}) copy-start(f32[1408,256]{1,0:T(8,128)} %param.39) | copy-start | bytes 4325380
  658.5 11.2 %copy-start.14 = (f32[1408,256]{1,0:T(8,128)S(1)}, f32[1408,256]{1,0:T(8,128)}, u32[]{:S(2)}) copy-start(f32[1408,256]{1,0:T(8,128)} %get-tuple-element.126) | copy-start | bytes 4325380
  669.7 2.9 copy-start.20
  669.7 2.9 copy-start.25
  669.7 2.9 copy-start.26
  (1 other events, 1.0 us)

commit v5 on v4

--- a/solution.py
+++ b/solution.py
@@ -25,10 +25,9 @@
 NEG = -1e30
 BOTH = ("dp", "mp")
 MESH = pl.DeviceIdType.MESH
-VMEM_LIMIT = 60 * 1024 * 1024
+MIB = 1024 * 1024
 ANY = pl.BlockSpec(memory_space=pl.ANY)
 GROUP = 16
-CARGO_CUTS = 2
 CARGO_EARLY = 4
 CARGO_LATE = 2
 
@@ -37,9 +36,9 @@
     return lax.axis_size("dp") == 8 and lax.axis_size("mp") == 4
 
 
-def comm_params(ident):
+def comm_params(ident, room):
     return pltpu.CompilerParams(
-        collective_id=ident, has_side_effects=True, vmem_limit_bytes=VMEM_LIMIT
+        collective_id=ident, has_side_effects=True, vmem_limit_bytes=room * MIB
     )
 
 
@@ -92,6 +91,10 @@
             copy.wait_send()
 
 
+def cargo_cuts(shape):
+    return 2 if shape[1] % 32 == 0 else 1
+
+
 class Cargo:
     def __init__(self, source, target, send_sem, recv_sem, own_sem):
         self.me, self.model_index = lax.axis_index("dp"), lax.axis_index("mp")
@@ -99,8 +102,9 @@
         self.send_sem, self.recv_sem, self.sent = send_sem, recv_sem, []
         self.own = pltpu.make_async_copy(source.at[self.me], target.at[self.me], own_sem)
         self.own.start()
-        size = source.shape[1] // CARGO_CUTS
-        cuts = [pl.ds(cut * size, size) for cut in range(CARGO_CUTS)]
+        count = cargo_cuts(source.shape)
+        size = source.shape[1] // count
+        cuts = [pl.ds(cut * size, size) for cut in range(count)]
         self.cuts = [(shift, cut) for cut in cuts for shift in (4, 3, 5, 2, 6, 1, 7)]
 
     def load(self, count):
@@ -399,7 +403,8 @@
     buffers = [pltpu.VMEM((count, rows, width), low) for count in (16, 16, 4, 8, 3)]
     semaphores = [pltpu.SemaphoreType.DMA((count,)) for count in (copies, copies, 16 * groups, steps)]
     if load:
-        semaphores += [pltpu.SemaphoreType.DMA((7 * CARGO_CUTS,))] * 2 + [pltpu.SemaphoreType.DMA]
+        semaphores += [pltpu.SemaphoreType.DMA((7 * cargo_cuts(cargo.shape),))] * 2
+        semaphores += [pltpu.SemaphoreType.DMA]
     return pl.pallas_call(
         functools.partial(relay_kernel, plan, row_step),
         out_shape=shapes,
@@ -408,7 +413,7 @@
         + [ANY] * len(load),
         out_specs=[ANY] * len(out_rows) + [vmem] * (kept + sums) + [ANY] * len(load),
         scratch_shapes=buffers + [pltpu.VMEM((steps, GROUP, width), low)] + semaphores,
-        compiler_params=comm_params(ident),
+        compiler_params=comm_params(ident, 60 if rows > 32 else 6 + rows // 4),
         cost_estimate=pl.CostEstimate(flops=1, bytes_accessed=1, transcendentals=0),
     )(*partials, *([] if ready is None else [ready]), *extras, *load)
 
@@ -467,7 +472,7 @@
             pltpu.SemaphoreType.DMA((31,)),
             pltpu.SemaphoreType.DMA,
         ],
-        compiler_params=comm_params(ident),
+        compiler_params=comm_params(ident, 2),
     )(value)
 
 
@@ -536,7 +541,7 @@
             pltpu.SemaphoreType.DMA((len(values), count - 1)),
             pltpu.SemaphoreType.DMA((len(values),)),
         ],
-        compiler_params=comm_params(ident),
+        compiler_params=comm_params(ident, 2),
     )(*values)
 
 
@@ -711,9 +716,9 @@
             parts_ref[part, : 3 * HEAD_DIM] = head_sum[:, lanes].astype(low)
 
 
-def local_params():
+def local_params(room):
     return dict(
-        compiler_params=pltpu.CompilerParams(vmem_limit_bytes=VMEM_LIMIT),
+        compiler_params=pltpu.CompilerParams(vmem_limit_bytes=room * MIB),
         cost_estimate=pl.CostEstimate(flops=1, bytes_accessed=1, transcendentals=0),
     )
 
@@ -755,7 +760,7 @@
             ],
             out_specs=[by_block] + [whole_spec(out) for out in outs[1:]],
         ),
-        **local_params(),
+        **local_params(60),
     )(exit_here, resid, gain, head, inner, outer, pick, places, live)
 
 
@@ -785,11 +790,11 @@
                 pltpu.VMEM((3 * HEAD_DIM, width), jnp.float32),
             ],
         ),
-        **local_params(),
+        **local_params(60),
     )(exit_here, done, *inner, attn)
 
 
-def local(kernel, outs, *values, scratch=()):
+def local(kernel, room, outs, *values, scratch=()):
     vmem = pl.BlockSpec(memory_space=pltpu.VMEM)
     return pl.pallas_call(
         kernel,
@@ -797,7 +802,7 @@
         in_specs=[vmem] * len(values),
         out_specs=[vmem] * len(outs),
         scratch_shapes=list(scratch),
-        **local_params(),
+        **local_params(room),
     )(*values)
 
 
@@ -854,13 +859,14 @@
     square_ref[...] = squares
 
 
-def unpack_hidden_kernel(parts_ref, gate_up_ref, down_ref, square_ref, turned_ref):
-    parts, hidden = parts_ref.shape[0], parts_ref.shape[1] // 3
+def unpack_hidden_kernel(parts_ref, down_parts_ref, gate_up_ref, down_ref, square_ref, turned_ref):
+    parts, hidden = down_parts_ref.shape[:2]
     squares = jnp.zeros(square_ref.shape, jnp.float32)
     for c in range(3):
         target = down_ref if c == 2 else turned_ref
         for part in range(parts):
-            block = parts_ref[part, c * hidden : (c + 1) * hidden].astype(jnp.float32)
+            block = down_parts_ref[part] if c == 2 else parts_ref[part, c * hidden : (c + 1) * hidden]
+            block = block.astype(jnp.float32)
             squares = squares + square_row(block)
             target[part * hidden : (part + 1) * hidden] = block
         if c < 2:
@@ -890,16 +896,23 @@
 
 
 def hidden_back_kernel(
-    dtwo_ref, rows_ref, weight_ref, gate_ref, up_ref, hidden_ref, partial_ref, parts_ref
+    dtwo_ref,
+    rows_ref,
+    weight_ref,
+    gate_ref,
+    up_ref,
+    hidden_ref,
+    partial_ref,
+    parts_ref,
+    down_parts_ref,
 ):
-    parts, columns = weight_ref.shape[0], weight_ref.shape[2]
-    hidden = weight_ref.shape[1] // 3
+    parts, hidden, columns = down_parts_ref.shape
     low = jnp.bfloat16
     dhidden = jnp.zeros(gate_ref.shape, jnp.float32)
     for part in range(parts):
         piece = dtwo_ref[:, part * columns : (part + 1) * columns]
         dhidden = dhidden + dot(piece, weight_ref[part, 2 * hidden :], 1, 1)
-        parts_ref[part, 2 * hidden :] = dot(hidden_ref[...], piece, 0, 0).astype(low)
+        down_parts_ref[part] = dot(hidden_ref[...], piece, 0, 0).astype(low)
     gate, up = gate_ref[...], up_ref[...]
     sigma = jax.nn.sigmoid(gate)
     dgate = (dhidden * up * sigma * (1.0 + gate * (1.0 - sigma))).astype(low)
@@ -941,7 +954,7 @@
             out_specs=[by_columns(tokens), by_columns(entries)],
             scratch_shapes=[pltpu.VMEM((tokens, entries), low)],
         ),
-        **local_params(),
+        **local_params(60),
     )(base, ids, table)
 
 
@@ -1023,7 +1036,7 @@
             out_specs=[by_columns(entries), by_columns(1)],
             scratch_shapes=[pltpu.VMEM((entries, 2 * slots + tokens), dzero.dtype)],
         ),
-        **local_params(),
+        **local_params(60),
     )(base, ids, *grads, *rows, dzero)
 
 
@@ -1078,6 +1091,57 @@
         / (jnp.sqrt(moment_two / (1.0 - BETA_TWO**STEP)) + ADAM_EPS)
     )
     return (weight - rate * (ratio + decay * weight), moment_one, moment_two)
+
+
+def small_sum_kernel(x_ref, o_ref, held, got, send_sem, recv_sem):
+    data_index, model_index = lax.axis_index("dp"), lax.axis_index("mp")
+    z, y = data_index // 2, data_index % 2
+    x, c = model_index // 2, model_index % 2
+    peers = [
+        (data_index, x * 2 + 1 - c),
+        (data_index, (1 - x) * 2 + c),
+        (z * 2 + 1 - y, model_index),
+        ((z + 1 - 2 * (z % 2)) * 2 + y, model_index),
+        (lax.rem(z + 2, 4) * 2 + y, model_index),
+    ]
+    greet(peers)
+    held[0] = x_ref[...]
+    sent = []
+    for step, peer in enumerate(peers):
+        copy = pltpu.make_async_remote_copy(
+            src_ref=held.at[step],
+            dst_ref=got.at[step],
+            send_sem=send_sem.at[step],
+            recv_sem=recv_sem.at[step],
+            device_id=peer,
+            device_id_type=MESH,
+        )
+        copy.start()
+        copy.wait_recv()
+        sent.append(copy)
+        held[step + 1] = held[step] + got[step]
+    o_ref[...] = held[len(peers)]
+    for copy in sent:
+        copy.wait_send()
+
+
+def sum_small(value, ident):
+    if not kernel_mesh():
+        return lax.psum(value, BOTH)
+    vmem = pl.BlockSpec(memory_space=pltpu.VMEM)
+    return pl.pallas_call(
+        small_sum_kernel,
+        out_shape=jax.ShapeDtypeStruct(value.shape, value.dtype),
+        in_specs=[vmem],
+        out_specs=vmem,
+        scratch_shapes=[
+            pltpu.VMEM((6,) + value.shape, value.dtype),
+            pltpu.VMEM((5,) + value.shape, value.dtype),
+            pltpu.SemaphoreType.DMA((5,)),
+            pltpu.SemaphoreType.DMA((5,)),
+        ],
+        compiler_params=comm_params(ident, 2),
+    )(value)
 
 
 def body(
@@ -1153,10 +1217,12 @@
 
     packed = kernel_mesh()
     head_shape = (data_size, 4 * HEAD_DIM, width_here)
-    hidden_shape = (data_size, 3 * hidden_here, width_here)
+    hidden_shape = (data_size, 2 * hidden_here, width_here)
+    down_shape = (data_size, hidden_here, width_here)
     if packed:
         (head_rows,) = local(
             pack_head_kernel,
+            10,
             [(head_shape, low)],
             jnp.transpose(qkv_weight, (1, 0, 2)),
             out_weight,
@@ -1185,7 +1251,8 @@
     if packed:
         (hidden_rows,) = local(
             pack_hidden_kernel,
-            [(hidden_shape, low)],
+            16,
+            [((data_size, 3 * hidden_here, width_here), low)],
             gate_up_weight,
             down_weight,
             scratch=[pltpu.VMEM((gate_up_weight.shape[2], width_here), jnp.float32)],
@@ -1196,8 +1263,8 @@
         )
         hidden_rows = jnp.concatenate(
             [
-                jnp.moveaxis(hidden_rows, 0, 1).reshape(data_size, 2 * hidden_here, width_here),
-                down_weight.astype(low).reshape(data_size, hidden_here, width_here),
+                jnp.moveaxis(hidden_rows, 0, 1).reshape(hidden_shape),
+                down_weight.astype(low).reshape(down_shape),
             ],
             axis=1,
         )
@@ -1302,6 +1369,7 @@
     if packed:
         gate_part, up_part, hidden_low, mlp_partial = local(
             hidden_kernel,
+            20,
             [
                 ((slots, hidden_here), jnp.float32),
                 ((slots, hidden_here), jnp.float32),
@@ -1333,6 +1401,7 @@
         target_rows, entry_row = slot_targets.reshape(-1, 128), vocab_ids[None]
         logits, stats = local(
             logits_kernel,
+            28,
             [((2 * slots, vocab_here), jnp.float32), ((3 * 2 * slots // 128, 128), jnp.float32)],
             *exit_rows,
             table_low,
@@ -1358,6 +1427,7 @@
     if packed:
         *grad_logits, one_terms, two_terms = local(
             head_grad_kernel,
+            28,
             [((slots, vocab_here), low)] * 2 + [((slots, width), low)] * 2,
             logits,
             row_lse.reshape(-1, 128),
@@ -1395,9 +1465,10 @@
         slot=lambda p: None if p == 0 else 0,
     )
     if packed:
-        dmlp_partial, hidden_parts = local(
+        dmlp_partial, hidden_parts, down_parts = local(
             hidden_back_kernel,
-            [((slots, width), low), (hidden_shape, low)],
+            28,
+            [((slots, width), low), (hidden_shape, low), (down_shape, low)],
             dtwo_low,
             mlp_low,
             hidden_rows,
@@ -1413,8 +1484,10 @@
         dgate_up = jnp.concatenate([dgate, dup_part], axis=1).astype(low)
         gate_up_local = dot(dgate_up, mlp_low, 0, 0)
         dmlp_partial = dot(dgate_up, gate_up_head).astype(low)
-        hidden_parts = jnp.concatenate([gate_up_local.astype(low), down_local.astype(low)])
-        hidden_parts = jnp.moveaxis(hidden_parts.reshape(-1, data_size, width_here), 1, 0)
+        hidden_parts, down_parts = (
+            jnp.moveaxis(value.astype(low).reshape(-1, data_size, width_here), 1, 0)
+            for value in (gate_up_local, down_local)
+        )
 
     def mlp_step(p, total, extras):
         gain = extras[2][1:2]
@@ -1422,7 +1495,7 @@
         back, gain_grad = norm_back(unit, scale, gain, total)
         return ((extras[1][GROUP : 2 * GROUP] + back).astype(low), (), (gain_grad[None],))
 
-    done_low, mlp_grad = relay(
+    done_low, mlp_grad, down_parts = relay(
         [dmlp_partial],
         mlp_step,
         6,
@@ -1430,6 +1503,7 @@
         sums=1,
         slot=lambda p: 1,
         ready=dexits[:GROUP].astype(low),
+        cargo=down_parts,
     )
     hidden_parts = swap_blocks(after(hidden_parts, done_low))
     done_low = done_low.reshape(devices, 2, slots_here, width)
@@ -1528,6 +1602,7 @@
     if packed:
         qkv_grad, out_grad, head_squares = local(
             unpack_head_kernel,
+            12,
             [
                 ((3, width_here, qkv_weight.shape[2]), jnp.float32),
                 (out_weight.shape, jnp.float32),
@@ -1536,17 +1611,19 @@
             ridden,
             later,
         )
-        qkv_grad = jnp.transpose(qkv_grad, (1, 0, 2))
         gate_up_grad, down_grad, hidden_squares = local(
             unpack_hidden_kernel,
+            20,
             [
                 (gate_up_weight.shape, jnp.float32),
                 (down_weight.shape, jnp.float32),
                 square_shape,
             ],
             hidden_parts,
+            down_parts,
             scratch=[pltpu.VMEM((gate_up_weight.shape[2], width_here), jnp.float32)],
         )
+        qkv_grad = jnp.transpose(qkv_grad, (1, 0, 2))
         squares = squares + jnp.sum(head_squares) + jnp.sum(hidden_squares)
     else:
         head_grad = jnp.sum(
@@ -1556,11 +1633,9 @@
         qkv_grad = jnp.transpose(head_grad[:, :3], (3, 1, 0, 2)).reshape(qkv_weight.shape)
         out_grad = head_grad[:, 3].reshape(out_weight.shape)
         hidden_parts = hidden_parts.astype(jnp.float32)
-        gate_up_grad = hidden_parts[:, : 2 * hidden_here].reshape(
-            data_size, 2, hidden_here, width_here
-        )
+        gate_up_grad = hidden_parts.reshape(data_size, 2, hidden_here, width_here)
         gate_up_grad = jnp.transpose(gate_up_grad, (3, 1, 0, 2)).reshape(gate_up_weight.shape)
-        down_grad = hidden_parts[:, 2 * hidden_here :].reshape(down_weight.shape)
+        down_grad = down_parts.reshape(down_weight.shape).astype(jnp.float32)
         squares = (
             squares
             + jnp.sum(qkv_grad * qkv_grad)
@@ -1574,21 +1649,20 @@
             jnp.full((8, 128), squares),
         ]
     )
-    parts = jnp.sum(gather_small(parts, 8), axis=0)
+    parts = sum_small(parts, 8)
     gain_sums = parts[:-8].reshape(3, width)
     gain_grad = lax.dynamic_slice_in_dim(gain_sums, data_index * width_here, width_here, 1)
     grad_norm = jnp.sqrt(parts[-1, 0] + jnp.sum(gain_sums * gain_sums))
     factor = jnp.minimum(1.0, CLIP / (grad_norm + 1e-06))
-    table_new = adam_update(
-        table, table_first, table_second, table_grad * factor, RATE_MATRIX, DECAY
-    )
-    qkv_new = adam_update(qkv_weight, qkv_first, qkv_second, qkv_grad * factor, RATE_MATRIX, DECAY)
-    out_new = adam_update(out_weight, out_first, out_second, out_grad * factor, RATE_MATRIX, DECAY)
-    gate_up_new = adam_update(
-        gate_up_weight, gate_up_first, gate_up_second, gate_up_grad * factor, RATE_MATRIX, DECAY
-    )
-    down_new = adam_update(
-        down_weight, down_first, down_second, down_grad * factor, RATE_MATRIX, DECAY
+    table_new, qkv_new, out_new, gate_up_new, down_new = (
+        adam_update(weight, first, second, grad * factor, RATE_MATRIX, DECAY)
+        for weight, first, second, grad in (
+            (table, table_first, table_second, table_grad),
+            (qkv_weight, qkv_first, qkv_second, qkv_grad),
+            (out_weight, out_first, out_second, out_grad),
+            (gate_up_weight, gate_up_first, gate_up_second, gate_up_grad),
+            (down_weight, down_first, down_second, down_grad),
+        )
     )
     gains_new = adam_update(gains, gains_first, gains_second, gain_grad * factor, RATE_GAIN, 0.0)
     return (

time: 688 us -> 650 us (0.945)
  Pallas kernels: 546 us -> 507 us
  local copies, waits for them, and re-layouts: 18.5 us -> 40.8 us
  waiting for transfers between devices: 20.2 us -> 4.1 us
    pallas_call x8, Pallas kernels: 51.8 us -> 20.5 us  [local(): pl.pallas_call(kernel, out_shape=[jax.ShapeDtypeStruct(shape, dtype) for...]
    unnamed x59 -> x113, local copies, waits for them, and re-layouts: 5.3 us -> 30.9 us
    pallas_call x2 -> x1, Pallas kernels: 35.3 us -> 10.5 us  [gather_small(): pl.pallas_call(small_gather_kernel, out_shape=jax.ShapeDtypeStruct((32,)...]
    pallas_call x0 -> x1, Pallas kernels: none -> 16.3 us  [sum_small(): pl.pallas_call(small_sum_kernel, out_shape=jax.ShapeDtypeStruct(value.sha...]
    all_to_all x4, waiting for transfers between devices: 20.2 us -> 4.1 us  [swap_blocks(): return lax.all_to_all(value, 'dp', split_axis=0, concat_axis=0, tiled=True)]
  transfers between devices with their start and end apart: 4 -> 4, of which waited for: 1 -> 1; matrix products, arithmetic and copies ran while one was open for 4% -> 3% of each run, Pallas kernels for 35% -> 36%
where the time goes in v5:
time: 650 us; the launch traced here: 640 us
  Pallas kernels  507 us (78%)
  other arithmetic  60.1 us (9%)
  local copies, waits for them, and re-layouts  40.8 us (6%)
  starting transfers between devices  18.4 us (3%)
    pallas_call x6, Pallas kernels, relay(): pl.pallas_call(functools.partial(relay_kernel, plan, row_step), out_shape...  373 us
    sub x6, other arithmetic, adam_update(): return (weight - rate * (ratio + decay * weight), moment_one, moment_two)  44 us
    unnamed x113, local copies, waits for them, and re-layouts  30.9 us
    pallas_call x1, Pallas kernels, attend_back(): pl.pallas_call(attend_back_kernel, out_shape=[jax.ShapeDtypeStruct((token...  23.2 us
    pallas_call x1, Pallas kernels, attend(): pl.pallas_call(attend_kernel, out_shape=outs, grid_spec=pltpu.PrefetchSca...  20.6 us
    pallas_call x8, Pallas kernels, local(): pl.pallas_call(kernel, out_shape=[jax.ShapeDtypeStruct(shape, dtype) for...  20.5 us
    pallas_call x1, Pallas kernels, table_gradient(): pl.pallas_call(table_grad_kernel, out_shape=[jax.ShapeDtypeStruct((entrie...  19.2 us
    all_to_all x4, starting transfers between devices, swap_blocks(): return lax.all_to_all(value, 'dp', split_axis=0, concat_axis=0, tiled=True)  18.4 us
  transfers between devices with their start and end apart: 4, of which 1 were waited for; matrix products, arithmetic and copies ran while one was open for 3% of the time, Pallas kernels for 36%

profile of v5, /device:TPU:0, one launch (start us, length us, event | category | flops | bytes accessed | tf_op | source)
XLA Modules:
  0.0 640.4 jit_solution(9011191397691698592)
XLA Ops:
  2.1 9.2 %shard_map.373 = (s32[8,4,256]{2,1,0:T(4,128)S(1)}, bf16[8,16,256]{2,1,0:T(8,128)(2,1)S(1)}) custom-call(s32[4,256]{1,0:T(4,128)S(1)} %pad_add_fusion.refs_0_, bf16[16,256]{1,0:T(8,128)(2,1)S(1)} %pad.5.refs_1_), custom_call_target="tpu_custom_call" | custom-call | tf_op jit(solution)/shard_map/pallas_call | solution.py:534
  15.3 5.7 all-to-all-start
  22.4 2.6 shard_map.375
  27.7 14.9 %shard_map.374 = (bf16[2048,2048]{1,0:T(8,128)(2,1)}, bf16[1000,2048]{1,0:T(8,128)(2,1)}) custom-call(s32[1]{0:T(128)} %bitcast.4.base_ref, s32[2048,1]{1,0:T(8,128)} %copy.59.ids_ref, f32[1000,2048]{1,0:T(8,128)} %table_ref.1), custom_call_target="tpu_custom_call" | custom-call | flops 1 | bytes 1 | tf_op jit(solution)/shard_map/pallas_call | solution.py:944
  42.6 90.3 %shard_map.376.resid_ref = bf16[2048,2048]{1,0:T(8,128)(2,1)} custom-call(bf16[2048,2048]{1,0:T(8,128)(2,1)} %get-tuple-element.78.refs_0_), custom_call_target="tpu_custom_call" | custom-call | flops 1 | bytes 1 | tf_op jit(solution)/shard_map/pallas_call | solution.py:408
  134.2 4.9 all-to-all-start.1
  148.7 20.6 %shard_map.378 = (bf16[2048,2048]{1,0:T(8,128)(2,1)}, bf16[512,128]{1,0:T(8,128)(2,1)}, bf16[2048,128]{1,0:T(8,128)(2,1)}, bf16[2048,128]{1,0:T(8,128)(2,1)}, bf...) custom-call(s32[1]{0:T(128)} %bitcast.3.exit_ref, ...), custom_call_target="tpu_custom_call" | custom-call | flops 1 | bytes 1 | tf_op jit(solution)/shard_map/pallas_call | solution.py:745
  169.3 2.2 copy-done.19
  171.5 57.8 %shard_map.379 = (bf16[512,2048]{1,0:T(8,128)(2,1)S(1)}, bf16[512,2048]{1,0:T(8,128)(2,1)S(1)}, f32[32,2048]{1,0:T(8,128)S(1)}) custom-call(bf16[1024,2048]{1,0:T(8,128)(2,1)S(1)} %bitcast.74, f32[32,2048]{1,0:T(8,128)S(1)} %fusion.5.refs_1_, f32[3,2048]{1,0:T(4,128)S(1)} %bitcast.75), custom_call_target="tpu_custom_call" | custom-call | flops 1 | bytes 1 | tf_op jit(solution)/shard_map/pallas_call | solution.py:408
  235.4 36.9 %shard_map.381 = (bf16[512,2048]{1,0:T(8,128)(2,1)S(1)}, f32[16,2048]{1,0:T(8,128)S(1)}) custom-call(bf16[512,2048]{1,0:T(8,128)(2,1)S(1)} %get-tuple-element.85.refs_0_, f32[32,2048]{1,0:T(8,128)S(1)} %get-tuple-element.86.refs_1_.refs_2_, f32[3,2048]{1,0:T(4,128)S(1)} %bitcast.76), custom_call_target="tpu_custom_call" | custom-call | flops 1 | bytes 1 | tf_op jit(solution)/shard_map/pallas_call | solution.py:408
  272.3 5.0 shard_map.382
  277.3 2.0 copy-done.17
  279.4 10.5 %shard_map.383 = f32[32,24,128]{2,1,0:T(8,128)S(1)} custom-call(f32[24,128]{1,0:T(8,128)S(1)} %get-tuple-element.89.x_ref), custom_call_target="tpu_custom_call" | custom-call | tf_op jit(solution)/shard_map/pallas_call | solution.py:465
  294.4 2.2 copy-done.1
  296.6 2.2 copy-done.18
  298.8 5.2 shard_map.384
  304.1 44.3 %shard_map.385 = (bf16[512,2048]{1,0:T(8,128)(2,1)S(1)}, f32[32,2048]{1,0:T(8,128)S(1)}, f32[1,2048]{1,0:T(1,128)S(1)}) custom-call(bf16[512,2048]{1,0:T(8,128)(2,1)S(1)} %get-tuple-element.91.refs_0_, bf16[512,2048]{1,0:T(8,128)(2,1)S(1)} %get-tuple-element.92.refs_1_, f32[32,2048]{1,0:T(8,128)S(1)} %get-tuple-element.86.refs_1_.refs_2_, ...), custom_call_target="tpu_custom_call" | custom-call | flops 1 | bytes 1 | tf_op jit(solution)/shard_map/pallas_call | solution.py:408
  348.5 3.3 shard_map.386
  351.8 48.2 %shard_map.387 = (bf16[1024,2048]{1,0:T(8,128)(2,1)S(1)}, f32[1,2048]{1,0:T(1,128)S(1)}, bf16[8,176,256]{2,1,0:T(8,128)(2,1)S(1)}) custom-call(bf16[512,2048]{1,0:T(8,128)(2,1)S(1)} %get-tuple-element.98.refs_0_, bf16[16,2048]{1,0:T(8,128)(2,1)S(1)} %slice.112.refs_1_, f32[32,2048]{1,0:T(8,128)S(1)} %get-tuple-element.86.refs_1_.refs_2_, ...), custom_call_target="tpu_custom_call" | custom-call | flops 1 | bytes 1 | tf_op jit(solution)/shard_map/pallas_call | solution.py:408
  402.9 4.0 all-to-all-start.2
  409.6 23.2 %shard_map.388 = (bf16[2048,2048]{1,0:T(8,128)(2,1)}, bf16[8,512,256]{2,1,0:T(8,128)(2,1)}) custom-call(s32[1]{0:T(128)} %bitcast.3.exit_ref, bf16[32,2,16,2048]{3,2,1,0:T(8,128)(2,1)} %bitcast.72, bf16[8,512,256]{2,1,0:T(8,128)(2,1)} %all-to-all-done.head_ref, bf16[512,128]{1,0:T(8,128)(2,1)} %get-tuple-element.102.out_ref, ...), custom_call_target="tpu_custom_call" | custom-call | flops 1 | bytes 1 | tf_op jit(solution)/shard_map/pallas_call | solution.py:774
  432.7 2.1 convolution_bitcast_fusion.refs_2_
  434.8 3.0 fusion.24
  437.9 4.1 all-to-all-done.2.parts_ref
  442.0 95.4 %shard_map.389 = (bf16[2048,2048]{1,0:T(8,128)(2,1)}, f32[1,2048]{1,0:T(1,128)}, bf16[8,256,256]{2,1,0:T(8,128)(2,1)}) custom-call(bf16[2048,2048]{1,0:T(8,128)(2,1)} %get-tuple-element.112.refs_0_, f32[64,2048]{1,0:T(8,128)} %dynamic-slice_convert_fusion.refs_1_, f32[64,2048]{1,0:T(8,128)} %convolution_bitcast_fusion.refs_2_, f32[3,2048]{1,0:T(4,128)} %bitcast.79, ...), custom_call_target="tpu_custom_call" | custom-call | flops 1 | bytes 1 | tf_op jit(solution)/shard_map/pallas_call | solution.py:408
  537.4 3.8 all-to-all-start.3
  541.1 19.2 %shard_map.390 = (f32[1000,2048]{1,0:T(8,128)}, f32[1,2048]{1,0:T(1,128)}) custom-call(s32[1]{0:T(128)} %bitcast.4.base_ref, s32[1,2048]{1,0:T(1,128)} %bitcast.82, bf16[512,1000]{1,0:T(8,128)(2,1)} %copy-done.31, bf16[512,1000]{1,0:T(8,128)(2,1)} %copy-done.32, bf16[512,2048]{1,0:T(8,128)(2,1)} %copy-done.5, bf16[512,2048]{1,0:T(8,128)(2,1)} %copy-done.7, ...), custom_call_target="tpu_custom_call" | custom-call | flops 1 | bytes 1 | tf_op jit(solution)/shard_map/pallas_call | solution.py:1025
  574.3 16.3 %shard_map.393 = f32[56,128]{1,0:T(8,128)S(1)} custom-call(f32[56,128]{1,0:T(8,128)S(1)} %concatenate.27.x_ref), custom_call_target="tpu_custom_call" | custom-call | tf_op jit(solution)/shard_map/pallas_call | solution.py:1132
  593.2 22.8 %multiply_subtract_fusion = (f32[1000,2048]{1,0:T(8,128)}, f32[1000,2048]{1,0:T(8,128)}, f32[1000,2048]{1,0:T(8,128)}) fusion(f32[1000,2048]{1,0:T(8,128)} %table_ref.1, f32[1000,2048]{1,0:T(8,128)} %get-tuple-element.126, f32[]{:T(128)S(6)} %min.3, f32[1000,2048]{1,0:T(8,128)} %param.26, f32[1000,2048]{1,0:T(8,128)} %param.27), kind=kLoop, calls=%fused_computation.2 | loop fusion | flops 32768000 | bytes 57344004 | tf_op jit(solution)/shard_map/sub | solution.py:1093
  616.1 5.1 multiply_subtract_fusion.2
  624.3 11.2 %multiply_subtract_fusion.1 = (f32[256,2,1408]{2,1,0:T(2,128)}, f32[256,2,1408]{2,1,0:T(2,128)}, f32[256,2,1408]{2,1,0:T(2,128)}) fusion(f32[256,2,1408]{2,1,0:T(2,128)S(1)} %copy-done.3, f32[256,2,1408]{2,1,0:T(2,128)S(1)} %copy-done.21, f32[]{:T(128)S(6)} %min.3, f32[256,2,1408]{2,1,0:T(2,128)S(1)} %copy-done.42, f32[256,2,1408]{2,1,0:T(2,128)S(1)} %copy-done.43), kind=kLoop, calls=%fused_computation.6 | loop fusion | flops 11534336 | bytes 20185092 | tf_op jit(solution)/shard_map/sub | solution.py:1093
  635.6 2.8 multiply_subtract_fusion.3
  (191 shorter events, 53.3 us)
Async XLA Ops:
  15.3 5.7 copy-start.2
  15.3 118.9 %all-to-all-start = ((bf16[8,512,256]{2,1,0:T(8,128)(2,1)}), bf16[8,512,256]{2,1,0:T(8,128)(2,1)}, u32[]{:S(2)}, u32[]{:S(2)}) async-start(bf16[8,512,256]{2,1,0:T(8,128)(2,1)} %copy-done.8), calls=%async_computation | async-start | bytes 4194304 | tf_op jit(solution)/shard_map/all_to_all | solution.py:426
  26.3 16.3 %copy-start.49 = (s32[8,1,256]{2,1,0:T(1,128)}, s32[8,1,256]{2,1,0:T(1,128)S(1)}, u32[]{:S(2)}) copy-start(s32[8,1,256]{2,1,0:T(1,128)S(1)} %get-tuple-element.158) | copy-start | bytes 24580
  133.5 218.3 %copy-start.29 = (f32[8,3,256]{2,1,0:T(4,128)}, f32[8,3,256]{2,1,0:T(4,128)S(1)}, u32[]{:S(2)}) copy-start(f32[8,3,256]{2,1,0:T(4,128)S(1)} %get-tuple-element.155) | copy-start | bytes 73732
  134.2 8.2 %copy-start.55 = (f32[2]{0:T(128)S(1)}, f32[2]{0:T(128)}, u32[]{:S(2)}) copy-start(f32[2]{0:T(128)} %constant.157.clone) | copy-start | bytes 28
  134.2 97.7 %all-to-all-start.1 = ((bf16[8,528,256]{2,1,0:T(8,128)(2,1)}), bf16[8,528,256]{2,1,0:T(8,128)(2,1)S(1)}, u32[]{:S(2)}, u32[]{:S(2)}) async-start(bf16[8,528,256]{2,1,0:T(8,128)(2,1)} %copy-done.4), calls=%async_computation.1 | async-start | bytes 4325376 | tf_op jit(solution)/shard_map/all_to_all | solution.py:426
  233.5 38.8 %copy-start = (bf16[1000,2048]{1,0:T(8,128)(2,1)S(1)}, bf16[1000,2048]{1,0:T(8,128)(2,1)}, u32[]{:S(2)}) copy-start(bf16[1000,2048]{1,0:T(8,128)(2,1)} %get-tuple-element.88.table_ref) | copy-start | bytes 12288004
  235.3 36.9 %copy-start.37 = (f32[512,176]{1,0:T(8,128)}, f32[512,176]{1,0:T(8,128)S(1)}, u32[]{:S(2)}) copy-start(f32[512,176]{1,0:T(8,128)S(1)} %get-tuple-element.96.up_ref) | copy-start | bytes 1081348
  235.3 42.0 %copy-start.39 = (bf16[512,176]{1,0:T(8,128)(2,1)}, bf16[512,176]{1,0:T(8,128)(2,1)S(1)}, u32[]{:S(2)}) copy-start(bf16[512,176]{1,0:T(8,128)(2,1)S(1)} %get-tuple-element.97.hidden_ref) | copy-start | bytes 540676
  235.4 36.9 %copy-start.6 = (bf16[512,2048]{1,0:T(8,128)(2,1)S(1)}, bf16[512,2048]{1,0:T(8,128)(2,1)}, u32[]{:S(2)}) copy-start(bf16[512,2048]{1,0:T(8,128)(2,1)} %copy-done.5) | copy-start | bytes 6291460
  304.0 44.4 %copy-start.31 = (bf16[512,1000]{1,0:T(8,128)(2,1)}, bf16[512,1000]{1,0:T(8,128)(2,1)S(1)}, u32[]{:S(2)}) copy-start(bf16[512,1000]{1,0:T(8,128)(2,1)S(1)} %get-tuple-element.117.one_ref) | copy-start | bytes 3072004
  304.0 44.4 %copy-start.32 = (bf16[512,1000]{1,0:T(8,128)(2,1)}, bf16[512,1000]{1,0:T(8,128)(2,1)S(1)}, u32[]{:S(2)}) copy-start(bf16[512,1000]{1,0:T(8,128)(2,1)S(1)} %get-tuple-element.118.two_ref) | copy-start | bytes 3072004
  304.0 44.4 %copy-start.11 = (bf16[512,2048]{1,0:T(8,128)(2,1)S(1)}, bf16[512,2048]{1,0:T(8,128)(2,1)}, u32[]{:S(2)}) copy-start(bf16[512,2048]{1,0:T(8,128)(2,1)} %copy-done.9) | copy-start | bytes 6291460
  304.0 44.4 %copy-start.38 = (f32[512,176]{1,0:T(8,128)S(1)}, f32[512,176]{1,0:T(8,128)}, u32[]{:S(2)}) copy-start(f32[512,176]{1,0:T(8,128)} %copy-done.37) | copy-start | bytes 1081348
  304.0 44.4 %copy-start.40 = (bf16[512,176]{1,0:T(8,128)(2,1)S(1)}, bf16[512,176]{1,0:T(8,128)(2,1)}, u32[]{:S(2)}) copy-start(bf16[512,176]{1,0:T(8,128)(2,1)} %copy-done.39) | copy-start | bytes 540676
  351.8 51.1 %copy-start.28 = (bf16[8,352,256]{2,1,0:T(8,128)(2,1)}, bf16[8,352,256]{2,1,0:T(8,128)(2,1)S(1)}, u32[]{:S(2)}) copy-start(bf16[8,352,256]{2,1,0:T(8,128)(2,1)S(1)} %get-tuple-element.111) | copy-start | bytes 4325380
  402.9 39.0 %all-to-all-start.2 = ((bf16[8,352,256]{2,1,0:T(8,128)(2,1)}), bf16[8,352,256]{2,1,0:T(8,128)(2,1)S(1)}, u32[]{:S(2)}, u32[]{:S(2)}) async-start(bf16[8,352,256]{2,1,0:T(8,128)(2,1)} %copy-done.28), calls=%async_computation.2 | async-start | bytes 2883584 | tf_op jit(solution)/shard_map/all_to_all | solution.py:426
  537.4 31.9 %all-to-all-start.3 = ((bf16[8,256,256]{2,1,0:T(8,128)(2,1)}), bf16[8,256,256]{2,1,0:T(8,128)(2,1)S(1)}, u32[]{:S(2)}, u32[]{:S(2)}) async-start(bf16[8,256,256]{2,1,0:T(8,128)(2,1)} %get-tuple-element.122), calls=%async_computation.3 | async-start | bytes 2097152 | tf_op jit(solution)/shard_map/all_to_all | solution.py:426
  560.3 8.9 %copy-start.30 = (bf16[8,256,256]{2,1,0:T(8,128)(2,1)S(1)}, bf16[8,256,256]{2,1,0:T(8,128)(2,1)}, u32[]{:S(2)}) copy-start(bf16[8,256,256]{2,1,0:T(8,128)(2,1)} %get-tuple-element.121.one_ref) | copy-start | bytes 3145732
  593.1 22.9 %copy-start.13 = (f32[256,3,512]{2,0,1:T(8,128)S(1)}, f32[256,3,512]{2,0,1:T(8,128)}, u32[]{:S(2)}) copy-start(f32[256,3,512]{2,0,1:T(8,128)} %param.28) | copy-start | bytes 4718596
  593.2 22.8 %copy-start.25 = (f32[3,256,512]{2,1,0:T(8,128)S(1)}, f32[3,256,512]{2,1,0:T(8,128)}, u32[]{:S(2)}) copy-start(f32[3,256,512]{2,1,0:T(8,128)} %copy-done.24) | copy-start | bytes 4718596
  616.0 5.2 copy-start.23
  616.0 5.2 copy-start.36
  616.0 5.2 copy-start.47
  616.0 5.2 copy-start.48
  616.1 6.6 %copy-start.21 = (f32[256,2,1408]{2,1,0:T(2,128)S(1)}, f32[256,2,1408]{2,1,0:T(2,128)}, u32[]{:S(2)}) copy-start(f32[256,2,1408]{2,1,0:T(2,128)} %copy-done.20) | copy-start | bytes 8650756
  616.1 6.6 %copy-start.42 = (f32[256,2,1408]{2,1,0:T(2,128)S(1)}, f32[256,2,1408]{2,1,0:T(2,128)}, u32[]{:S(2)}) copy-start(f32[256,2,1408]{2,1,0:T(2,128)} %param.35) | copy-start | bytes 8650756
  616.1 7.3 %copy-start.43 = (f32[256,2,1408]{2,1,0:T(2,128)S(1)}, f32[256,2,1408]{2,1,0:T(2,128)}, u32[]{:S(2)}) copy-start(f32[256,2,1408]{2,1,0:T(2,128)} %param.36) | copy-start | bytes 8650756
  624.3 11.2 %copy-start.15 = (f32[1408,256]{1,0:T(8,128)S(1)}, f32[1408,256]{1,0:T(8,128)}, u32[]{:S(2)}) copy-start(f32[1408,256]{1,0:T(8,128)} %down_ref.1) | copy-start | bytes 4325380
  624.3 11.2 %copy-start.27 = (f32[1408,256]{1,0:T(8,128)S(1)}, f32[1408,256]{1,0:T(8,128)}, u32[]{:S(2)}) copy-start(f32[1408,256]{1,0:T(8,128)} %copy-done.26) | copy-start | bytes 4325380
  624.3 11.2 %copy-start.44 = (f32[1408,256]{1,0:T(8,128)S(1)}, f32[1408,256]{1,0:T(8,128)}, u32[]{:S(2)}) copy-start(f32[1408,256]{1,0:T(8,128)} %param.38) | copy-start | bytes 4325380
  624.3 11.2 %copy-start.45 = (f32[1408,256]{1,0:T(8,128)S(1)}, f32[1408,256]{1,0:T(8,128)}, u32[]{:S(2)}) copy-start(f32[1408,256]{1,0:T(8,128)} %param.39) | copy-start | bytes 4325380
  (28 other events, 53.3 us)

commit v6 on v5

--- a/solution.py
+++ b/solution.py
@@ -426,7 +426,7 @@
     return lax.all_to_all(value, "dp", split_axis=0, concat_axis=0, tiled=True)
 
 
-def small_gather_kernel(x_ref, o_ref, send_sem, recv_sem, own_sem):
+def small_gather_kernel(then, x_ref, result_ref, o_ref, send_sem, recv_sem, own_sem):
     data_index, model_index = lax.axis_index("dp"), lax.axis_index("mp")
     me = data_index * 4 + model_index
     own = pltpu.make_async_copy(x_ref, o_ref.at[me], own_sem)
@@ -454,20 +454,22 @@
         here = o_ref.at[lax.rem(me + 31 - index, 32)]
         pltpu.make_async_copy(here, here, recv_sem.at[index]).wait()
     own.wait()
+    result_ref[...] = then(o_ref)
     for copy in sent:
         copy.wait_send()
 
 
-def gather_small(value, ident):
+def gather_small(value, then, shape, ident):
     if not kernel_mesh():
-        return lax.all_gather(value, BOTH)
+        return then(lax.all_gather(value, BOTH))
     vmem = pl.BlockSpec(memory_space=pltpu.VMEM)
     return pl.pallas_call(
-        small_gather_kernel,
-        out_shape=jax.ShapeDtypeStruct((32,) + value.shape, value.dtype),
+        functools.partial(small_gather_kernel, then),
+        out_shape=jax.ShapeDtypeStruct(shape, value.dtype),
         in_specs=[vmem],
         out_specs=vmem,
         scratch_shapes=[
+            pltpu.VMEM((32,) + value.shape, value.dtype),
             pltpu.SemaphoreType.DMA((31,)),
             pltpu.SemaphoreType.DMA((31,)),
             pltpu.SemaphoreType.DMA,
@@ -806,6 +808,41 @@
     )(*values)
 
 
+def slots_kernel(ints_ref, pick_ref, place_ref, target_ref, live_ref, weight_ref):
+    blocks, _, rows = ints_ref.shape
+    slots, lanes = pick_ref.shape[2], place_ref.shape[1]
+    low = jnp.bfloat16
+    across = lax.broadcasted_iota(jnp.int32, (rows, rows), 1)
+    down = lax.broadcasted_iota(jnp.int32, (rows, rows), 0)
+    until = jnp.where(down <= across, 1.0, 0.0).astype(low)
+    slot = lax.broadcasted_iota(jnp.int32, (slots, rows), 0).astype(jnp.float32)
+    kind = lax.broadcasted_iota(jnp.int32, (8, rows), 0)
+    inner = lax.broadcasted_iota(jnp.int32, (1, rows), 1).astype(jnp.float32)
+    for e in range(2):
+        mask = ints_ref[:, 2 + e].astype(jnp.float32)
+        ranks = dot(mask.astype(low), until) - 1.0
+        for block in range(blocks):
+            at = slice(block, block + 1)
+            pick = jnp.where((ranks[at] == slot) & (mask[at] == 1.0), 1.0, 0.0).astype(low)
+            pick_ref[e, block] = pick
+            target = ints_ref[block, 1:2]
+            high = (target >> 8).astype(jnp.float32)
+            rest = (target & 255).astype(jnp.float32)
+            facts = jnp.where(kind == 0, inner, jnp.where(kind == 1, high, rest))
+            facts = jnp.where(kind == 3, 1.0, facts).astype(low)
+            found = dot(facts, pick, 1, 1)
+            live = found[3:4]
+            row = slice((e * blocks + block) * slots // lanes, (e * blocks + block) * slots // lanes + 1)
+            lane = slice(block * slots % lanes, block * slots % lanes + slots)
+            place = found[0:1] + live * float(block * rows)
+            place_ref[row, lane] = place.astype(jnp.int32)
+            target_ref[row, lane] = (found[1:2] * 256.0 + found[2:3]).astype(jnp.int32)
+            live_ref[row, lane] = live
+        half = slice(e * blocks * slots // lanes, (e + 1) * blocks * slots // lanes)
+        live = live_ref[half]
+        weight_ref[half] = live * (EXIT_SCALE[e] / jnp.sum(live, keepdims=True))
+
+
 def pack_head_kernel(qkv_ref, out_ref, packed_ref):
     heads = out_ref.shape[0] // HEAD_DIM
     sharers = packed_ref.shape[0] // heads
@@ -1093,34 +1130,44 @@
     return (weight - rate * (ratio + decay * weight), moment_one, moment_two)
 
 
-def small_sum_kernel(x_ref, o_ref, held, got, send_sem, recv_sem):
+def small_sum_kernel(x_ref, o_ref, held, plane, column, send_sem, recv_sem):
     data_index, model_index = lax.axis_index("dp"), lax.axis_index("mp")
     z, y = data_index // 2, data_index % 2
     x, c = model_index // 2, model_index % 2
-    peers = [
-        (data_index, x * 2 + 1 - c),
+    core = (data_index, x * 2 + 1 - c)
+    corners = [
         (data_index, (1 - x) * 2 + c),
         (z * 2 + 1 - y, model_index),
-        ((z + 1 - 2 * (z % 2)) * 2 + y, model_index),
-        (lax.rem(z + 2, 4) * 2 + y, model_index),
+        (z * 2 + 1 - y, (1 - x) * 2 + c),
     ]
-    greet(peers)
+    zs = (z + 1 - 2 * (z % 2), (z + 2) % 4, 3 - z)
+    greet([core] + corners + [(zd * 2 + y, model_index) for zd in zs])
+    sent = []
+
+    def send(source, target, device):
+        index = len(sent)
+        copy = pltpu.make_async_remote_copy(
+            src_ref=source,
+            dst_ref=target,
+            send_sem=send_sem.at[index],
+            recv_sem=recv_sem.at[index],
+            device_id=device,
+            device_id_type=MESH,
+        )
+        copy.start()
+        sent.append(copy)
+        return copy
+
     held[0] = x_ref[...]
-    sent = []
-    for step, peer in enumerate(peers):
-        copy = pltpu.make_async_remote_copy(
-            src_ref=held.at[step],
-            dst_ref=got.at[step],
-            send_sem=send_sem.at[step],
-            recv_sem=recv_sem.at[step],
-            device_id=peer,
-            device_id_type=MESH,
-        )
-        copy.start()
+    send(held.at[0], held.at[1], core).wait_recv()
+    mine = y * 2 + x
+    plane[mine] = held[0] + held[1]
+    for copy in [send(plane.at[mine], plane.at[mine], device) for device in corners]:
         copy.wait_recv()
-        sent.append(copy)
-        held[step + 1] = held[step] + got[step]
-    o_ref[...] = held[len(peers)]
+    column[z] = (plane[0] + plane[1]) + (plane[2] + plane[3])
+    for copy in [send(column.at[z], column.at[z], (zd * 2 + y, model_index)) for zd in zs]:
+        copy.wait_recv()
+    o_ref[...] = (column[0] + column[1]) + (column[2] + column[3])
     for copy in sent:
         copy.wait_send()
 
@@ -1135,10 +1182,11 @@
         in_specs=[vmem],
         out_specs=vmem,
         scratch_shapes=[
-            pltpu.VMEM((6,) + value.shape, value.dtype),
-            pltpu.VMEM((5,) + value.shape, value.dtype),
-            pltpu.SemaphoreType.DMA((5,)),
-            pltpu.SemaphoreType.DMA((5,)),
+            pltpu.VMEM((2,) + value.shape, value.dtype),
+            pltpu.VMEM((4,) + value.shape, value.dtype),
+            pltpu.VMEM((4,) + value.shape, value.dtype),
+            pltpu.SemaphoreType.DMA((7,)),
+            pltpu.SemaphoreType.DMA((7,)),
         ],
         compiler_params=comm_params(ident, 2),
     )(value)
@@ -1200,22 +1248,42 @@
     )
     gain_rows = jnp.moveaxis(gain_low[:, :3], 0, 1).reshape(3, width).astype(jnp.float32)
     all_ids = ints[:, 0].reshape(tokens)
-    mask_blocks = jnp.moveaxis(ints[:, 2:], 0, 1)
-    slot_ids = jnp.arange(R_DEV, dtype=jnp.int32)
-    slot_ranks = jnp.cumsum(mask_blocks, axis=2) - 1
-    pick_int = (
-        (slot_ranks[:, :, None, :] == slot_ids[:, None]) & (mask_blocks[:, :, None, :] == 1)
-    ).astype(jnp.int32)
-    pick_low = pick_int.astype(low)
     token_places = jnp.arange(tokens, dtype=jnp.int32)
-    slot_targets = jnp.sum(pick_int * ints[:, 1][None, :, None, :], axis=3).reshape(2, -1)
-    slot_places = jnp.sum(
-        pick_int * token_places.reshape(1, data_size, 1, block_rows), axis=3
-    ).reshape(2, -1)
-    live = (slot_ids < jnp.sum(mask_blocks, axis=2)[:, :, None]).astype(jnp.float32).reshape(2, -1)
+    packed = kernel_mesh()
+    slot_shape = (2 * data_size * R_DEV // 128, 128)
+    if packed:
+        pick_low, place_rows, target_rows, live_rows, weight_rows = local(
+            slots_kernel,
+            16,
+            [
+                ((2, data_size, R_DEV, block_rows), low),
+                (slot_shape, jnp.int32),
+                (slot_shape, jnp.int32),
+                (slot_shape, jnp.float32),
+                (slot_shape, jnp.float32),
+            ],
+            ints,
+        )
+    else:
+        mask_blocks = jnp.moveaxis(ints[:, 2:], 0, 1)
+        slot_ids = jnp.arange(R_DEV, dtype=jnp.int32)
+        slot_ranks = jnp.cumsum(mask_blocks, axis=2) - 1
+        pick_int = (
+            (slot_ranks[:, :, None, :] == slot_ids[:, None]) & (mask_blocks[:, :, None, :] == 1)
+        ).astype(jnp.int32)
+        pick_low = pick_int.astype(low)
+        target_rows = jnp.sum(pick_int * ints[:, 1][None, :, None, :], axis=3).reshape(slot_shape)
+        place_rows = jnp.sum(
+            pick_int * token_places.reshape(1, data_size, 1, block_rows), axis=3
+        ).reshape(slot_shape)
+        live_rows = (slot_ids < jnp.sum(mask_blocks, axis=2)[:, :, None]).astype(jnp.float32)
+        live_rows = live_rows.reshape(slot_shape)
+        scales = jnp.array(EXIT_SCALE, jnp.float32) / jnp.sum(live_rows.reshape(2, -1), axis=1)
+        weight_rows = live_rows * jnp.repeat(scales, slot_shape[0] // 2)[:, None]
+    slot_targets, live = target_rows.reshape(2, -1), live_rows.reshape(2, -1)
+    row_weight = weight_rows.reshape(2, -1)
     counts = jnp.sum(live, axis=1)
 
-    packed = kernel_mesh()
     head_shape = (data_size, 4 * HEAD_DIM, width_here)
     hidden_shape = (data_size, 2 * hidden_here, width_here)
     down_shape = (data_size, hidden_here, width_here)
@@ -1270,7 +1338,8 @@
         )
     (resid_low,) = relay([after(id_rows, hidden_rows)], lambda p, total, extras: (total.astype(low), (), ()), 1)
 
-    hidden_rows = swap_blocks(after(hidden_rows, resid_low))
+    hidden_rows, resid_low = lax.optimization_barrier((hidden_rows, resid_low))
+    hidden_rows = swap_blocks(hidden_rows)
 
     pick_share = lax.dynamic_slice_in_dim(
         lax.dynamic_index_in_dim(pick_low, exit_here, 0, keepdims=False),
@@ -1278,12 +1347,11 @@
         data_size // shares,
         0,
     )
-    def share_of(per_slot):
-        return lax.dynamic_slice(per_slot, (exit_here, share_here * share_slots), (1, share_slots))[
-            0
-        ]
-
-    places_share, live_share = share_of(slot_places), share_of(live)
+    def share_of(rows):
+        count = share_slots // 128
+        return lax.dynamic_slice_in_dim(rows, (exit_here * shares + share_here) * count, count, 0)
+
+    place_share, live_rows_share = share_of(place_rows), share_of(live_rows)
     if packed:
 
         def turns(places):
@@ -1297,8 +1365,8 @@
             turns(token_places[:block_rows]),
             turns(token_places[::block_rows]),
             pick_share,
-            places_share.reshape(-1, 2 * R_DEV),
-            live_share.reshape(-1, 2 * R_DEV),
+            place_share,
+            live_rows_share,
             slots_here,
         )
         out_partial = out_partial.reshape(-1, width)
@@ -1306,6 +1374,7 @@
         head_rows = jnp.moveaxis(head_rows, 0, 1).reshape(4 * HEAD_DIM, width)
         qkv_head, out_head = head_rows[: 3 * HEAD_DIM], head_rows[3 * HEAD_DIM :]
         cosine, sine_table = rotary(token_places, HEAD_DIM)
+        places_share, live_share = place_share.reshape(-1), live_rows_share.reshape(-1)
         cosine_share, sine_share = rotary(places_share, HEAD_DIM)
         attn_low = norm_fwd(resid_low.astype(jnp.float32), gain_rows[0])[0].astype(low)
 
@@ -1398,7 +1467,7 @@
 
     exit_rows = (exit_rows_one, exit_rows_two)
     if packed:
-        target_rows, entry_row = slot_targets.reshape(-1, 128), vocab_ids[None]
+        entry_row = vocab_ids[None]
         logits, stats = local(
             logits_kernel,
             28,
@@ -1417,21 +1486,25 @@
         ]
         found = [jnp.sum(jnp.where(hit, values, 0.0), axis=1) for hit, values in zip(hits, logits)]
         stats = jnp.concatenate(tops + masses + found).reshape(-1, 128)
-    stats = gather_small(stats, 4).reshape(devices, 3, 2, -1)
-    row_top = jnp.max(stats[:, 0], axis=0)
-    row_mass = jnp.sum(stats[:, 1] * jnp.exp(stats[:, 0] - row_top), axis=0)
-    row_lse = row_top + jnp.log(row_mass)
-    entropy = row_lse - jnp.sum(stats[:, 2], axis=0)
+    part = stats.shape[0] // 3
+
+    def joined(stats):
+        tops, masses, found = (stats[:, k * part : (k + 1) * part] for k in range(3))
+        top = jnp.max(tops, axis=0)
+        lse = top + jnp.log(jnp.sum(masses * jnp.exp(tops - top), axis=0))
+        return jnp.concatenate([lse, lse - jnp.sum(found, axis=0)])
+
+    joint = gather_small(stats, joined, (2 * part, 128), 4)
+    row_lse, entropy = joint[:part].reshape(2, -1), joint[part:].reshape(2, -1)
     loss_sums = jnp.sum(entropy * live, axis=1)
-    row_weight = live * (jnp.array(EXIT_SCALE, jnp.float32) / counts)[:, None]
     if packed:
         *grad_logits, one_terms, two_terms = local(
             head_grad_kernel,
             28,
             [((slots, vocab_here), low)] * 2 + [((slots, width), low)] * 2,
             logits,
-            row_lse.reshape(-1, 128),
-            row_weight.reshape(-1, 128),
+            joint[:part],
+            weight_rows,
             target_rows,
             entry_row,
             table_low,
@@ -1505,7 +1578,8 @@
         ready=dexits[:GROUP].astype(low),
         cargo=down_parts,
     )
-    hidden_parts = swap_blocks(after(hidden_parts, done_low))
+    hidden_parts, done_low = lax.optimization_barrier((hidden_parts, done_low))
+    hidden_parts = swap_blocks(hidden_parts)
     done_low = done_low.reshape(devices, 2, slots_here, width)
 
     if kernel_mesh():
@@ -1520,7 +1594,7 @@
             turn,
             slot_turn,
             pick_share,
-            places_share.reshape(-1, 2 * R_DEV),
+            place_share,
             attn_low,
         )
     else:
@@ -1586,7 +1660,8 @@
         sums=1,
         cargo=head_parts[:, :ride],
     )
-    later = swap_blocks(after(head_parts[:, ride:], dzero_low))
+    later, dzero_low = lax.optimization_barrier((head_parts[:, ride:], dzero_low))
+    later = swap_blocks(later)
     if packed:
         table_grad, squares = table_gradient(
             base, all_ids[None, :], grad_logits, exit_rows, dzero_low

time: 650 us -> 632 us (0.972)
  local copies, waits for them, and re-layouts: 40.8 us -> 31.7 us
    unnamed x113 -> x92, local copies, waits for them, and re-layouts: 30.9 us -> 23.9 us
    pallas_call x8 -> x9, Pallas kernels: 20.5 us -> 21.2 us  [local(): pl.pallas_call(kernel, out_shape=[jax.ShapeDtypeStruct(shape, dtype) for...]
  transfers between devices with their start and end apart: 4 -> 4, of which waited for: 1 -> 1; matrix products, arithmetic and copies ran while one was open for 3% -> 3% of each run, Pallas kernels for 36% -> 37%
where the time goes in v6:
time: 632 us; the launch traced here: 623 us
  Pallas kernels  504 us (80%)
  other arithmetic  54.6 us (9%)
  local copies, waits for them, and re-layouts  31.7 us (5%)
  starting transfers between devices  18.3 us (3%)
    pallas_call x6, Pallas kernels, relay(): pl.pallas_call(functools.partial(relay_kernel, plan, row_step), out_shape...  373 us
    sub x6, other arithmetic, adam_update(): return (weight - rate * (ratio + decay * weight), moment_one, moment_two)  44 us
    unnamed x92, local copies, waits for them, and re-layouts  23.9 us
    pallas_call x1, Pallas kernels, attend_back(): pl.pallas_call(attend_back_kernel, out_shape=[jax.ShapeDtypeStruct((token...  23.2 us
    pallas_call x9, Pallas kernels, local(): pl.pallas_call(kernel, out_shape=[jax.ShapeDtypeStruct(shape, dtype) for...  21.2 us
    pallas_call x1, Pallas kernels, attend(): pl.pallas_call(attend_kernel, out_shape=outs, grid_spec=pltpu.PrefetchSca...  20.7 us
    pallas_call x1, Pallas kernels, table_gradient(): pl.pallas_call(table_grad_kernel, out_shape=[jax.ShapeDtypeStruct((entrie...  19.2 us
    all_to_all x4, starting transfers between devices, swap_blocks(): return lax.all_to_all(value, 'dp', split_axis=0, concat_axis=0, tiled=True)  18.3 us
  transfers between devices with their start and end apart: 4, of which 1 were waited for; matrix products, arithmetic and copies ran while one was open for 3% of the time, Pallas kernels for 37%

profile of v6, /device:TPU:0, one launch (start us, length us, event | category | flops | bytes accessed | tf_op | source)
XLA Modules:
  0.0 623.4 jit_solution(8878730170354389469)
XLA Ops:
  2.1 9.2 %shard_map.365 = (s32[8,4,256]{2,1,0:T(4,128)S(1)}, bf16[8,16,256]{2,1,0:T(8,128)(2,1)S(1)}) custom-call(s32[4,256]{1,0:T(4,128)S(1)} %pad_add_fusion.refs_0_, bf16[16,256]{1,0:T(8,128)(2,1)S(1)} %pad.5.refs_1_), custom_call_target="tpu_custom_call" | custom-call | tf_op jit(solution)/shard_map/pallas_call | solution.py:536
  15.3 5.7 all-to-all-start
  22.4 2.6 shard_map.364
  27.7 14.9 %shard_map.366 = (bf16[2048,2048]{1,0:T(8,128)(2,1)}, bf16[1000,2048]{1,0:T(8,128)(2,1)}) custom-call(s32[1]{0:T(128)} %bitcast.1.base_ref, s32[2048,1]{1,0:T(8,128)} %copy.43.ids_ref, f32[1000,2048]{1,0:T(8,128)} %table_ref.1), custom_call_target="tpu_custom_call" | custom-call | flops 1 | bytes 1 | tf_op jit(solution)/shard_map/pallas_call | solution.py:981
  42.6 90.3 %shard_map.367.resid_ref = bf16[2048,2048]{1,0:T(8,128)(2,1)} custom-call(bf16[2048,2048]{1,0:T(8,128)(2,1)} %get-tuple-element.86.refs_0_), custom_call_target="tpu_custom_call" | custom-call | flops 1 | bytes 1 | tf_op jit(solution)/shard_map/pallas_call | solution.py:408
  132.9 4.9 all-to-all-start.1
  145.1 20.7 %shard_map.370 = (bf16[2048,2048]{1,0:T(8,128)(2,1)}, bf16[512,128]{1,0:T(8,128)(2,1)}, bf16[2048,128]{1,0:T(8,128)(2,1)}, bf16[2048,128]{1,0:T(8,128)(2,1)}, bf...) custom-call(s32[1]{0:T(128)} %bitcast.exit_ref, ...), custom_call_target="tpu_custom_call" | custom-call | flops 1 | bytes 1 | tf_op jit(solution)/shard_map/pallas_call | solution.py:747
  165.7 2.2 copy-done.16
  167.9 57.3 %shard_map.371 = (bf16[512,2048]{1,0:T(8,128)(2,1)S(1)}, bf16[512,2048]{1,0:T(8,128)(2,1)S(1)}, f32[32,2048]{1,0:T(8,128)S(1)}) custom-call(bf16[1024,2048]{1,0:T(8,128)(2,1)S(1)} %bitcast.43, f32[32,2048]{1,0:T(8,128)S(1)} %fusion.5.refs_1_, f32[3,2048]{1,0:T(4,128)S(1)} %bitcast.44), custom_call_target="tpu_custom_call" | custom-call | flops 1 | bytes 1 | tf_op jit(solution)/shard_map/pallas_call | solution.py:408
  229.4 1.8 shard_map.372
  231.3 37.3 %shard_map.373 = (bf16[512,2048]{1,0:T(8,128)(2,1)S(1)}, f32[16,2048]{1,0:T(8,128)S(1)}) custom-call(bf16[512,2048]{1,0:T(8,128)(2,1)S(1)} %get-tuple-element.97.refs_0_, f32[32,2048]{1,0:T(8,128)S(1)} %get-tuple-element.98.refs_1_.refs_2_, f32[3,2048]{1,0:T(4,128)S(1)} %bitcast.45), custom_call_target="tpu_custom_call" | custom-call | flops 1 | bytes 1 | tf_op jit(solution)/shard_map/pallas_call | solution.py:408
  268.6 5.0 shard_map.374
  273.6 10.1 %shard_map.375 = f32[16,128]{1,0:T(8,128)S(1)} custom-call(f32[24,128]{1,0:T(8,128)S(1)} %get-tuple-element.102.x_ref), custom_call_target="tpu_custom_call" | custom-call | tf_op jit(solution)/shard_map/pallas_call | solution.py:466
  283.9 5.2 shard_map.376
  289.1 44.2 %shard_map.377 = (bf16[512,2048]{1,0:T(8,128)(2,1)S(1)}, f32[32,2048]{1,0:T(8,128)S(1)}, f32[1,2048]{1,0:T(1,128)S(1)}) custom-call(bf16[512,2048]{1,0:T(8,128)(2,1)S(1)} %get-tuple-element.105.refs_0_, bf16[512,2048]{1,0:T(8,128)(2,1)S(1)} %get-tuple-element.106.refs_1_, f32[32,2048]{1,0:T(8,128)S(1)} %get-tuple-element.98.refs_1_.refs_2_, ...), custom_call_target="tpu_custom_call" | custom-call | flops 1 | bytes 1 | tf_op jit(solution)/shard_map/pallas_call | solution.py:408
  333.3 3.3 shard_map.378
  336.6 48.7 %shard_map.379 = (bf16[1024,2048]{1,0:T(8,128)(2,1)S(1)}, f32[1,2048]{1,0:T(1,128)S(1)}, bf16[8,176,256]{2,1,0:T(8,128)(2,1)S(1)}) custom-call(bf16[512,2048]{1,0:T(8,128)(2,1)S(1)} %get-tuple-element.113.refs_0_, bf16[16,2048]{1,0:T(8,128)(2,1)S(1)} %slice.73.refs_1_, f32[32,2048]{1,0:T(8,128)S(1)} %get-tuple-element.98.refs_1_.refs_2_, ...), custom_call_target="tpu_custom_call" | custom-call | flops 1 | bytes 1 | tf_op jit(solution)/shard_map/pallas_call | solution.py:408
  385.3 2.0 copy-done.15
  388.2 4.0 all-to-all-start.2
  394.0 23.2 %shard_map.380 = (bf16[2048,2048]{1,0:T(8,128)(2,1)}, bf16[8,512,256]{2,1,0:T(8,128)(2,1)}) custom-call(s32[1]{0:T(128)} %bitcast.exit_ref, bf16[32,2,16,2048]{3,2,1,0:T(8,128)(2,1)} %bitcast.41, bf16[8,512,256]{2,1,0:T(8,128)(2,1)} %all-to-all-done.head_ref, bf16[512,128]{1,0:T(8,128)(2,1)} %get-tuple-element.118.out_ref, ...), custom_call_target="tpu_custom_call" | custom-call | flops 1 | bytes 1 | tf_op jit(solution)/shard_map/pallas_call | solution.py:776
  417.2 2.1 convolution_bitcast_fusion.refs_2_
  419.3 3.0 fusion.20
  422.4 4.9 all-to-all-done.2.parts_ref
  427.2 95.3 %shard_map.381 = (bf16[2048,2048]{1,0:T(8,128)(2,1)}, f32[1,2048]{1,0:T(1,128)}, bf16[8,256,256]{2,1,0:T(8,128)(2,1)}) custom-call(bf16[2048,2048]{1,0:T(8,128)(2,1)} %get-tuple-element.127.refs_0_, f32[64,2048]{1,0:T(8,128)} %dynamic-slice_convert_fusion.refs_1_, f32[64,2048]{1,0:T(8,128)} %convolution_bitcast_fusion.refs_2_, f32[3,2048]{1,0:T(4,128)} %bitcast.48, ...), custom_call_target="tpu_custom_call" | custom-call | flops 1 | bytes 1 | tf_op jit(solution)/shard_map/pallas_call | solution.py:408
  522.5 3.7 all-to-all-start.3
  527.7 19.2 %shard_map.382 = (f32[1000,2048]{1,0:T(8,128)}, f32[1,2048]{1,0:T(1,128)}) custom-call(s32[1]{0:T(128)} %bitcast.1.base_ref, s32[1,2048]{1,0:T(1,128)} %bitcast.51, bf16[512,1000]{1,0:T(8,128)(2,1)} %copy-done.28, bf16[512,1000]{1,0:T(8,128)(2,1)} %copy-done.29, bf16[512,2048]{1,0:T(8,128)(2,1)} %copy-done.4, bf16[512,2048]{1,0:T(8,128)(2,1)} %copy-done.6, ...), custom_call_target="tpu_custom_call" | custom-call | flops 1 | bytes 1 | tf_op jit(solution)/shard_map/pallas_call | solution.py:1062
  548.1 1.8 shard_map.384
  560.8 12.8 %shard_map.385 = f32[56,128]{1,0:T(8,128)S(1)} custom-call(f32[56,128]{1,0:T(8,128)S(1)} %concatenate.27.x_ref), custom_call_target="tpu_custom_call" | custom-call | tf_op jit(solution)/shard_map/pallas_call | solution.py:1179
  576.1 22.8 %multiply_subtract_fusion = (f32[1000,2048]{1,0:T(8,128)}, f32[1000,2048]{1,0:T(8,128)}, f32[1000,2048]{1,0:T(8,128)}) fusion(f32[1000,2048]{1,0:T(8,128)} %table_ref.1, f32[1000,2048]{1,0:T(8,128)} %get-tuple-element.142, f32[]{:T(128)S(6)} %min.3, f32[1000,2048]{1,0:T(8,128)} %param.25, f32[1000,2048]{1,0:T(8,128)} %param.26), kind=kLoop, calls=%fused_computation.2 | loop fusion | flops 32768000 | bytes 57344004 | tf_op jit(solution)/shard_map/sub | solution.py:1130
  599.0 5.1 multiply_subtract_fusion.2
  607.3 11.2 %multiply_subtract_fusion.1 = (f32[256,2,1408]{2,1,0:T(2,128)}, f32[256,2,1408]{2,1,0:T(2,128)}, f32[256,2,1408]{2,1,0:T(2,128)}) fusion(f32[256,2,1408]{2,1,0:T(2,128)S(1)} %copy-done.2, f32[256,2,1408]{2,1,0:T(2,128)S(1)} %copy-done.18, f32[]{:T(128)S(6)} %min.3, f32[256,2,1408]{2,1,0:T(2,128)S(1)} %copy-done.35, f32[256,2,1408]{2,1,0:T(2,128)S(1)} %copy-done.36), kind=kLoop, calls=%fused_computation.6 | loop fusion | flops 11534336 | bytes 20185092 | tf_op jit(solution)/shard_map/sub | solution.py:1130
  618.5 2.8 multiply_subtract_fusion.3
  (139 shorter events, 40.2 us)
Async XLA Ops:
  15.3 5.7 copy-start.1
  15.3 117.6 %all-to-all-start = ((bf16[8,512,256]{2,1,0:T(8,128)(2,1)}), bf16[8,512,256]{2,1,0:T(8,128)(2,1)}, u32[]{:S(2)}, u32[]{:S(2)}) async-start(bf16[8,512,256]{2,1,0:T(8,128)(2,1)} %copy-done.7), calls=%async_computation | async-start | bytes 4194304 | tf_op jit(solution)/shard_map/all_to_all | solution.py:426
  26.3 16.3 %copy-start.41 = (s32[8,1,256]{2,1,0:T(1,128)}, s32[8,1,256]{2,1,0:T(1,128)S(1)}, u32[]{:S(2)}) copy-start(s32[8,1,256]{2,1,0:T(1,128)S(1)} %slice.52) | copy-start | bytes 24580
  132.9 94.9 %all-to-all-start.1 = ((bf16[8,528,256]{2,1,0:T(8,128)(2,1)}), bf16[8,528,256]{2,1,0:T(8,128)(2,1)S(1)}, u32[]{:S(2)}, u32[]{:S(2)}) async-start(bf16[8,528,256]{2,1,0:T(8,128)(2,1)} %copy-done.3), calls=%async_computation.1 | async-start | bytes 4325376 | tf_op jit(solution)/shard_map/all_to_all | solution.py:426
  138.7 197.9 %copy-start.26 = (f32[8,3,256]{2,1,0:T(4,128)}, f32[8,3,256]{2,1,0:T(4,128)S(1)}, u32[]{:S(2)}) copy-start(f32[8,3,256]{2,1,0:T(4,128)S(1)} %get-tuple-element.169) | copy-start | bytes 73732
  229.4 39.1 %copy-start = (bf16[1000,2048]{1,0:T(8,128)(2,1)S(1)}, bf16[1000,2048]{1,0:T(8,128)(2,1)}, u32[]{:S(2)}) copy-start(bf16[1000,2048]{1,0:T(8,128)(2,1)} %get-tuple-element.100.table_ref) | copy-start | bytes 12288004
  231.2 37.4 %copy-start.5 = (bf16[512,2048]{1,0:T(8,128)(2,1)S(1)}, bf16[512,2048]{1,0:T(8,128)(2,1)}, u32[]{:S(2)}) copy-start(bf16[512,2048]{1,0:T(8,128)(2,1)} %copy-done.4) | copy-start | bytes 6291460
  268.6 5.0 copy-start.6
  289.0 44.2 %copy-start.28 = (bf16[512,1000]{1,0:T(8,128)(2,1)}, bf16[512,1000]{1,0:T(8,128)(2,1)S(1)}, u32[]{:S(2)}) copy-start(bf16[512,1000]{1,0:T(8,128)(2,1)S(1)} %get-tuple-element.132.one_ref) | copy-start | bytes 3072004
  289.0 44.2 %copy-start.29 = (bf16[512,1000]{1,0:T(8,128)(2,1)}, bf16[512,1000]{1,0:T(8,128)(2,1)S(1)}, u32[]{:S(2)}) copy-start(bf16[512,1000]{1,0:T(8,128)(2,1)S(1)} %get-tuple-element.133.two_ref) | copy-start | bytes 3072004
  289.1 44.2 %copy-start.10 = (bf16[512,2048]{1,0:T(8,128)(2,1)S(1)}, bf16[512,2048]{1,0:T(8,128)(2,1)}, u32[]{:S(2)}) copy-start(bf16[512,2048]{1,0:T(8,128)(2,1)} %copy-done.8) | copy-start | bytes 6291460
  336.6 51.6 %copy-start.25 = (bf16[8,352,256]{2,1,0:T(8,128)(2,1)}, bf16[8,352,256]{2,1,0:T(8,128)(2,1)S(1)}, u32[]{:S(2)}) copy-start(bf16[8,352,256]{2,1,0:T(8,128)(2,1)S(1)} %get-tuple-element.126) | copy-start | bytes 4325380
  388.2 39.0 %all-to-all-start.2 = ((bf16[8,352,256]{2,1,0:T(8,128)(2,1)}), bf16[8,352,256]{2,1,0:T(8,128)(2,1)S(1)}, u32[]{:S(2)}, u32[]{:S(2)}) async-start(bf16[8,352,256]{2,1,0:T(8,128)(2,1)} %copy-done.25), calls=%async_computation.2 | async-start | bytes 2883584 | tf_op jit(solution)/shard_map/all_to_all | solution.py:426
  522.5 33.3 %all-to-all-start.3 = ((bf16[8,256,256]{2,1,0:T(8,128)(2,1)}), bf16[8,256,256]{2,1,0:T(8,128)(2,1)S(1)}, u32[]{:S(2)}, u32[]{:S(2)}) async-start(bf16[8,256,256]{2,1,0:T(8,128)(2,1)} %get-tuple-element.138), calls=%async_computation.3 | async-start | bytes 2097152 | tf_op jit(solution)/shard_map/all_to_all | solution.py:426
  546.9 8.9 %copy-start.27 = (bf16[8,256,256]{2,1,0:T(8,128)(2,1)S(1)}, bf16[8,256,256]{2,1,0:T(8,128)(2,1)}, u32[]{:S(2)}) copy-start(bf16[8,256,256]{2,1,0:T(8,128)(2,1)} %get-tuple-element.137.one_ref) | copy-start | bytes 3145732
  548.1 5.1 copy-start.43
  576.1 22.9 %copy-start.12 = (f32[256,3,512]{2,0,1:T(8,128)S(1)}, f32[256,3,512]{2,0,1:T(8,128)}, u32[]{:S(2)}) copy-start(f32[256,3,512]{2,0,1:T(8,128)} %param.27) | copy-start | bytes 4718596
  576.1 22.8 %copy-start.22 = (f32[3,256,512]{2,1,0:T(8,128)S(1)}, f32[3,256,512]{2,1,0:T(8,128)}, u32[]{:S(2)}) copy-start(f32[3,256,512]{2,1,0:T(8,128)} %copy-done.21) | copy-start | bytes 4718596
  599.0 5.2 copy-start.20
  599.0 5.2 copy-start.33
  599.0 5.2 copy-start.39
  599.0 5.2 copy-start.40
  599.0 6.6 %copy-start.18 = (f32[256,2,1408]{2,1,0:T(2,128)S(1)}, f32[256,2,1408]{2,1,0:T(2,128)}, u32[]{:S(2)}) copy-start(f32[256,2,1408]{2,1,0:T(2,128)} %copy-done.17) | copy-start | bytes 8650756
  599.0 6.6 %copy-start.35 = (f32[256,2,1408]{2,1,0:T(2,128)S(1)}, f32[256,2,1408]{2,1,0:T(2,128)}, u32[]{:S(2)}) copy-start(f32[256,2,1408]{2,1,0:T(2,128)} %param.34) | copy-start | bytes 8650756
  599.0 7.3 %copy-start.36 = (f32[256,2,1408]{2,1,0:T(2,128)S(1)}, f32[256,2,1408]{2,1,0:T(2,128)}, u32[]{:S(2)}) copy-start(f32[256,2,1408]{2,1,0:T(2,128)} %param.35) | copy-start | bytes 8650756
  604.1 3.1 copy-start.2
  607.3 11.2 %copy-start.14 = (f32[1408,256]{1,0:T(8,128)S(1)}, f32[1408,256]{1,0:T(8,128)}, u32[]{:S(2)}) copy-start(f32[1408,256]{1,0:T(8,128)} %down_ref.1) | copy-start | bytes 4325380
  607.3 11.2 %copy-start.24 = (f32[1408,256]{1,0:T(8,128)S(1)}, f32[1408,256]{1,0:T(8,128)}, u32[]{:S(2)}) copy-start(f32[1408,256]{1,0:T(8,128)} %copy-done.23) | copy-start | bytes 4325380
  607.3 11.2 %copy-start.37 = (f32[1408,256]{1,0:T(8,128)S(1)}, f32[1408,256]{1,0:T(8,128)}, u32[]{:S(2)}) copy-start(f32[1408,256]{1,0:T(8,128)} %param.37) | copy-start | bytes 4325380
  607.3 11.2 %copy-start.38 = (f32[1408,256]{1,0:T(8,128)S(1)}, f32[1408,256]{1,0:T(8,128)}, u32[]{:S(2)}) copy-start(f32[1408,256]{1,0:T(8,128)} %param.38) | copy-start | bytes 4325380
  618.5 2.9 copy-start.42
  618.5 2.9 copy-start.44
  (18 other events, 25.0 us)

commit v7 on v6

--- a/solution.py
+++ b/solution.py
@@ -341,6 +341,17 @@
         cargo.finish()
 
 
+def wide_sum(value):
+    pieces = jnp.moveaxis(value.reshape(value.shape[0], 4, -1), 1, 0)
+    sums = lax.map(
+        lambda piece: lax.psum_scatter(
+            piece.astype(jnp.float32), BOTH, scatter_dimension=0, tiled=True
+        ),
+        pieces,
+    )
+    return jnp.moveaxis(sums, 0, 1).reshape(sums.shape[1], -1)
+
+
 def relay(
     partials,
     row_step,
@@ -362,9 +373,8 @@
     steps = sum(slot(p) is not None for p in order) + (ready is not None)
     if not kernel_mesh():
         total = jnp.concatenate(
-            [lax.psum_scatter(part, BOTH, scatter_dimension=0, tiled=True) for part in partials]
-        )
-        total = total.astype(jnp.float32)
+            [wide_sum(part) for part in partials]
+        )
         outs, keeps, adds = [None] * steps, [None] * groups, [0.0] * sums
         if ready is not None:
             outs[0] = ready

time: 632 us -> 632 us (level)
  no operation moved by 1% of the time
where the time goes in v7:
time: 632 us; the launch traced here: 623 us
  Pallas kernels  504 us (80%)
  other arithmetic  54.6 us (9%)
  local copies, waits for them, and re-layouts  31.7 us (5%)
  starting transfers between devices  18.3 us (3%)
    pallas_call x6, Pallas kernels, relay(): pl.pallas_call(functools.partial(relay_kernel, plan, row_step), out_shape...  373 us
    sub x6, other arithmetic, adam_update(): return (weight - rate * (ratio + decay * weight), moment_one, moment_two)  44 us
    unnamed x92, local copies, waits for them, and re-layouts  23.9 us
    pallas_call x1, Pallas kernels, attend_back(): pl.pallas_call(attend_back_kernel, out_shape=[jax.ShapeDtypeStruct((token...  23.2 us
    pallas_call x9, Pallas kernels, local(): pl.pallas_call(kernel, out_shape=[jax.ShapeDtypeStruct(shape, dtype) for...  21.2 us
    pallas_call x1, Pallas kernels, attend(): pl.pallas_call(attend_kernel, out_shape=outs, grid_spec=pltpu.PrefetchSca...  20.7 us
    pallas_call x1, Pallas kernels, table_gradient(): pl.pallas_call(table_grad_kernel, out_shape=[jax.ShapeDtypeStruct((entrie...  19.2 us
    all_to_all x4, starting transfers between devices, swap_blocks(): return lax.all_to_all(value, 'dp', split_axis=0, concat_axis=0, tiled=True)  18.3 us
  transfers between devices with their start and end apart: 4, of which 1 were waited for; matrix products, arithmetic and copies ran while one was open for 3% of the time, Pallas kernels for 37%

profile of v7, /device:TPU:0, one launch (start us, length us, event | category | flops | bytes accessed | tf_op | source)
XLA Modules:
  0.0 623.4 jit_solution(8878730170354389469)
XLA Ops:
  2.1 9.2 %shard_map.365 = (s32[8,4,256]{2,1,0:T(4,128)S(1)}, bf16[8,16,256]{2,1,0:T(8,128)(2,1)S(1)}) custom-call(s32[4,256]{1,0:T(4,128)S(1)} %pad_add_fusion.refs_0_, bf16[16,256]{1,0:T(8,128)(2,1)S(1)} %pad.5.refs_1_), custom_call_target="tpu_custom_call" | custom-call | tf_op jit(solution)/shard_map/pallas_call | solution.py:546
  15.3 5.7 all-to-all-start
  22.4 2.6 shard_map.364
  27.7 14.9 %shard_map.366 = (bf16[2048,2048]{1,0:T(8,128)(2,1)}, bf16[1000,2048]{1,0:T(8,128)(2,1)}) custom-call(s32[1]{0:T(128)} %bitcast.1.base_ref, s32[2048,1]{1,0:T(8,128)} %copy.43.ids_ref, f32[1000,2048]{1,0:T(8,128)} %table_ref.1), custom_call_target="tpu_custom_call" | custom-call | flops 1 | bytes 1 | tf_op jit(solution)/shard_map/pallas_call | solution.py:991
  42.6 90.3 %shard_map.367.resid_ref = bf16[2048,2048]{1,0:T(8,128)(2,1)} custom-call(bf16[2048,2048]{1,0:T(8,128)(2,1)} %get-tuple-element.86.refs_0_), custom_call_target="tpu_custom_call" | custom-call | flops 1 | bytes 1 | tf_op jit(solution)/shard_map/pallas_call | solution.py:418
  132.9 4.9 all-to-all-start.1
  145.1 20.7 %shard_map.370 = (bf16[2048,2048]{1,0:T(8,128)(2,1)}, bf16[512,128]{1,0:T(8,128)(2,1)}, bf16[2048,128]{1,0:T(8,128)(2,1)}, bf16[2048,128]{1,0:T(8,128)(2,1)}, bf...) custom-call(s32[1]{0:T(128)} %bitcast.exit_ref, ...), custom_call_target="tpu_custom_call" | custom-call | flops 1 | bytes 1 | tf_op jit(solution)/shard_map/pallas_call | solution.py:757
  165.7 2.2 copy-done.16
  167.9 57.3 %shard_map.371 = (bf16[512,2048]{1,0:T(8,128)(2,1)S(1)}, bf16[512,2048]{1,0:T(8,128)(2,1)S(1)}, f32[32,2048]{1,0:T(8,128)S(1)}) custom-call(bf16[1024,2048]{1,0:T(8,128)(2,1)S(1)} %bitcast.43, f32[32,2048]{1,0:T(8,128)S(1)} %fusion.5.refs_1_, f32[3,2048]{1,0:T(4,128)S(1)} %bitcast.44), custom_call_target="tpu_custom_call" | custom-call | flops 1 | bytes 1 | tf_op jit(solution)/shard_map/pallas_call | solution.py:418
  229.4 1.8 shard_map.372
  231.3 37.3 %shard_map.373 = (bf16[512,2048]{1,0:T(8,128)(2,1)S(1)}, f32[16,2048]{1,0:T(8,128)S(1)}) custom-call(bf16[512,2048]{1,0:T(8,128)(2,1)S(1)} %get-tuple-element.97.refs_0_, f32[32,2048]{1,0:T(8,128)S(1)} %get-tuple-element.98.refs_1_.refs_2_, f32[3,2048]{1,0:T(4,128)S(1)} %bitcast.45), custom_call_target="tpu_custom_call" | custom-call | flops 1 | bytes 1 | tf_op jit(solution)/shard_map/pallas_call | solution.py:418
  268.6 5.0 shard_map.374
  273.6 10.1 %shard_map.375 = f32[16,128]{1,0:T(8,128)S(1)} custom-call(f32[24,128]{1,0:T(8,128)S(1)} %get-tuple-element.102.x_ref), custom_call_target="tpu_custom_call" | custom-call | tf_op jit(solution)/shard_map/pallas_call | solution.py:476
  283.9 5.2 shard_map.376
  289.1 44.2 %shard_map.377 = (bf16[512,2048]{1,0:T(8,128)(2,1)S(1)}, f32[32,2048]{1,0:T(8,128)S(1)}, f32[1,2048]{1,0:T(1,128)S(1)}) custom-call(bf16[512,2048]{1,0:T(8,128)(2,1)S(1)} %get-tuple-element.105.refs_0_, bf16[512,2048]{1,0:T(8,128)(2,1)S(1)} %get-tuple-element.106.refs_1_, f32[32,2048]{1,0:T(8,128)S(1)} %get-tuple-element.98.refs_1_.refs_2_, ...), custom_call_target="tpu_custom_call" | custom-call | flops 1 | bytes 1 | tf_op jit(solution)/shard_map/pallas_call | solution.py:418
  333.3 3.3 shard_map.378
  336.6 48.7 %shard_map.379 = (bf16[1024,2048]{1,0:T(8,128)(2,1)S(1)}, f32[1,2048]{1,0:T(1,128)S(1)}, bf16[8,176,256]{2,1,0:T(8,128)(2,1)S(1)}) custom-call(bf16[512,2048]{1,0:T(8,128)(2,1)S(1)} %get-tuple-element.113.refs_0_, bf16[16,2048]{1,0:T(8,128)(2,1)S(1)} %slice.73.refs_1_, f32[32,2048]{1,0:T(8,128)S(1)} %get-tuple-element.98.refs_1_.refs_2_, ...), custom_call_target="tpu_custom_call" | custom-call | flops 1 | bytes 1 | tf_op jit(solution)/shard_map/pallas_call | solution.py:418
  385.3 2.0 copy-done.15
  388.2 4.0 all-to-all-start.2
  394.0 23.2 %shard_map.380 = (bf16[2048,2048]{1,0:T(8,128)(2,1)}, bf16[8,512,256]{2,1,0:T(8,128)(2,1)}) custom-call(s32[1]{0:T(128)} %bitcast.exit_ref, bf16[32,2,16,2048]{3,2,1,0:T(8,128)(2,1)} %bitcast.41, bf16[8,512,256]{2,1,0:T(8,128)(2,1)} %all-to-all-done.head_ref, bf16[512,128]{1,0:T(8,128)(2,1)} %get-tuple-element.118.out_ref, ...), custom_call_target="tpu_custom_call" | custom-call | flops 1 | bytes 1 | tf_op jit(solution)/shard_map/pallas_call | solution.py:786
  417.2 2.1 convolution_bitcast_fusion.refs_2_
  419.3 3.0 fusion.20
  422.4 4.9 all-to-all-done.2.parts_ref
  427.2 95.3 %shard_map.381 = (bf16[2048,2048]{1,0:T(8,128)(2,1)}, f32[1,2048]{1,0:T(1,128)}, bf16[8,256,256]{2,1,0:T(8,128)(2,1)}) custom-call(bf16[2048,2048]{1,0:T(8,128)(2,1)} %get-tuple-element.127.refs_0_, f32[64,2048]{1,0:T(8,128)} %dynamic-slice_convert_fusion.refs_1_, f32[64,2048]{1,0:T(8,128)} %convolution_bitcast_fusion.refs_2_, f32[3,2048]{1,0:T(4,128)} %bitcast.48, ...), custom_call_target="tpu_custom_call" | custom-call | flops 1 | bytes 1 | tf_op jit(solution)/shard_map/pallas_call | solution.py:418
  522.5 3.7 all-to-all-start.3
  527.7 19.2 %shard_map.382 = (f32[1000,2048]{1,0:T(8,128)}, f32[1,2048]{1,0:T(1,128)}) custom-call(s32[1]{0:T(128)} %bitcast.1.base_ref, s32[1,2048]{1,0:T(1,128)} %bitcast.51, bf16[512,1000]{1,0:T(8,128)(2,1)} %copy-done.28, bf16[512,1000]{1,0:T(8,128)(2,1)} %copy-done.29, bf16[512,2048]{1,0:T(8,128)(2,1)} %copy-done.4, bf16[512,2048]{1,0:T(8,128)(2,1)} %copy-done.6, ...), custom_call_target="tpu_custom_call" | custom-call | flops 1 | bytes 1 | tf_op jit(solution)/shard_map/pallas_call | solution.py:1072
  548.1 1.8 shard_map.384
  560.8 12.8 %shard_map.385 = f32[56,128]{1,0:T(8,128)S(1)} custom-call(f32[56,128]{1,0:T(8,128)S(1)} %concatenate.27.x_ref), custom_call_target="tpu_custom_call" | custom-call | tf_op jit(solution)/shard_map/pallas_call | solution.py:1189
  576.1 22.8 %multiply_subtract_fusion = (f32[1000,2048]{1,0:T(8,128)}, f32[1000,2048]{1,0:T(8,128)}, f32[1000,2048]{1,0:T(8,128)}) fusion(f32[1000,2048]{1,0:T(8,128)} %table_ref.1, f32[1000,2048]{1,0:T(8,128)} %get-tuple-element.142, f32[]{:T(128)S(6)} %min.3, f32[1000,2048]{1,0:T(8,128)} %param.25, f32[1000,2048]{1,0:T(8,128)} %param.26), kind=kLoop, calls=%fused_computation.2 | loop fusion | flops 32768000 | bytes 57344004 | tf_op jit(solution)/shard_map/sub | solution.py:1140
  599.0 5.1 multiply_subtract_fusion.2
  607.3 11.2 %multiply_subtract_fusion.1 = (f32[256,2,1408]{2,1,0:T(2,128)}, f32[256,2,1408]{2,1,0:T(2,128)}, f32[256,2,1408]{2,1,0:T(2,128)}) fusion(f32[256,2,1408]{2,1,0:T(2,128)S(1)} %copy-done.2, f32[256,2,1408]{2,1,0:T(2,128)S(1)} %copy-done.18, f32[]{:T(128)S(6)} %min.3, f32[256,2,1408]{2,1,0:T(2,128)S(1)} %copy-done.35, f32[256,2,1408]{2,1,0:T(2,128)S(1)} %copy-done.36), kind=kLoop, calls=%fused_computation.6 | loop fusion | flops 11534336 | bytes 20185092 | tf_op jit(solution)/shard_map/sub | solution.py:1140
  618.5 2.8 multiply_subtract_fusion.3
  (139 shorter events, 40.2 us)
Async XLA Ops:
  15.3 5.7 copy-start.1
  15.3 117.6 %all-to-all-start = ((bf16[8,512,256]{2,1,0:T(8,128)(2,1)}), bf16[8,512,256]{2,1,0:T(8,128)(2,1)}, u32[]{:S(2)}, u32[]{:S(2)}) async-start(bf16[8,512,256]{2,1,0:T(8,128)(2,1)} %copy-done.7), calls=%async_computation | async-start | bytes 4194304 | tf_op jit(solution)/shard_map/all_to_all | solution.py:436
  26.3 16.3 %copy-start.41 = (s32[8,1,256]{2,1,0:T(1,128)}, s32[8,1,256]{2,1,0:T(1,128)S(1)}, u32[]{:S(2)}) copy-start(s32[8,1,256]{2,1,0:T(1,128)S(1)} %slice.52) | copy-start | bytes 24580
  132.9 94.9 %all-to-all-start.1 = ((bf16[8,528,256]{2,1,0:T(8,128)(2,1)}), bf16[8,528,256]{2,1,0:T(8,128)(2,1)S(1)}, u32[]{:S(2)}, u32[]{:S(2)}) async-start(bf16[8,528,256]{2,1,0:T(8,128)(2,1)} %copy-done.3), calls=%async_computation.1 | async-start | bytes 4325376 | tf_op jit(solution)/shard_map/all_to_all | solution.py:436
  138.7 197.9 %copy-start.26 = (f32[8,3,256]{2,1,0:T(4,128)}, f32[8,3,256]{2,1,0:T(4,128)S(1)}, u32[]{:S(2)}) copy-start(f32[8,3,256]{2,1,0:T(4,128)S(1)} %get-tuple-element.169) | copy-start | bytes 73732
  229.4 39.1 %copy-start = (bf16[1000,2048]{1,0:T(8,128)(2,1)S(1)}, bf16[1000,2048]{1,0:T(8,128)(2,1)}, u32[]{:S(2)}) copy-start(bf16[1000,2048]{1,0:T(8,128)(2,1)} %get-tuple-element.100.table_ref) | copy-start | bytes 12288004
  231.2 37.4 %copy-start.5 = (bf16[512,2048]{1,0:T(8,128)(2,1)S(1)}, bf16[512,2048]{1,0:T(8,128)(2,1)}, u32[]{:S(2)}) copy-start(bf16[512,2048]{1,0:T(8,128)(2,1)} %copy-done.4) | copy-start | bytes 6291460
  268.6 5.0 copy-start.6
  289.0 44.2 %copy-start.28 = (bf16[512,1000]{1,0:T(8,128)(2,1)}, bf16[512,1000]{1,0:T(8,128)(2,1)S(1)}, u32[]{:S(2)}) copy-start(bf16[512,1000]{1,0:T(8,128)(2,1)S(1)} %get-tuple-element.132.one_ref) | copy-start | bytes 3072004
  289.0 44.2 %copy-start.29 = (bf16[512,1000]{1,0:T(8,128)(2,1)}, bf16[512,1000]{1,0:T(8,128)(2,1)S(1)}, u32[]{:S(2)}) copy-start(bf16[512,1000]{1,0:T(8,128)(2,1)S(1)} %get-tuple-element.133.two_ref) | copy-start | bytes 3072004
  289.1 44.2 %copy-start.10 = (bf16[512,2048]{1,0:T(8,128)(2,1)S(1)}, bf16[512,2048]{1,0:T(8,128)(2,1)}, u32[]{:S(2)}) copy-start(bf16[512,2048]{1,0:T(8,128)(2,1)} %copy-done.8) | copy-start | bytes 6291460
  336.6 51.6 %copy-start.25 = (bf16[8,352,256]{2,1,0:T(8,128)(2,1)}, bf16[8,352,256]{2,1,0:T(8,128)(2,1)S(1)}, u32[]{:S(2)}) copy-start(bf16[8,352,256]{2,1,0:T(8,128)(2,1)S(1)} %get-tuple-element.126) | copy-start | bytes 4325380
  388.2 39.0 %all-to-all-start.2 = ((bf16[8,352,256]{2,1,0:T(8,128)(2,1)}), bf16[8,352,256]{2,1,0:T(8,128)(2,1)S(1)}, u32[]{:S(2)}, u32[]{:S(2)}) async-start(bf16[8,352,256]{2,1,0:T(8,128)(2,1)} %copy-done.25), calls=%async_computation.2 | async-start | bytes 2883584 | tf_op jit(solution)/shard_map/all_to_all | solution.py:436
  522.5 33.3 %all-to-all-start.3 = ((bf16[8,256,256]{2,1,0:T(8,128)(2,1)}), bf16[8,256,256]{2,1,0:T(8,128)(2,1)S(1)}, u32[]{:S(2)}, u32[]{:S(2)}) async-start(bf16[8,256,256]{2,1,0:T(8,128)(2,1)} %get-tuple-element.138), calls=%async_computation.3 | async-start | bytes 2097152 | tf_op jit(solution)/shard_map/all_to_all | solution.py:436
  546.9 8.9 %copy-start.27 = (bf16[8,256,256]{2,1,0:T(8,128)(2,1)S(1)}, bf16[8,256,256]{2,1,0:T(8,128)(2,1)}, u32[]{:S(2)}) copy-start(bf16[8,256,256]{2,1,0:T(8,128)(2,1)} %get-tuple-element.137.one_ref) | copy-start | bytes 3145732
  548.1 5.1 copy-start.43
  576.1 22.9 %copy-start.12 = (f32[256,3,512]{2,0,1:T(8,128)S(1)}, f32[256,3,512]{2,0,1:T(8,128)}, u32[]{:S(2)}) copy-start(f32[256,3,512]{2,0,1:T(8,128)} %param.27) | copy-start | bytes 4718596
  576.1 22.8 %copy-start.22 = (f32[3,256,512]{2,1,0:T(8,128)S(1)}, f32[3,256,512]{2,1,0:T(8,128)}, u32[]{:S(2)}) copy-start(f32[3,256,512]{2,1,0:T(8,128)} %copy-done.21) | copy-start | bytes 4718596
  599.0 5.2 copy-start.20
  599.0 5.2 copy-start.33
  599.0 5.2 copy-start.39
  599.0 5.2 copy-start.40
  599.0 6.6 %copy-start.18 = (f32[256,2,1408]{2,1,0:T(2,128)S(1)}, f32[256,2,1408]{2,1,0:T(2,128)}, u32[]{:S(2)}) copy-start(f32[256,2,1408]{2,1,0:T(2,128)} %copy-done.17) | copy-start | bytes 8650756
  599.0 6.6 %copy-start.35 = (f32[256,2,1408]{2,1,0:T(2,128)S(1)}, f32[256,2,1408]{2,1,0:T(2,128)}, u32[]{:S(2)}) copy-start(f32[256,2,1408]{2,1,0:T(2,128)} %param.34) | copy-start | bytes 8650756
  599.0 7.3 %copy-start.36 = (f32[256,2,1408]{2,1,0:T(2,128)S(1)}, f32[256,2,1408]{2,1,0:T(2,128)}, u32[]{:S(2)}) copy-start(f32[256,2,1408]{2,1,0:T(2,128)} %param.35) | copy-start | bytes 8650756
  604.1 3.1 copy-start.2
  607.3 11.2 %copy-start.14 = (f32[1408,256]{1,0:T(8,128)S(1)}, f32[1408,256]{1,0:T(8,128)}, u32[]{:S(2)}) copy-start(f32[1408,256]{1,0:T(8,128)} %down_ref.1) | copy-start | bytes 4325380
  607.3 11.2 %copy-start.24 = (f32[1408,256]{1,0:T(8,128)S(1)}, f32[1408,256]{1,0:T(8,128)}, u32[]{:S(2)}) copy-start(f32[1408,256]{1,0:T(8,128)} %copy-done.23) | copy-start | bytes 4325380
  607.3 11.2 %copy-start.37 = (f32[1408,256]{1,0:T(8,128)S(1)}, f32[1408,256]{1,0:T(8,128)}, u32[]{:S(2)}) copy-start(f32[1408,256]{1,0:T(8,128)} %param.37) | copy-start | bytes 4325380
  607.3 11.2 %copy-start.38 = (f32[1408,256]{1,0:T(8,128)S(1)}, f32[1408,256]{1,0:T(8,128)}, u32[]{:S(2)}) copy-start(f32[1408,256]{1,0:T(8,128)} %param.38) | copy-start | bytes 4325380
  618.5 2.9 copy-start.42
  618.5 2.9 copy-start.44
  (18 other events, 25.0 us)
